TPU v7x, 256 devices: a whole 4x4x8 slice. The times are simulated.
256 devices in a mesh: seq: 64 (over y, z_hi, x, core), head: 4 (over z_lo).
Axes of the slice: x: 4, y: 4, z: 8 (z_hi: 2, z_lo: 4; z = z_hi * 4 + z_lo), core: 2. Of those that a mesh axis runs over, the one named last changes fastest.
Arguments:
- queries: bfloat16 [24576, 3072], P('seq', 'head'), may hold values from -18 to 18
- key_states: bfloat16 [24576, 3072], P('seq', 'head'), may hold values from -6 to 6
- value_states: bfloat16 [24576, 3072], P('seq', 'head'), may hold values from -6 to 6
- out_weight: bfloat16 [3072, 3072], P('head'), may hold values from -0.15625 to 0.15625
Outputs:
- mixed: bfloat16 [24576, 3072], P('seq', 'head')
All inputs are finite; a program needn't handle non-finite values.
Results may differ from a plain program's by a relative error of at most 0.023.
Values may be sent and summed in bfloat16 or wider, within the bound.
No kernel may reach another device: no remote copies, remote signals or barrier semaphores. Data moves between devices by JAX's collectives and lax.ppermute only.
A program may use at most 64 MiB of HBM per device.

v0:
```python
import jax
import jax.numpy as jnp
from jax import lax
from jax.sharding import PartitionSpec as P

HD = 128


NEG_FILL = -1e30


def passed_along(array, axis, by):
    peers = lax.axis_size(axis)
    pairs = [(i, i + by) for i in range(peers) if 0 <= i + by < peers]
    return lax.ppermute(array, axis, pairs)


def shortened(array):

    def short(part):
        return part.astype(jnp.bfloat16) if part.dtype == jnp.float32 else part

    return jax.tree.map(short, array)


def block_part(query_part, key_part, value_part):
    scores = jnp.einsum(
        "qhd,khd->hqk", query_part, key_part, preferred_element_type=jnp.float32
    ) * HD ** (-0.5)
    row_max = jnp.max(scores, axis=2)
    weights = jnp.exp(scores - row_max[:, :, None])
    row_sum = jnp.sum(weights, axis=2)
    summed = jnp.einsum(
        "hqk,khd->hqd", weights.astype(jnp.bfloat16), value_part, preferred_element_type=jnp.float32
    )
    return (summed, row_max, row_sum)


def combine_parts(earlier, later, usable):
    early_sum, early_max, early_total = earlier
    late_sum, late_max, late_total = later
    late_max = jnp.where(usable, late_max, NEG_FILL)
    joint_max = jnp.maximum(early_max, late_max)
    scale_early = jnp.exp(early_max - joint_max)
    scale_late = jnp.exp(late_max - joint_max)
    joint_total = early_total * scale_early + late_total * scale_late
    joint_sum = early_sum * scale_early[:, :, None] + late_sum * scale_late[:, :, None]
    return (joint_sum, joint_max, joint_total)


def body(queries, key_states, value_states, out_weight):
    span_len = queries.shape[0]
    query_heads = queries.reshape(span_len, -1, HD)
    key_heads = key_states.reshape(span_len, -1, HD)
    value_heads = value_states.reshape(span_len, -1, HD)
    seq_place = lax.axis_index("seq")
    seq_count = lax.axis_size("seq")
    running = block_part(query_heads, key_heads, value_heads)
    for offset in (1, 2):
        far_query, far_key, far_value = passed_along(
            (query_heads, key_heads, value_heads), "seq", -offset
        )
        running = combine_parts(
            running, block_part(query_heads, far_key, far_value), seq_place + offset < seq_count
        )
        returned = passed_along(
            shortened(block_part(far_query, key_heads, value_heads)), "seq", offset
        )
        running = combine_parts(running, returned, seq_place >= offset)
    summed, row_max, row_sum = running
    attended = (
        jnp.transpose(summed / row_sum[:, :, None], (1, 0, 2))
        .reshape(span_len, -1)
        .astype(jnp.bfloat16)
    )
    mixed = lax.psum_scatter(
        jnp.einsum("fc,qf->cq", out_weight, attended, preferred_element_type=jnp.float32).astype(
            jnp.bfloat16
        ),
        "head",
        scatter_dimension=0,
        tiled=True,
    ).astype(jnp.float32)
    return jnp.transpose(mixed).astype(jnp.bfloat16)


def solution(mesh):
    placed = (P("seq", "head"), P("seq", "head"), P("seq", "head"), P("head", None))
    return jax.shard_map(
        body, mesh=mesh, in_specs=placed, out_specs=P("seq", "head"), check_vma=False
    )
```

profile of v0, /device:TPU:24, one launch (start us, length us, event | category | flops | bytes accessed | tf_op | source)
XLA Modules:
  0.0 264.5 jit_solution(13099711962078914006)
XLA Ops:
  8.0 11.5 %collective-permute-start.6 = (bf16[384,6,128]{0,2,1:T(8,128)(2,1)S(1)}, bf16[384,6,128]{0,2,1:T(8,128)(2,1)S(1)}, u32[]{:S(2)}, u32[]{:S(2)}) collective-permute-start(bf16[384,6,128]{0,2,1:T(8,128)(2,1)S(1)} %bitcast.36), channel_id=1, source_target_pairs={{8,0},{12,4},{16,8},{20,12},{24,16},{28,20},{32,24},{36,28},{40,32... | collective-permute-start | bytes 1769480 | tf_op jit(solution)/shard_map/ppermute | solution.py:15
  19.5 1.9 collective-permute-start.1
  23.1 2.7 %collective-permute-start.5 = (bf16[384,6,128]{2,0,1:T(8,128)(2,1)S(1)}, bf16[384,6,128]{2,0,1:T(8,128)(2,1)}, u32[]{:S(2)}, u32[]{:S(2)}) collective-permute-start(bf16[384,6,128]{2,0,1:T(8,128)(2,1)S(1)} %copy.21), channel_id=1, source_target_pairs={{8,0},{12,4},{16,8},{20,12},{24,16},{28,20},{32,24},{36,28},{40,32... | collective-permute-start | bytes 1769480 | tf_op jit(solution)/shard_map/ppermute | solution.py:15
  25.8 2.3 collective-permute-start
  28.7 2.2 collective-permute-start.2
  32.2 76.0 %collective-permute-done.2 = bf16[384,6,128]{2,0,1:T(8,128)(2,1)} collective-permute-done((bf16[384,6,128]{2,0,1:T(8,128)(2,1)S(1)}, bf16[384,6,128]{2,0,1:T(8,128)(2,1)}, u32[]{:S(2)}, u32[]{:S(2)}) %collective-permute-start.2) | collective-permute-done | bytes 589856 | tf_op jit(solution)/shard_map/ppermute | solution.py:15
  108.2 1.9 collective-permute-start.7
  110.1 1.7 multiply_reduce_fusion.2
  112.5 15.6 %collective-permute-done.7 = bf16[384,6,128]{2,0,1:T(8,128)(2,1)S(1)} collective-permute-done((bf16[384,6,128]{2,0,1:T(8,128)(2,1)S(1)}, bf16[384,6,128]{2,0,1:T(8,128)(2,1)S(1)}, u32[]{:S(2)}, u32[]{:S(2)}) %collective-permute-start.7) | collective-permute-done | bytes 589856 | tf_op jit(solution)/shard_map/ppermute | solution.py:15
  128.0 10.1 %collective-permute-start.3 = (bf16[6,384]{1,0:T(8,128)(2,1)S(1)}, bf16[6,384]{1,0:T(8,128)(2,1)S(1)}, u32[]{:S(2)}, u32[]{:S(2)}) collective-permute-start(bf16[6,384]{1,0:T(8,128)(2,1)S(1)} %convert_element_type.78), channel_id=1, source_target_pairs={{0,4},{4,8},{8,12},{12,16},{16,20},{20,24},{24,28},{28,32},{32,36}... | collective-permute-start | bytes 13832 | tf_op jit(solution)/shard_map/ppermute | solution.py:15
  140.2 1.9 collective-permute-start.10
  142.1 1.7 multiply_reduce_fusion.3
  145.2 1.9 collective-permute-start.8
  147.2 1.7 multiply_reduce_fusion.1
  149.5 4.5 %collective-permute-start.11 = (bf16[6,384]{1,0:T(8,128)(2,1)S(1)}, bf16[6,384]{1,0:T(8,128)(2,1)S(1)}, u32[]{:S(2)}, u32[]{:S(2)}) collective-permute-start(bf16[6,384]{1,0:T(8,128)(2,1)S(1)} %fusion.9), channel_id=1, source_target_pairs={{0,8},{4,12},{8,16},{12,20},{16,24},{20,28},{24,32},{28,36},{32,40... | collective-permute-start | bytes 13832 | tf_op jit(solution)/shard_map/ppermute | solution.py:15
  154.1 1.9 collective-permute-start.4
  156.0 1.9 collective-permute-done.8
  157.9 2.1 collective-permute-start.9
  160.0 7.1 %collective-permute-done.11 = bf16[6,384]{1,0:T(8,128)(2,1)S(1)} collective-permute-done((bf16[6,384]{1,0:T(8,128)(2,1)S(1)}, bf16[6,384]{1,0:T(8,128)(2,1)S(1)}, u32[]{:S(2)}, u32[]{:S(2)}) %collective-permute-start.11) | collective-permute-done | bytes 4640 | tf_op jit(solution)/shard_map/ppermute | solution.py:15
  168.8 14.5 %collective-permute-done.4 = bf16[6,384,128]{1,2,0:T(8,128)(2,1)S(1)} collective-permute-done((bf16[6,384,128]{1,2,0:T(8,128)(2,1)S(1)}, bf16[6,384,128]{1,2,0:T(8,128)(2,1)S(1)}, u32[]{:S(2)}, u32[]{:S(2)}) %collective-permute-start.4) | collective-permute-done | bytes 589856 | tf_op jit(solution)/shard_map/ppermute | solution.py:15
  183.3 5.4 %collective-permute-done.9 = bf16[6,384,128]{1,2,0:T(8,128)(2,1)S(1)} collective-permute-done((bf16[6,384,128]{1,2,0:T(8,128)(2,1)S(1)}, bf16[6,384,128]{1,2,0:T(8,128)(2,1)S(1)}, u32[]{:S(2)}, u32[]{:S(2)}) %collective-permute-start.9) | collective-permute-done | bytes 589856 | tf_op jit(solution)/shard_map/ppermute | solution.py:15
  188.7 2.4 divide_convert_fusion
  191.1 3.5 %fusion = bf16[3072,384]{0,1:T(8,128)(2,1)} fusion(bf16[384,768]{0,1:T(8,128)(2,1)S(1)} %bitcast.41, bf16[768,3072]{1,0:T(8,128)(2,1)S(1)} %bitcast.35), kind=kOutput, calls=%fused_computation.1 | convolution fusion | flops 1813118976 | bytes 7667712 | tf_op jit(solution)/shard_map/fc,qf->cq/dot_general | solution.py:77
  194.7 63.0 %reduce-scatter.2.cloned.1.call-done = bf16[768,384]{0,1:T(8,128)(2,1)} async-done(((bf16[3072,384]{0,1:T(8,128)(2,1)}), bf16[768,384]{0,1:T(8,128)(2,1)}) %reduce-scatter.2.cloned.1.call-update) | async-done | bytes 589840 | tf_op jit(solution)/shard_map/reduce_scatter | solution.py:76
  (35 shorter events, 11.3 us)
Async XLA Ops:
  6.5 21.6 %copy-start = (bf16[384,768]{1,0:T(8,128)(2,1)S(1)}, bf16[384,768]{1,0:T(8,128)(2,1)}, u32[]{:S(2)}) copy-start(bf16[384,768]{1,0:T(8,128)(2,1)} %param.4) | copy-start | bytes 1769476
  6.5 251.1 %reduce-scatter.2.cloned.1.call-start = ((), (), s32[]{:S(2)}) async-start(), calls=%async_computation.1 | async-start | bytes 2949120 | tf_op jit(solution)/shard_map/reduce_scatter | solution.py:76
  8.0 160.0 %collective-permute-start.6 = (bf16[384,6,128]{0,2,1:T(8,128)(2,1)S(1)}, bf16[384,6,128]{0,2,1:T(8,128)(2,1)S(1)}, u32[]{:S(2)}, u32[]{:S(2)}) collective-permute-start(bf16[384,6,128]{0,2,1:T(8,128)(2,1)S(1)} %bitcast.36), channel_id=1, source_target_pairs={{8,0},{12,4},{16,8},{20,12},{24,16},{28,20},{32,24},{36,28},{40,32... | collective-permute-start | bytes 1769480 | tf_op jit(solution)/shard_map/ppermute | solution.py:15
  19.5 149.3 %collective-permute-start.1 = (bf16[384,6,128]{0,2,1:T(8,128)(2,1)S(1)}, bf16[384,6,128]{0,2,1:T(8,128)(2,1)}, u32[]{:S(2)}, u32[]{:S(2)}) collective-permute-start(bf16[384,6,128]{0,2,1:T(8,128)(2,1)S(1)} %bitcast.37), channel_id=1, source_target_pairs={{4,0},{8,4},{12,8},{16,12},{20,16},{24,20},{28,24},{32,28},{36,32}... | collective-permute-start | bytes 1769480 | tf_op jit(solution)/shard_map/ppermute | solution.py:15
  23.1 122.2 %collective-permute-start.5 = (bf16[384,6,128]{2,0,1:T(8,128)(2,1)S(1)}, bf16[384,6,128]{2,0,1:T(8,128)(2,1)}, u32[]{:S(2)}, u32[]{:S(2)}) collective-permute-start(bf16[384,6,128]{2,0,1:T(8,128)(2,1)S(1)} %copy.21), channel_id=1, source_target_pairs={{8,0},{12,4},{16,8},{20,12},{24,16},{28,20},{32,24},{36,28},{40,32... | collective-permute-start | bytes 1769480 | tf_op jit(solution)/shard_map/ppermute | solution.py:15
  25.8 114.4 %collective-permute-start = (bf16[384,6,128]{2,0,1:T(8,128)(2,1)S(1)}, bf16[384,6,128]{2,0,1:T(8,128)(2,1)}, u32[]{:S(2)}, u32[]{:S(2)}) collective-permute-start(bf16[384,6,128]{2,0,1:T(8,128)(2,1)S(1)} %copy.21), channel_id=1, source_target_pairs={{4,0},{8,4},{12,8},{16,12},{20,16},{24,20},{28,24},{32,28},{36,32}... | collective-permute-start | bytes 1769480 | tf_op jit(solution)/shard_map/ppermute | solution.py:15
  28.7 79.5 %collective-permute-start.2 = (bf16[384,6,128]{2,0,1:T(8,128)(2,1)S(1)}, bf16[384,6,128]{2,0,1:T(8,128)(2,1)}, u32[]{:S(2)}, u32[]{:S(2)}) collective-permute-start(bf16[384,6,128]{2,0,1:T(8,128)(2,1)S(1)} %copy.24), channel_id=1, source_target_pairs={{4,0},{8,4},{12,8},{16,12},{20,16},{24,20},{28,24},{32,28},{36,32}... | collective-permute-start | bytes 1769480 | tf_op jit(solution)/shard_map/ppermute | solution.py:15
  108.2 19.8 %collective-permute-start.7 = (bf16[384,6,128]{2,0,1:T(8,128)(2,1)S(1)}, bf16[384,6,128]{2,0,1:T(8,128)(2,1)S(1)}, u32[]{:S(2)}, u32[]{:S(2)}) collective-permute-start(bf16[384,6,128]{2,0,1:T(8,128)(2,1)S(1)} %copy.24), channel_id=1, source_target_pairs={{8,0},{12,4},{16,8},{20,12},{24,16},{28,20},{32,24},{36,28},{40,32... | collective-permute-start | bytes 1769480 | tf_op jit(solution)/shard_map/ppermute | solution.py:15
  128.0 21.4 %collective-permute-start.3 = (bf16[6,384]{1,0:T(8,128)(2,1)S(1)}, bf16[6,384]{1,0:T(8,128)(2,1)S(1)}, u32[]{:S(2)}, u32[]{:S(2)}) collective-permute-start(bf16[6,384]{1,0:T(8,128)(2,1)S(1)} %convert_element_type.78), channel_id=1, source_target_pairs={{0,4},{4,8},{8,12},{12,16},{16,20},{20,24},{24,28},{28,32},{32,36}... | collective-permute-start | bytes 13832 | tf_op jit(solution)/shard_map/ppermute | solution.py:15
  140.2 13.8 %collective-permute-start.10 = (bf16[6,384]{1,0:T(8,128)(2,1)S(1)}, bf16[6,384]{1,0:T(8,128)(2,1)S(1)}, u32[]{:S(2)}, u32[]{:S(2)}) collective-permute-start(bf16[6,384]{1,0:T(8,128)(2,1)S(1)} %fusion.5), channel_id=1, source_target_pairs={{0,4},{4,8},{8,12},{12,16},{16,20},{20,24},{24,28},{28,32},{32,36}... | collective-permute-start | bytes 13832 | tf_op jit(solution)/shard_map/ppermute | solution.py:15
  145.2 12.7 %collective-permute-start.8 = (bf16[6,384]{1,0:T(8,128)(2,1)S(1)}, bf16[6,384]{1,0:T(8,128)(2,1)S(1)}, u32[]{:S(2)}, u32[]{:S(2)}) collective-permute-start(bf16[6,384]{1,0:T(8,128)(2,1)S(1)} %convert_element_type.84), channel_id=1, source_target_pairs={{0,8},{4,12},{8,16},{12,20},{16,24},{20,28},{24,32},{28,36},{32,40... | collective-permute-start | bytes 13832 | tf_op jit(solution)/shard_map/ppermute | solution.py:15
  149.5 17.7 %collective-permute-start.11 = (bf16[6,384]{1,0:T(8,128)(2,1)S(1)}, bf16[6,384]{1,0:T(8,128)(2,1)S(1)}, u32[]{:S(2)}, u32[]{:S(2)}) collective-permute-start(bf16[6,384]{1,0:T(8,128)(2,1)S(1)} %fusion.9), channel_id=1, source_target_pairs={{0,8},{4,12},{8,16},{12,20},{16,24},{20,28},{24,32},{28,36},{32,40... | collective-permute-start | bytes 13832 | tf_op jit(solution)/shard_map/ppermute | solution.py:15
  154.1 29.3 %collective-permute-start.4 = (bf16[6,384,128]{1,2,0:T(8,128)(2,1)S(1)}, bf16[6,384,128]{1,2,0:T(8,128)(2,1)S(1)}, u32[]{:S(2)}, u32[]{:S(2)}) collective-permute-start(bf16[6,384,128]{1,2,0:T(8,128)(2,1)S(1)} %fusion.61), channel_id=1, source_target_pairs={{0,4},{4,8},{8,12},{12,16},{16,20},{20,24},{24,28},{28,32},{32,36}... | collective-permute-start | bytes 1769480 | tf_op jit(solution)/shard_map/ppermute | solution.py:15
  157.9 30.8 %collective-permute-start.9 = (bf16[6,384,128]{1,2,0:T(8,128)(2,1)S(1)}, bf16[6,384,128]{1,2,0:T(8,128)(2,1)S(1)}, u32[]{:S(2)}, u32[]{:S(2)}) collective-permute-start(bf16[6,384,128]{1,2,0:T(8,128)(2,1)S(1)} %fusion.64), channel_id=1, source_target_pairs={{0,8},{4,12},{8,16},{12,20},{16,24},{20,28},{24,32},{28,36},{32,40... | collective-permute-start | bytes 1769480 | tf_op jit(solution)/shard_map/ppermute | solution.py:15
  168.0 23.1 %slice-start = ((s8[4718592]{0:T(1024)(128)(4,1)}), s8[4194304]{0:T(1024)(128)(4,1)S(1)}, s32[]{:S(2)}) async-start(s8[4718592]{0:T(1024)(128)(4,1)} %bitcast.34), calls=%async_computation.2 | async-start | bytes 8388608
  188.7 2.4 slice-start.1
Sparse Core Ops, SparseCore 0:
  194.8 62.8 reduce-scatter.1
where the time goes:
time: 266 us; the launch traced here: 265 us
  waiting for transfers between devices  183 us (69%)
  starting transfers between devices  45 us (17%)
  matrix products  15.5 us (6%)
  between operations  13.7 us (5%)
  local copies, waits for them, and re-layouts  3.74 us (1%)
  other arithmetic  3.03 us (1%)
    ppermute x12, waiting for transfers between devices, passed_along(): return lax.ppermute(array, axis, pairs)  120 us
    reduce_scatter x1, waiting for transfers between devices, body(): lax.psum_scatter(jnp.einsum('fc,qf->cq', out_weight, attended, preferred_...  63 us
    ppermute x12, starting transfers between devices, passed_along(): return lax.ppermute(array, axis, pairs)  45 us
    dot_general x5, matrix products, block_part(): jnp.einsum('qhd,khd->hqk', query_part, key_part, preferred_element_type=j...  6.46 us
    dot_general x5, matrix products, block_part(): jnp.einsum('hqk,khd->hqd', weights.astype(jnp.bfloat16), value_part, pref...  5.54 us
  transfers between devices with their start and end apart: 13, of which 7 were waited for; matrix products, arithmetic and copies ran while one was open for 6% of the time, Pallas kernels for 0%

commit v1 on v0

v1 whole, which is shorter than its diff:
```python
import functools
import math

import jax
import jax.numpy as jnp
from jax import lax
from jax.experimental import pallas as pl
from jax.experimental.pallas import tpu as pltpu
from jax.sharding import PartitionSpec as P

HD = 128
SPANS = 64
HEAD_PEERS = 4
CHUNK = 2
SCALE = math.log2(math.e) / math.sqrt(HD)
LOWEST = -1e30


def scores_of(query, key):
    return lax.dot_general(query, key, (((1,), (1,)), ((), ())), preferred_element_type=jnp.float32)


def with_ones(value):
    return jnp.concatenate([value, jnp.ones_like(value)], axis=1)


def widen(column, times):
    return jnp.concatenate([column] * times, axis=1)


def weights_of(scores, shift):
    return jnp.exp2(scores * SCALE - widen(shift, scores.shape[1] // HD)).astype(jnp.bfloat16)


def lanes(h):
    return slice(h * HD, (h + 1) * HD)


def near_kernel(q_ref, k_ref, v_ref, pk_ref, pv_ref, acc_ref, max_ref):
    rows = q_ref.shape[0]
    for h in range(q_ref.shape[1] // HD):
        at = lanes(h)
        query = q_ref[:, at]
        s0 = scores_of(query, k_ref[:, at])
        s1 = scores_of(query, pk_ref[:, at])
        top = jnp.maximum(jnp.max(s0, axis=1, keepdims=True), jnp.max(s1, axis=1, keepdims=True))
        top = jnp.broadcast_to(top, (rows, HD))
        shift = top * SCALE
        acc_ref[h] = jnp.dot(
            weights_of(s0, shift), with_ones(v_ref[:, at]), preferred_element_type=jnp.float32
        ) + jnp.dot(
            weights_of(s1, shift), with_ones(pv_ref[:, at]), preferred_element_type=jnp.float32
        )
        max_ref[h] = top


def far_kernel(first, valid_ref, q_ref, acc_ref, max_ref, *refs):
    *blocks, out_ref = refs
    rows = q_ref.shape[0]
    half = CHUNK * HD
    for i in range(CHUNK):
        h = first + i
        query = q_ref[:, lanes(h)]
        old = max_ref[h]
        scores = []
        top = old
        for b, ref in enumerate(blocks):
            s = scores_of(query, ref[:, lanes(i)])
            peak = jnp.broadcast_to(jnp.max(s, axis=1, keepdims=True), (rows, HD))
            top = jnp.maximum(top, jnp.where(valid_ref[b] > 0, peak, LOWEST))
            scores.append(s)
        shift = top * SCALE
        total = acc_ref[h] * widen(jnp.exp2(old * SCALE - shift), 2)
        for b, ref in enumerate(blocks):
            used = jnp.where(valid_ref[b] > 0, shift, -LOWEST)
            total += jnp.dot(
                weights_of(scores[b], used),
                with_ones(ref[:, half + i * HD : half + (i + 1) * HD]),
                preferred_element_type=jnp.float32,
            )
        out_ref[:, lanes(i)] = (total[:, :HD] / total[:, HD:]).astype(out_ref.dtype)


def in_vmem(count):
    return [pl.BlockSpec(memory_space=pltpu.VMEM)] * count


def near_part(q, k, v, pk, pv):
    rows, width = q.shape
    heads = width // HD
    return pl.pallas_call(
        near_kernel,
        out_shape=(
            jax.ShapeDtypeStruct((heads, rows, 2 * HD), jnp.float32),
            jax.ShapeDtypeStruct((heads, rows, HD), jnp.float32),
        ),
        in_specs=in_vmem(5),
        out_specs=tuple(in_vmem(2)),
        compiler_params=pltpu.CompilerParams(vmem_limit_bytes=32 * 2**20),
        cost_estimate=pl.CostEstimate(
            flops=12 * heads * rows * rows * HD,
            bytes_accessed=10 * rows * width,
            transcendentals=2 * heads * rows * rows,
        ),
        name="near",
    )(q, k, v, pk, pv)


def far_part(first, valid, q, acc, top, blocks):
    rows = q.shape[0]
    return pl.pallas_call(
        functools.partial(far_kernel, first),
        out_shape=jax.ShapeDtypeStruct((rows, CHUNK * HD), jnp.bfloat16),
        in_specs=[pl.BlockSpec(memory_space=pltpu.SMEM)] + in_vmem(3 + len(blocks)),
        out_specs=pl.BlockSpec(memory_space=pltpu.VMEM),
        compiler_params=pltpu.CompilerParams(vmem_limit_bytes=32 * 2**20),
        cost_estimate=pl.CostEstimate(
            flops=6 * len(blocks) * CHUNK * rows * rows * HD,
            bytes_accessed=10 * rows * CHUNK * HD,
            transcendentals=len(blocks) * CHUNK * rows * rows,
        ),
        name=f"far{first}",
    )(valid, q, acc, top, *blocks)


def seq_pairs(step_of):
    return [(s, s + step_of(s)) for s in range(SPANS) if 0 <= s + step_of(s) < SPANS]


PAIR = seq_pairs(lambda s: 1 if s % 2 == 0 else -1)
SHARED = seq_pairs(lambda s: -2 if s % 2 == 0 else 2)
SINGLE = seq_pairs(lambda s: 2 if s % 2 == 0 else -2)


def body(queries, key_states, value_states, out_weight):
    rows, width = queries.shape
    heads = width // HD
    place = lax.axis_index("seq")
    even = place % 2 == 0
    has_after2, has_before2 = place + 2 < SPANS, place >= 2
    shared_ok = jnp.where(even, has_after2, has_before2)
    single_ok = jnp.where(even, has_before2, has_after2)
    swapped_ok = jnp.where(even, place >= 1, place + 1 < SPANS)
    valid = jnp.stack([shared_ok, single_ok, swapped_ok]).astype(jnp.int32)

    pair_key = lax.ppermute(key_states, "seq", PAIR)
    pair_value = lax.ppermute(value_states, "seq", PAIR)
    step = CHUNK * HD
    packed = [
        jnp.concatenate([key_states[:, a : a + step], value_states[:, a : a + step]], axis=1)
        for a in range(0, width, step)
    ]
    shared, single, swapped = [], [], []
    for chunk in packed:
        shared.append(lax.ppermute(chunk, "seq", SHARED))
        single.append(lax.ppermute(chunk, "seq", SINGLE))
    for chunk in shared:
        swapped.append(lax.ppermute(chunk, "seq", PAIR))

    acc, top = near_part(queries, key_states, value_states, pair_key, pair_value)
    attended = [
        far_part(i * CHUNK, valid, queries, acc, top, [shared[i], single[i], swapped[i]])
        for i in range(heads // CHUNK)
    ]
    return projected(jnp.concatenate(attended, axis=1), out_weight)


def projected(attended, out_weight):
    z = lax.axis_index("head")
    cols = out_weight.shape[1] // HEAD_PEERS
    low = z < 2
    half = attended.shape[0] // 2

    def term(part, which):
        weight = lax.dynamic_slice_in_dim(out_weight, which * cols, cols, 1)
        return jnp.dot(part, weight, preferred_element_type=jnp.float32)

    ends_in = [(0, 1), (3, 2)]
    across = [(1, 2), (2, 1)]
    outward = [(1, 0), (2, 3)]

    def sent(value, pairs):
        return lax.ppermute(value.astype(jnp.bfloat16), "head", pairs)

    outs = []
    for r in range(2):
        part = attended[r * half : (r + 1) * half]
        far = term(part, jnp.where(low, 3, 0))
        mid = term(part, jnp.where(low, 2, 1))
        beside = term(part, z ^ 1)
        own = term(part, z)
        far_in = sent(far, ends_in)
        mid_in = sent(mid, ends_in)
        beside_in = sent(beside, ends_in)
        crossed_far = sent(far + far_in, across)
        crossed_mid = sent(mid + mid_in, across)
        out_in = sent(beside + crossed_far, outward)
        outs.append((own + out_in + beside_in + crossed_mid).astype(jnp.bfloat16))
    return jnp.concatenate(outs, axis=0)


def solution(mesh):
    placed = (P("seq", "head"), P("seq", "head"), P("seq", "head"), P("head", None))
    return jax.shard_map(
        body, mesh=mesh, in_specs=placed, out_specs=P("seq", "head"), check_vma=False
    )
```

time: 266 us -> 149 us (0.56)
  the two profiles are of different devices: /device:TPU:24 before, /device:TPU:30 now
where the time goes in v1:
time: 149 us; the launch traced here: 148 us
  starting transfers between devices  87.9 us (59%)
  waiting for transfers between devices  32.8 us (22%)
  Pallas kernels  12.9 us (9%)
  matrix products  6.06 us (4%)
  local copies, waits for them, and re-layouts  5.18 us (3%)
  other arithmetic  2.8 us (2%)
    ppermute x12, starting transfers between devices, sent(): return lax.ppermute(value.astype(jnp.bfloat16), 'head', pairs)  46.1 us
    ppermute x12, waiting for transfers between devices, sent(): return lax.ppermute(value.astype(jnp.bfloat16), 'head', pairs)  25.8 us
    ppermute x3, starting transfers between devices, body(): swapped.append(lax.ppermute(chunk, 'seq', PAIR))  18.4 us
    ppermute x3, starting transfers between devices, body(): single.append(lax.ppermute(chunk, 'seq', SINGLE))  10.4 us
    pallas_call x3, Pallas kernels, far_part(): pl.pallas_call(functools.partial(far_kernel, first), out_shape=jax.ShapeD...  9.46 us
    ppermute x3, starting transfers between devices, body(): shared.append(lax.ppermute(chunk, 'seq', SHARED))  6.91 us
    dot_general x8, matrix products, term(): return jnp.dot(part, weight, preferred_element_type=jnp.float32)  6.06 us
    ppermute x1, starting transfers between devices, body(): pair_key = lax.ppermute(key_states, 'seq', PAIR)  5.92 us
  transfers between devices with their start and end apart: 23, of which 8 were waited for; matrix products, arithmetic and copies ran while one was open for 4% of the time, Pallas kernels for 7%

profile of v1, /device:TPU:30, one launch (start us, length us, event | category | flops | bytes accessed | tf_op | source)
XLA Modules:
  0.0 148.1 jit_solution(13475744273765815083)
XLA Ops:
  1.4 2.9 %collective-permute-start.8 = (bf16[384,512]{1,0:T(8,128)(2,1)S(1)}, bf16[384,512]{1,0:T(8,128)(2,1)S(1)}, u32[]{:S(2)}, u32[]{:S(2)}) collective-permute-start(bf16[384,512]{1,0:T(8,128)(2,1)S(1)} %pad_maximum_fusion.4), channel_id=1, source_target_pairs={{4,12},{8,0},{12,20},{16,8},{20,28},{24,16},{28,36},{32,24},{36,44... | collective-permute-start | bytes 1179656 | tf_op jit(solution)/shard_map/ppermute | solution.py:155
  4.3 5.9 %collective-permute-start = (bf16[384,768]{1,0:T(8,128)(2,1)S(1)}, bf16[384,768]{1,0:T(8,128)(2,1)S(1)}, u32[]{:S(2)}, u32[]{:S(2)}) collective-permute-start(bf16[384,768]{1,0:T(8,128)(2,1)S(1)} %copy-done.1), channel_id=1, source_target_pairs={{0,4},{4,0},{8,12},{12,8},{16,20},{20,16},{24,28},{28,24},{32,36},... | collective-permute-start | bytes 1769480 | tf_op jit(solution)/shard_map/ppermute | solution.py:146
  10.4 3.7 %collective-permute-start.9 = (bf16[384,512]{1,0:T(8,128)(2,1)S(1)}, bf16[384,512]{1,0:T(8,128)(2,1)S(1)}, u32[]{:S(2)}, u32[]{:S(2)}) collective-permute-start(bf16[384,512]{1,0:T(8,128)(2,1)S(1)} %pad_maximum_fusion.4), channel_id=1, source_target_pairs={{0,8},{8,16},{12,4},{16,24},{20,12},{24,32},{28,20},{32,40},{36,28... | collective-permute-start | bytes 1179656 | tf_op jit(solution)/shard_map/ppermute | solution.py:156
  14.8 2.1 %collective-permute-start.5 = (bf16[384,512]{1,0:T(8,128)(2,1)}, bf16[384,512]{1,0:T(8,128)(2,1)S(1)}, u32[]{:S(2)}, u32[]{:S(2)}) collective-permute-start(bf16[384,512]{1,0:T(8,128)(2,1)} %pad_maximum_fusion.3), channel_id=1, source_target_pairs={{4,12},{8,0},{12,20},{16,8},{20,28},{24,16},{28,36},{32,24},{36,44... | collective-permute-start | bytes 1179656 | tf_op jit(solution)/shard_map/ppermute | solution.py:155
  17.8 1.9 %collective-permute-start.2 = (bf16[384,512]{1,0:T(8,128)(2,1)}, bf16[384,512]{1,0:T(8,128)(2,1)S(1)}, u32[]{:S(2)}, u32[]{:S(2)}) collective-permute-start(bf16[384,512]{1,0:T(8,128)(2,1)} %pad_maximum_fusion.2), channel_id=1, source_target_pairs={{4,12},{8,0},{12,20},{16,8},{20,28},{24,16},{28,36},{32,24},{36,44... | collective-permute-start | bytes 1179656 | tf_op jit(solution)/shard_map/ppermute | solution.py:155
  19.7 2.1 %collective-permute-done.9.refs_1_ = bf16[384,512]{1,0:T(8,128)(2,1)S(1)} collective-permute-done((bf16[384,512]{1,0:T(8,128)(2,1)S(1)}, bf16[384,512]{1,0:T(8,128)(2,1)S(1)}, u32[]{:S(2)}, u32[]{:S(2)}) %collective-permute-start.9) | collective-permute-done | bytes 393248 | tf_op jit(solution)/shard_map/ppermute | solution.py:156
  21.8 18.4 %collective-permute-start.10 = (bf16[384,512]{1,0:T(8,128)(2,1)S(1)}, bf16[384,512]{1,0:T(8,128)(2,1)}, u32[]{:S(2)}, u32[]{:S(2)}) collective-permute-start(bf16[384,512]{1,0:T(8,128)(2,1)S(1)} %collective-permute-done.8.refs_0_), channel_id=1, source_target_pairs={{0,4},{4,0},{8,12},{12,8},{16,20},{20,16},{24,28},{28,24},{32,36},... | collective-permute-start | bytes 1179656 | tf_op jit(solution)/shard_map/ppermute | solution.py:158
  40.2 1.4 collective-permute-done.5.refs_0_
  41.6 1.9 %collective-permute-start.6 = (bf16[384,512]{1,0:T(8,128)(2,1)}, bf16[384,512]{1,0:T(8,128)(2,1)}, u32[]{:S(2)}, u32[]{:S(2)}) collective-permute-start(bf16[384,512]{1,0:T(8,128)(2,1)} %pad_maximum_fusion.3), channel_id=1, source_target_pairs={{0,8},{8,16},{12,4},{16,24},{20,12},{24,32},{28,20},{32,40},{36,28... | collective-permute-start | bytes 1179656 | tf_op jit(solution)/shard_map/ppermute | solution.py:156
  43.5 3.6 %collective-permute-done.2.refs_0_ = bf16[384,512]{1,0:T(8,128)(2,1)S(1)} collective-permute-done((bf16[384,512]{1,0:T(8,128)(2,1)}, bf16[384,512]{1,0:T(8,128)(2,1)S(1)}, u32[]{:S(2)}, u32[]{:S(2)}) %collective-permute-start.2) | collective-permute-done | bytes 393248 | tf_op jit(solution)/shard_map/ppermute | solution.py:155
  47.9 4.8 %collective-permute-start.3 = (bf16[384,512]{1,0:T(8,128)(2,1)}, bf16[384,512]{1,0:T(8,128)(2,1)}, u32[]{:S(2)}, u32[]{:S(2)}) collective-permute-start(bf16[384,512]{1,0:T(8,128)(2,1)} %pad_maximum_fusion.2), channel_id=1, source_target_pairs={{0,8},{8,16},{12,4},{16,24},{20,12},{24,32},{28,20},{32,40},{36,28... | collective-permute-start | bytes 1179656 | tf_op jit(solution)/shard_map/ppermute | solution.py:156
  55.8 3.4 %near.1 = (f32[6,384,256]{2,1,0:T(8,128)S(1)}, f32[6,384,128]{2,1,0:T(8,128)S(1)}) custom-call(bf16[384,768]{1,0:T(8,128)(2,1)S(1)} %copy-done, bf16[384,768]{1,0:T(8,128)(2,1)S(1)} %copy-done.1, bf16[384,768]{1,0:T(8,128)(2,1)S(1)} %copy-done.2, bf16[384,768]{1,0:T(8,128)(2,1)S(1)} %copy-done.4, bf16[384,768]{1,0:T(8,128)(2,1)S(1)} %copy-done.6), custom_call_target="tpu_custom_call" | custom-call | flops 1358954496 | bytes 2949120 | tf_op jit(solution)/shard_map/near/pallas_call | solution.py:91
  59.3 3.2 %far4.1 = bf16[384,256]{1,0:T(8,128)(2,1)S(1)} custom-call(s32[3]{0:T(128)S(1)} %add_convert_fusion.6.valid_ref, bf16[384,768]{1,0:T(8,128)(2,1)S(1)} %copy-done, f32[6,384,256]{2,1,0:T(8,128)S(1)} %get-tuple-element.7.acc_ref, f32[6,384,128]{2,1,0:T(8,128)S(1)} %get-tuple-element.8.max_ref, bf16[384,512]{1,0:T(8,128)(2,1)S(1)} %collective-permute-done.8.refs_0_, ...), custom_call_target="tpu_custom_call" | custom-call | flops 679477248 | bytes 983040 | tf_op jit(solution)/shard_map/far4/pallas_call | solution.py:111
  62.5 3.2 %far2.1 = bf16[384,256]{1,0:T(8,128)(2,1)S(1)} custom-call(s32[3]{0:T(128)S(1)} %add_convert_fusion.6.valid_ref, bf16[384,768]{1,0:T(8,128)(2,1)S(1)} %copy-done, f32[6,384,256]{2,1,0:T(8,128)S(1)} %get-tuple-element.7.acc_ref, f32[6,384,128]{2,1,0:T(8,128)S(1)} %get-tuple-element.8.max_ref, bf16[384,512]{1,0:T(8,128)(2,1)S(1)} %collective-permute-done.5.refs_0_, ...), custom_call_target="tpu_custom_call" | custom-call | flops 679477248 | bytes 983040 | tf_op jit(solution)/shard_map/far2/pallas_call | solution.py:111
  65.6 3.1 %far0.1 = bf16[384,256]{1,0:T(8,128)(2,1)S(1)} custom-call(s32[3]{0:T(128)S(1)} %add_convert_fusion.6.valid_ref, bf16[384,768]{1,0:T(8,128)(2,1)S(1)} %copy-done, f32[6,384,256]{2,1,0:T(8,128)S(1)} %get-tuple-element.7.acc_ref, f32[6,384,128]{2,1,0:T(8,128)S(1)} %get-tuple-element.8.max_ref, bf16[384,512]{1,0:T(8,128)(2,1)S(1)} %collective-permute-done.2.refs_0_, ...), custom_call_target="tpu_custom_call" | custom-call | flops 679477248 | bytes 983040 | tf_op jit(solution)/shard_map/far0/pallas_call | solution.py:111
  69.7 22.7 %collective-permute-start.17 = (bf16[192,768]{1,0:T(8,128)(2,1)S(1)}, bf16[192,768]{1,0:T(8,128)(2,1)S(1)}, u32[]{:S(2)}, u32[]{:S(2)}) collective-permute-start(bf16[192,768]{1,0:T(8,128)(2,1)S(1)} %get-tuple-element.21), channel_id=1, source_target_pairs={{0,1},{3,2},{4,5},{7,6},{8,9},{11,10},{12,13},{15,14},{16,17},{19,... | collective-permute-start | bytes 884744 | tf_op jit(solution)/shard_map/ppermute | solution.py:183
  97.2 2.5 %collective-permute-done.17 = bf16[192,768]{1,0:T(8,128)(2,1)S(1)} collective-permute-done((bf16[192,768]{1,0:T(8,128)(2,1)S(1)}, bf16[192,768]{1,0:T(8,128)(2,1)S(1)}, u32[]{:S(2)}, u32[]{:S(2)}) %collective-permute-start.17) | collective-permute-done | bytes 294944 | tf_op jit(solution)/shard_map/ppermute | solution.py:183
  100.4 5.6 %collective-permute-done.21 = bf16[192,768]{1,0:T(8,128)(2,1)S(1)} collective-permute-done((bf16[192,768]{1,0:T(8,128)(2,1)S(1)}, bf16[192,768]{1,0:T(8,128)(2,1)S(1)}, u32[]{:S(2)}, u32[]{:S(2)}) %collective-permute-start.21) | collective-permute-done | bytes 294944 | tf_op jit(solution)/shard_map/ppermute | solution.py:183
  106.8 11.5 %collective-permute-done.11 = bf16[192,768]{1,0:T(8,128)(2,1)S(1)} collective-permute-done((bf16[192,768]{1,0:T(8,128)(2,1)S(1)}, bf16[192,768]{1,0:T(8,128)(2,1)S(1)}, u32[]{:S(2)}, u32[]{:S(2)}) %collective-permute-start.11) | collective-permute-done | bytes 294944 | tf_op jit(solution)/shard_map/ppermute | solution.py:183
  119.5 7.2 %collective-permute-start.20 = (bf16[192,768]{1,0:T(8,128)(2,1)S(1)}, bf16[192,768]{1,0:T(8,128)(2,1)S(1)}, u32[]{:S(2)}, u32[]{:S(2)}) collective-permute-start(bf16[192,768]{1,0:T(8,128)(2,1)S(1)} %get-tuple-element.12), channel_id=1, source_target_pairs={{0,1},{3,2},{4,5},{7,6},{8,9},{11,10},{12,13},{15,14},{16,17},{19,... | collective-permute-start | bytes 884744 | tf_op jit(solution)/shard_map/ppermute | solution.py:183
  129.1 7.0 %collective-permute-start.14 = (bf16[192,768]{1,0:T(8,128)(2,1)S(1)}, bf16[192,768]{1,0:T(8,128)(2,1)}, u32[]{:S(2)}, u32[]{:S(2)}) collective-permute-start(bf16[192,768]{1,0:T(8,128)(2,1)S(1)} %get-tuple-element.10), channel_id=1, source_target_pairs={{0,1},{3,2},{4,5},{7,6},{8,9},{11,10},{12,13},{15,14},{16,17},{19,... | collective-permute-start | bytes 884744 | tf_op jit(solution)/shard_map/ppermute | solution.py:183
  137.5 1.7 %fusion.4 = bf16[192,768]{1,0:T(8,128)(2,1)S(1)} fusion(bf16[768,3072]{1,0:T(8,128)(2,1)} %param.7, s32[]{:T(128)S(6)} %select_n.46, bf16[192,768]{1,0:T(8,128)(2,1)S(1)} %collective-permute-done.22, bf16[192,768]{1,0:T(8,128)(2,1)S(1)} %collective-permute-done.20, bf16[192,768]{1,0:T(8,128)(2,1)S(1)} %collective-permute-done.19, ...), kind=kOutput, calls=%fused_computation.6 | convolution fusion | flops 227524608 | bytes 2654212 | tf_op jit(solution)/shard_map/dot_general | solution.py:176
  140.4 4.9 %collective-permute-done.13 = bf16[192,768]{1,0:T(8,128)(2,1)} collective-permute-done((bf16[192,768]{1,0:T(8,128)(2,1)S(1)}, bf16[192,768]{1,0:T(8,128)(2,1)}, u32[]{:S(2)}, u32[]{:S(2)}) %collective-permute-start.13) | collective-permute-done | bytes 294944 | tf_op jit(solution)/shard_map/ppermute | solution.py:183
  145.4 1.8 %fusion.5 = bf16[192,768]{1,0:T(8,128)(2,1)S(1)} fusion(bf16[768,3072]{1,0:T(8,128)(2,1)} %param.7, s32[]{:T(128)S(6)} %select_n.46, bf16[192,768]{1,0:T(8,128)(2,1)S(1)} %collective-permute-done.16, bf16[192,768]{1,0:T(8,128)(2,1)} %collective-permute-done.14, bf16[192,768]{1,0:T(8,128)(2,1)} %collective-permute-done.13, ...), kind=kOutput, calls=%fused_computation.7 | convolution fusion | flops 227524608 | bytes 2654212 | tf_op jit(solution)/shard_map/dot_general | solution.py:176
  (65 shorter events, 21.1 us)
Async XLA Ops:
  1.4 52.3 %copy-start = (bf16[384,768]{1,0:T(8,128)(2,1)S(1)}, bf16[384,768]{1,0:T(8,128)(2,1)}, u32[]{:S(2)}) copy-start(bf16[384,768]{1,0:T(8,128)(2,1)} %q_ref.7) | copy-start | bytes 1769476
  1.4 16.3 %collective-permute-start.8 = (bf16[384,512]{1,0:T(8,128)(2,1)S(1)}, bf16[384,512]{1,0:T(8,128)(2,1)S(1)}, u32[]{:S(2)}, u32[]{:S(2)}) collective-permute-start(bf16[384,512]{1,0:T(8,128)(2,1)S(1)} %pad_maximum_fusion.4), channel_id=1, source_target_pairs={{4,12},{8,0},{12,20},{16,8},{20,28},{24,16},{28,36},{32,24},{36,44... | collective-permute-start | bytes 1179656 | tf_op jit(solution)/shard_map/ppermute | solution.py:155
  4.3 42.8 %collective-permute-start = (bf16[384,768]{1,0:T(8,128)(2,1)S(1)}, bf16[384,768]{1,0:T(8,128)(2,1)S(1)}, u32[]{:S(2)}, u32[]{:S(2)}) collective-permute-start(bf16[384,768]{1,0:T(8,128)(2,1)S(1)} %copy-done.1), channel_id=1, source_target_pairs={{0,4},{4,0},{8,12},{12,8},{16,20},{20,16},{24,28},{28,24},{32,36},... | collective-permute-start | bytes 1769480 | tf_op jit(solution)/shard_map/ppermute | solution.py:146
  10.2 42.5 %collective-permute-start.1 = (bf16[384,768]{1,0:T(8,128)(2,1)S(1)}, bf16[384,768]{1,0:T(8,128)(2,1)S(1)}, u32[]{:S(2)}, u32[]{:S(2)}) collective-permute-start(bf16[384,768]{1,0:T(8,128)(2,1)S(1)} %copy-done.2), channel_id=1, source_target_pairs={{0,4},{4,0},{8,12},{12,8},{16,20},{20,16},{24,28},{28,24},{32,36},... | collective-permute-start | bytes 1769480 | tf_op jit(solution)/shard_map/ppermute | solution.py:147
  10.4 11.4 %collective-permute-start.9 = (bf16[384,512]{1,0:T(8,128)(2,1)S(1)}, bf16[384,512]{1,0:T(8,128)(2,1)S(1)}, u32[]{:S(2)}, u32[]{:S(2)}) collective-permute-start(bf16[384,512]{1,0:T(8,128)(2,1)S(1)} %pad_maximum_fusion.4), channel_id=1, source_target_pairs={{0,8},{8,16},{12,4},{16,24},{20,12},{24,32},{28,20},{32,40},{36,28... | collective-permute-start | bytes 1179656 | tf_op jit(solution)/shard_map/ppermute | solution.py:156
  14.8 26.8 %collective-permute-start.5 = (bf16[384,512]{1,0:T(8,128)(2,1)}, bf16[384,512]{1,0:T(8,128)(2,1)S(1)}, u32[]{:S(2)}, u32[]{:S(2)}) collective-permute-start(bf16[384,512]{1,0:T(8,128)(2,1)} %pad_maximum_fusion.3), channel_id=1, source_target_pairs={{4,12},{8,0},{12,20},{16,8},{20,28},{24,16},{28,36},{32,24},{36,44... | collective-permute-start | bytes 1179656 | tf_op jit(solution)/shard_map/ppermute | solution.py:155
  17.8 29.3 %collective-permute-start.2 = (bf16[384,512]{1,0:T(8,128)(2,1)}, bf16[384,512]{1,0:T(8,128)(2,1)S(1)}, u32[]{:S(2)}, u32[]{:S(2)}) collective-permute-start(bf16[384,512]{1,0:T(8,128)(2,1)} %pad_maximum_fusion.2), channel_id=1, source_target_pairs={{4,12},{8,0},{12,20},{16,8},{20,28},{24,16},{28,36},{32,24},{36,44... | collective-permute-start | bytes 1179656 | tf_op jit(solution)/shard_map/ppermute | solution.py:155
  21.8 37.4 %collective-permute-start.10 = (bf16[384,512]{1,0:T(8,128)(2,1)S(1)}, bf16[384,512]{1,0:T(8,128)(2,1)}, u32[]{:S(2)}, u32[]{:S(2)}) collective-permute-start(bf16[384,512]{1,0:T(8,128)(2,1)S(1)} %collective-permute-done.8.refs_0_), channel_id=1, source_target_pairs={{0,4},{4,0},{8,12},{12,8},{16,20},{20,16},{24,28},{28,24},{32,36},... | collective-permute-start | bytes 1179656 | tf_op jit(solution)/shard_map/ppermute | solution.py:158
  41.6 20.8 %collective-permute-start.6 = (bf16[384,512]{1,0:T(8,128)(2,1)}, bf16[384,512]{1,0:T(8,128)(2,1)}, u32[]{:S(2)}, u32[]{:S(2)}) collective-permute-start(bf16[384,512]{1,0:T(8,128)(2,1)} %pad_maximum_fusion.3), channel_id=1, source_target_pairs={{0,8},{8,16},{12,4},{16,24},{20,12},{24,32},{28,20},{32,40},{36,28... | collective-permute-start | bytes 1179656 | tf_op jit(solution)/shard_map/ppermute | solution.py:156
  47.1 15.3 %collective-permute-start.7 = (bf16[384,512]{1,0:T(8,128)(2,1)S(1)}, bf16[384,512]{1,0:T(8,128)(2,1)}, u32[]{:S(2)}, u32[]{:S(2)}) collective-permute-start(bf16[384,512]{1,0:T(8,128)(2,1)S(1)} %collective-permute-done.5.refs_0_), channel_id=1, source_target_pairs={{0,4},{4,0},{8,12},{12,8},{16,20},{20,16},{24,28},{28,24},{32,36},... | collective-permute-start | bytes 1179656 | tf_op jit(solution)/shard_map/ppermute | solution.py:158
  47.9 17.7 %collective-permute-start.3 = (bf16[384,512]{1,0:T(8,128)(2,1)}, bf16[384,512]{1,0:T(8,128)(2,1)}, u32[]{:S(2)}, u32[]{:S(2)}) collective-permute-start(bf16[384,512]{1,0:T(8,128)(2,1)} %pad_maximum_fusion.2), channel_id=1, source_target_pairs={{0,8},{8,16},{12,4},{16,24},{20,12},{24,32},{28,20},{32,40},{36,28... | collective-permute-start | bytes 1179656 | tf_op jit(solution)/shard_map/ppermute | solution.py:156
  53.6 12.1 %collective-permute-start.4 = (bf16[384,512]{1,0:T(8,128)(2,1)S(1)}, bf16[384,512]{1,0:T(8,128)(2,1)}, u32[]{:S(2)}, u32[]{:S(2)}) collective-permute-start(bf16[384,512]{1,0:T(8,128)(2,1)S(1)} %collective-permute-done.2.refs_0_), channel_id=1, source_target_pairs={{0,4},{4,0},{8,12},{12,8},{16,20},{20,16},{24,28},{28,24},{32,36},... | collective-permute-start | bytes 1179656 | tf_op jit(solution)/shard_map/ppermute | solution.py:158
  69.7 30.0 %collective-permute-start.17 = (bf16[192,768]{1,0:T(8,128)(2,1)S(1)}, bf16[192,768]{1,0:T(8,128)(2,1)S(1)}, u32[]{:S(2)}, u32[]{:S(2)}) collective-permute-start(bf16[192,768]{1,0:T(8,128)(2,1)S(1)} %get-tuple-element.21), channel_id=1, source_target_pairs={{0,1},{3,2},{4,5},{7,6},{8,9},{11,10},{12,13},{15,14},{16,17},{19,... | collective-permute-start | bytes 884744 | tf_op jit(solution)/shard_map/ppermute | solution.py:183
  92.8 13.2 %collective-permute-start.21 = (bf16[192,768]{1,0:T(8,128)(2,1)S(1)}, bf16[192,768]{1,0:T(8,128)(2,1)S(1)}, u32[]{:S(2)}, u32[]{:S(2)}) collective-permute-start(bf16[192,768]{1,0:T(8,128)(2,1)S(1)} %get-tuple-element.19), channel_id=1, source_target_pairs={{0,1},{3,2},{4,5},{7,6},{8,9},{11,10},{12,13},{15,14},{16,17},{19,... | collective-permute-start | bytes 884744 | tf_op jit(solution)/shard_map/ppermute | solution.py:183
  94.6 33.4 %collective-permute-start.15 = (bf16[192,768]{1,0:T(8,128)(2,1)S(1)}, bf16[192,768]{1,0:T(8,128)(2,1)S(1)}, u32[]{:S(2)}, u32[]{:S(2)}) collective-permute-start(bf16[192,768]{1,0:T(8,128)(2,1)S(1)} %get-tuple-element.23), channel_id=1, source_target_pairs={{0,1},{3,2},{4,5},{7,6},{8,9},{11,10},{12,13},{15,14},{16,17},{19,... | collective-permute-start | bytes 884744 | tf_op jit(solution)/shard_map/ppermute | solution.py:183
  95.9 22.4 %collective-permute-start.11 = (bf16[192,768]{1,0:T(8,128)(2,1)S(1)}, bf16[192,768]{1,0:T(8,128)(2,1)S(1)}, u32[]{:S(2)}, u32[]{:S(2)}) collective-permute-start(bf16[192,768]{1,0:T(8,128)(2,1)S(1)} %get-tuple-element.25), channel_id=1, source_target_pairs={{0,1},{3,2},{4,5},{7,6},{8,9},{11,10},{12,13},{15,14},{16,17},{19,... | collective-permute-start | bytes 884744 | tf_op jit(solution)/shard_map/ppermute | solution.py:183
  99.8 19.3 %collective-permute-start.18 = (bf16[192,768]{1,0:T(8,128)(2,1)S(1)}, bf16[192,768]{1,0:T(8,128)(2,1)S(1)}, u32[]{:S(2)}, u32[]{:S(2)}) collective-permute-start(bf16[192,768]{1,0:T(8,128)(2,1)S(1)} %add_convert_fusion.2), channel_id=1, source_target_pairs={{1,2},{2,1},{5,6},{6,5},{9,10},{10,9},{13,14},{14,13},{17,18},{18,... | collective-permute-start | bytes 884744 | tf_op jit(solution)/shard_map/ppermute | solution.py:183
  106.1 30.1 %collective-permute-start.22 = (bf16[192,768]{1,0:T(8,128)(2,1)S(1)}, bf16[192,768]{1,0:T(8,128)(2,1)S(1)}, u32[]{:S(2)}, u32[]{:S(2)}) collective-permute-start(bf16[192,768]{1,0:T(8,128)(2,1)S(1)} %add_convert_fusion), channel_id=1, source_target_pairs={{1,2},{2,1},{5,6},{6,5},{9,10},{10,9},{13,14},{14,13},{17,18},{18,... | collective-permute-start | bytes 884744 | tf_op jit(solution)/shard_map/ppermute | solution.py:183
  118.3 10.4 %collective-permute-start.12 = (bf16[192,768]{1,0:T(8,128)(2,1)S(1)}, bf16[192,768]{1,0:T(8,128)(2,1)S(1)}, u32[]{:S(2)}, u32[]{:S(2)}) collective-permute-start(bf16[192,768]{1,0:T(8,128)(2,1)S(1)} %add_convert_fusion.5), channel_id=1, source_target_pairs={{1,2},{2,1},{5,6},{6,5},{9,10},{10,9},{13,14},{14,13},{17,18},{18,... | collective-permute-start | bytes 884744 | tf_op jit(solution)/shard_map/ppermute | solution.py:183
  119.5 18.0 %collective-permute-start.20 = (bf16[192,768]{1,0:T(8,128)(2,1)S(1)}, bf16[192,768]{1,0:T(8,128)(2,1)S(1)}, u32[]{:S(2)}, u32[]{:S(2)}) collective-permute-start(bf16[192,768]{1,0:T(8,128)(2,1)S(1)} %get-tuple-element.12), channel_id=1, source_target_pairs={{0,1},{3,2},{4,5},{7,6},{8,9},{11,10},{12,13},{15,14},{16,17},{19,... | collective-permute-start | bytes 884744 | tf_op jit(solution)/shard_map/ppermute | solution.py:183
  126.6 10.8 %collective-permute-start.19 = (bf16[192,768]{1,0:T(8,128)(2,1)S(1)}, bf16[192,768]{1,0:T(8,128)(2,1)S(1)}, u32[]{:S(2)}, u32[]{:S(2)}) collective-permute-start(bf16[192,768]{1,0:T(8,128)(2,1)S(1)} %get-tuple-element.11), channel_id=1, source_target_pairs={{1,0},{2,3},{5,4},{6,7},{9,8},{10,11},{13,12},{14,15},{17,16},{18,... | collective-permute-start | bytes 884744 | tf_op jit(solution)/shard_map/ppermute | solution.py:183
  128.0 11.2 %collective-permute-start.16 = (bf16[192,768]{1,0:T(8,128)(2,1)S(1)}, bf16[192,768]{1,0:T(8,128)(2,1)S(1)}, u32[]{:S(2)}, u32[]{:S(2)}) collective-permute-start(bf16[192,768]{1,0:T(8,128)(2,1)S(1)} %add_convert_fusion.3), channel_id=1, source_target_pairs={{1,2},{2,1},{5,6},{6,5},{9,10},{10,9},{13,14},{14,13},{17,18},{18,... | collective-permute-start | bytes 884744 | tf_op jit(solution)/shard_map/ppermute | solution.py:183
  129.1 11.3 %collective-permute-start.14 = (bf16[192,768]{1,0:T(8,128)(2,1)S(1)}, bf16[192,768]{1,0:T(8,128)(2,1)}, u32[]{:S(2)}, u32[]{:S(2)}) collective-permute-start(bf16[192,768]{1,0:T(8,128)(2,1)S(1)} %get-tuple-element.10), channel_id=1, source_target_pairs={{0,1},{3,2},{4,5},{7,6},{8,9},{11,10},{12,13},{15,14},{16,17},{19,... | collective-permute-start | bytes 884744 | tf_op jit(solution)/shard_map/ppermute | solution.py:183
  136.1 9.2 %collective-permute-start.13 = (bf16[192,768]{1,0:T(8,128)(2,1)S(1)}, bf16[192,768]{1,0:T(8,128)(2,1)}, u32[]{:S(2)}, u32[]{:S(2)}) collective-permute-start(bf16[192,768]{1,0:T(8,128)(2,1)S(1)} %get-tuple-element.9), channel_id=1, source_target_pairs={{1,0},{2,3},{5,4},{6,7},{9,8},{10,11},{13,12},{14,15},{17,16},{18,... | collective-permute-start | bytes 884744 | tf_op jit(solution)/shard_map/ppermute | solution.py:183
  (8 other events, 30.0 us)

commit v2 on v1

v2 whole, which is shorter than its diff:
```python
import functools
import math

import jax
import jax.numpy as jnp
from jax import lax
from jax.experimental import pallas as pl
from jax.experimental.pallas import tpu as pltpu
from jax.sharding import PartitionSpec as P

HD = 128
SPANS = 64
HEAD_PEERS = 4
ROW = 8
DIRECT = 4
WEIGHT = 30
SCALE = math.log2(math.e) / math.sqrt(HD)
LOWEST = -1e30


def scores_of(query, key):
    return lax.dot_general(query, key, (((1,), (1,)), ((), ())), preferred_element_type=jnp.float32)


def with_ones(value):
    return jnp.concatenate([value, jnp.ones_like(value)], axis=1)


def widen(column, times):
    return jnp.concatenate([column] * times, axis=1)


def weights_of(scores, shift):
    return jnp.exp2(scores * SCALE - widen(shift, scores.shape[1] // HD)).astype(jnp.bfloat16)


def inverse(x):
    guess = pl.reciprocal(x, approx=True)
    return guess * (2.0 - x * guess)


def lanes(h):
    return slice(h * HD, (h + 1) * HD)


def near_kernel(q_ref, k_ref, v_ref, pk_ref, pv_ref, state_ref):
    rows = q_ref.shape[0]
    for h in range(q_ref.shape[1] // HD):
        at = lanes(h)
        query = q_ref[:, at]
        s0 = scores_of(query, k_ref[:, at])
        s1 = scores_of(query, pk_ref[:, at])
        top = jnp.maximum(jnp.max(s0, axis=1, keepdims=True), jnp.max(s1, axis=1, keepdims=True))
        top = jnp.broadcast_to(top, (rows, HD))
        shift = top * SCALE
        state_ref[h, :, : 2 * HD] = jnp.dot(
            weights_of(s0, shift), with_ones(v_ref[:, at]), preferred_element_type=jnp.float32
        ) + jnp.dot(
            weights_of(s1, shift), with_ones(pv_ref[:, at]), preferred_element_type=jnp.float32
        )
        state_ref[h, :, 2 * HD :] = top


def far_kernel(first, counts, closes, valid_ref, q_ref, state_ref, *refs):
    *blocks, out_ref = refs
    half = blocks[0].shape[1] // 2
    groups, at = [], 0
    for count in counts:
        groups.append(blocks[at : at + count])
        at += count
    rows = q_ref.shape[0]

    def part(group, lane):
        value = group[0][:, lane]
        for ref in group[1:]:
            value = value + ref[:, lane]
        return value

    for i in range(half // HD):
        h = first + i
        query = q_ref[:, lanes(h)]
        held = h if state_ref.shape[0] > half // HD else i
        old = state_ref[held, :, 2 * HD :]
        before = state_ref[held, :, : 2 * HD]
        scores = []
        top = old
        for b, group in enumerate(groups):
            s = scores_of(query, part(group, lanes(i)))
            peak = jnp.broadcast_to(jnp.max(s, axis=1, keepdims=True), (rows, HD))
            top = jnp.maximum(top, jnp.where(valid_ref[b] > 0, peak, LOWEST))
            scores.append(s)
        shift = top * SCALE
        total = before * widen(jnp.exp2(old * SCALE - shift), 2)
        for b, group in enumerate(groups):
            used = jnp.where(valid_ref[b] > 0, shift, -LOWEST)
            value = part(group, slice(half + i * HD, half + (i + 1) * HD))
            total += jnp.dot(
                weights_of(scores[b], used), with_ones(value), preferred_element_type=jnp.float32
            )
        if closes:
            out_ref[:, lanes(i)] = (total[:, :HD] * inverse(total[:, HD:])).astype(out_ref.dtype)
        else:
            out_ref[i, :, : 2 * HD] = total
            out_ref[i, :, 2 * HD :] = top


def pack_kernel(cut, k_ref, v_ref, out_ref, sems):
    wide = out_ref.shape[1] // 2
    copies = [
        pltpu.make_async_copy(
            ref.at[:, pl.ds(cut, wide)], out_ref.at[:, pl.ds(i * wide, wide)], sems.at[i]
        )
        for i, ref in enumerate((k_ref, v_ref))
    ]
    for copy in copies:
        copy.start()
    for copy in copies:
        copy.wait()


def columns_kernel(which_ref, w_ref, *refs):
    *outs, sems = refs
    copies = []
    for i, out in enumerate(outs):
        cols = out.shape[1]
        at = pl.ds(pl.multiple_of(which_ref[i] * cols, cols), cols)
        copies.append(pltpu.make_async_copy(w_ref.at[:, at], out, sems.at[i]))
    for copy in copies:
        copy.start()
    for copy in copies:
        copy.wait()


def project_kernel(att0_ref, att1_ref, *refs):
    half = len(refs) // 2
    weights, outs = (refs[:1], refs[1:]) if len(refs) == 3 else (refs[:half], refs[half:])
    cut = att0_ref.shape[1]
    each = len(outs) // len(weights)
    for i, w_ref in enumerate(weights):
        for j in range(each):
            out_ref = outs[i * each + j]
            rows = out_ref.shape[0]
            at = slice(j * rows, (j + 1) * rows)
            out_ref[...] = (
                jnp.dot(att0_ref[at, :], w_ref[:cut, :], preferred_element_type=jnp.float32)
                + jnp.dot(att1_ref[at, :], w_ref[cut:, :], preferred_element_type=jnp.float32)
            ).astype(out_ref.dtype)


def last_sum_kernel(*refs):
    *parts, out_ref = refs
    out_ref[...] = sum(ref[...].astype(jnp.float32) for ref in parts).astype(out_ref.dtype)


def in_vmem(count):
    return [pl.BlockSpec(memory_space=pltpu.VMEM)] * count


def near_part(q, k, v, pk, pv):
    rows, width = q.shape
    heads = width // HD
    return pl.pallas_call(
        near_kernel,
        out_shape=jax.ShapeDtypeStruct((heads, rows, 3 * HD), jnp.float32),
        in_specs=in_vmem(5),
        out_specs=in_vmem(1)[0],
        compiler_params=pltpu.CompilerParams(vmem_limit_bytes=8 * 2**20),
        cost_estimate=pl.CostEstimate(
            flops=WEIGHT * 12 * heads * rows * rows * HD,
            bytes_accessed=10 * rows * width,
            transcendentals=2 * heads * rows * rows,
        ),
        name="near",
    )(q, k, v, pk, pv)


def far_part(first, closes, valid, q, state, blocks):
    rows = q.shape[0]
    arrays = [array for block in blocks for array in block]
    heads = arrays[0].shape[1] // 2 // HD
    if closes:
        shape = jax.ShapeDtypeStruct((rows, heads * HD), jnp.bfloat16)
    else:
        shape = jax.ShapeDtypeStruct((heads, rows, 3 * HD), jnp.float32)
    return pl.pallas_call(
        functools.partial(far_kernel, first, [len(block) for block in blocks], closes),
        out_shape=shape,
        in_specs=[pl.BlockSpec(memory_space=pltpu.SMEM)] + in_vmem(2 + len(arrays)),
        out_specs=in_vmem(1)[0],
        compiler_params=pltpu.CompilerParams(vmem_limit_bytes=8 * 2**20),
        cost_estimate=pl.CostEstimate(
            flops=6 * len(blocks) * heads * rows * rows * HD,
            bytes_accessed=10 * rows * heads * HD,
            transcendentals=len(blocks) * heads * rows * rows,
        ),
        name=f"far{first}_{len(blocks)}",
    )(valid, q, state, *arrays)


def packed(k, v, cut, heads):
    rows = k.shape[0]
    return pl.pallas_call(
        functools.partial(pack_kernel, cut * HD),
        out_shape=jax.ShapeDtypeStruct((rows, 2 * heads * HD), k.dtype),
        in_specs=[pl.BlockSpec(memory_space=pl.ANY)] * 2,
        out_specs=pl.BlockSpec(memory_space=pltpu.VMEM),
        scratch_shapes=[pltpu.SemaphoreType.DMA((2,))],
        compiler_params=pltpu.CompilerParams(vmem_limit_bytes=60 * 2**20),
        cost_estimate=pl.CostEstimate(
            flops=0, bytes_accessed=8 * rows * heads * HD, transcendentals=0
        ),
        name=f"pack{cut}",
    )(k, v)


def seq_pairs(step_of, among=lambda s: True):
    return [
        (s, s + step_of(s)) for s in range(SPANS) if 0 <= s + step_of(s) < SPANS and among(s)
    ]


def mate_step(s):
    return 2 if s // 2 % 2 == 0 else -2


def other_step(s):
    return -mate_step(s)


def is_end(s):
    return s % ROW < 2 or s % ROW >= ROW - 2


MATE = seq_pairs(mate_step)
OTHER = seq_pairs(other_step)
OTHER_IN_ROW = seq_pairs(other_step, lambda s: not is_end(s))
ONWARD = [
    (s + mate_step(s), s + other_step(s))
    for s in range(SPANS)
    if is_end(s) and 0 <= s + other_step(s) < SPANS
]
PAIR = seq_pairs(lambda s: 1 if s % 2 == 0 else -1)
MATE_SHARED = [(s, p) for s, p in PAIR if s % 2 == s // 2 % 2]
OTHER_SHARED = [(s, p) for s, p in PAIR if s % 2 != s // 2 % 2]


def body(queries, key_states, value_states, out_weight):
    place = lax.axis_index("seq")
    chip = place // 2
    mate_chip = chip ^ 1
    other_chip = 2 * chip - mate_chip
    third = jnp.where(place % 2 == 0, chip - 1, chip + 1)

    def inside(c):
        return (c >= 0) & (c < SPANS // 2)

    valid = jnp.stack([inside(mate_chip), inside(other_chip), inside(third)]).astype(jnp.int32)
    total_heads = key_states.shape[1] // HD

    pair_key = lax.ppermute(key_states, "seq", PAIR)
    pair_value = lax.ppermute(value_states, "seq", PAIR)
    direct = packed(key_states, value_states, 0, DIRECT)
    other0 = lax.ppermute(direct, "seq", OTHER)
    direct, keys, values = lax.optimization_barrier((direct, key_states, value_states))
    relayed = packed(keys, values, DIRECT, total_heads - DIRECT)
    mate1 = lax.ppermute(relayed, "seq", MATE)
    mate0 = lax.ppermute(direct, "seq", MATE)
    relayed, pair_key, pair_value = lax.optimization_barrier((relayed, pair_key, pair_value))
    row_other1 = lax.ppermute(relayed, "seq", OTHER_IN_ROW)

    z = lax.axis_index("head")
    weights = weight_columns(
        jnp.stack([z ^ 3, z ^ 1, z ^ 2, z]), out_weight
    )
    queries, mate1, *weights = lax.optimization_barrier((queries, mate1, *weights))
    passed_other1 = lax.ppermute(mate1, "seq", ONWARD)
    state = near_part(queries, key_states, value_states, pair_key, pair_value)
    other1 = row_other1 + passed_other1

    mate_shared0 = lax.ppermute(mate0, "seq", MATE_SHARED)
    mate_shared1 = lax.ppermute(mate1, "seq", MATE_SHARED)
    other_shared1 = lax.ppermute(other1, "seq", OTHER_SHARED)

    mate1, mate_shared1 = lax.optimization_barrier((mate1, mate_shared1))
    state1 = far_part(DIRECT, False, valid[:1], queries, state, [[mate1]])
    mate0, mate_shared0, state1 = lax.optimization_barrier((mate0, mate_shared0, state1))
    state0 = far_part(0, False, valid[:1], queries, state, [[mate0]])
    other0, state0, state1 = lax.optimization_barrier((other0, state0, state1))
    other_shared0 = lax.ppermute(other0, "seq", OTHER_SHARED)
    att1 = far_part(
        DIRECT, True, valid[1:], queries, state1, [[other1], [mate_shared1, other_shared1]]
    )
    state0 = far_part(0, False, valid[1:2], queries, state0, [[other0]])
    att0 = far_part(0, True, valid[2:], queries, state0, [[mate_shared0, other_shared0]])
    return projected(att0, att1, weights)


def small_call(kernel, name, out_shape, operands, scalars=(), in_hbm=(), sems=0, limit=8 * 2**20):
    return pl.pallas_call(
        kernel,
        out_shape=out_shape,
        in_specs=[pl.BlockSpec(memory_space=pltpu.SMEM)] * len(scalars)
        + [pl.BlockSpec(memory_space=pltpu.HBM)] * len(in_hbm)
        + in_vmem(len(operands)),
        out_specs=in_vmem(len(out_shape)),
        scratch_shapes=[pltpu.SemaphoreType.DMA((sems,))] if sems else [],
        compiler_params=pltpu.CompilerParams(vmem_limit_bytes=limit),
        cost_estimate=pl.CostEstimate(
            flops=0,
            bytes_accessed=2 * sum(o.size * o.dtype.itemsize for o in out_shape),
            transcendentals=0,
        ),
        name=name,
    )(*[x.astype(jnp.int32) for x in scalars], *in_hbm, *operands)


def weight_columns(which, out_weight):
    depth = out_weight.shape[0]
    cols = out_weight.shape[1] // HEAD_PEERS
    return small_call(
        columns_kernel,
        "columns",
        [jax.ShapeDtypeStruct((depth, cols), out_weight.dtype)] * HEAD_PEERS,
        (),
        scalars=(which,),
        in_hbm=(out_weight,),
        sems=HEAD_PEERS,
        limit=48 * 2**20,
    )


def projection(att0, att1, weights, pieces):
    rows = att0.shape[0]
    depth, cols = weights[0].shape
    count = len(weights)
    return pl.pallas_call(
        project_kernel,
        out_shape=[jax.ShapeDtypeStruct((rows // pieces, cols), jnp.bfloat16)] * (count * pieces),
        in_specs=in_vmem(2 + count),
        out_specs=in_vmem(count * pieces),
        compiler_params=pltpu.CompilerParams(vmem_limit_bytes=8 * 2**20),
        cost_estimate=pl.CostEstimate(
            flops=2 * count * rows * depth * cols,
            bytes_accessed=2 * count * depth * cols,
            transcendentals=0,
        ),
        name=f"project{count}",
    )(att0, att1, *weights)


def projected(att0, att1, weights):
    def sent(value, apart):
        return lax.ppermute(value, "head", [(i, i ^ apart) for i in range(HEAD_PEERS)])

    (distant,) = projection(att0, att1, weights[:1], 1)
    distant_in = sent(distant, 1)
    beside, across, own = projection(att0, att1, weights[1:], 1)
    beside_in = sent(beside, 1)
    across = (across.astype(jnp.float32) + distant_in.astype(jnp.float32)).astype(jnp.bfloat16)
    across_in = sent(across, 2)
    return small_call(
        last_sum_kernel,
        "last_sum",
        [jax.ShapeDtypeStruct(own.shape, own.dtype)],
        (own, beside_in, across_in),
    )[0]


def solution(mesh):
    placed = (P("seq", "head"), P("seq", "head"), P("seq", "head"), P("head", None))
    return jax.shard_map(
        body, mesh=mesh, in_specs=placed, out_specs=P("seq", "head"), check_vma=False
    )
```

time: 149 us -> 117 us (0.79)
  the two profiles are of different devices: /device:TPU:30 before, /device:TPU:24 now
where the time goes in v2:
time: 117 us; the launch traced here: 116 us
  waiting for transfers between devices  58.2 us (50%)
  starting transfers between devices  32 us (27%)
  Pallas kernels  24.4 us (21%)
    ppermute x3, waiting for transfers between devices, sent(): lax.ppermute(value, 'head', [(i, i ^ apart) for i in range(HEAD_PEERS)])  39 us
    ppermute x1, starting transfers between devices, body(): other0 = lax.ppermute(direct, 'seq', OTHER)  11.5 us
    ppermute x1, waiting for transfers between devices, body(): other0 = lax.ppermute(direct, 'seq', OTHER)  11 us
    ppermute x3, starting transfers between devices, sent(): lax.ppermute(value, 'head', [(i, i ^ apart) for i in range(HEAD_PEERS)])  10.5 us
    pallas_call x5, Pallas kernels, far_part(): pl.pallas_call(functools.partial(far_kernel, first, [len(block) for block...  9.68 us
    ppermute x1, waiting for transfers between devices, body(): mate1 = lax.ppermute(relayed, 'seq', MATE)  8.16 us
    pallas_call x1, Pallas kernels, near_part(): pl.pallas_call(near_kernel, out_shape=jax.ShapeDtypeStruct((heads, rows,...  4.63 us
    pallas_call x2, Pallas kernels, small_call(): pl.pallas_call(kernel, out_shape=out_shape, in_specs=[pl.BlockSpec(memory...  4.05 us
  transfers between devices with their start and end apart: 14, of which 5 were waited for; matrix products, arithmetic and copies ran while one was open for 1% of the time, Pallas kernels for 16%

profile of v2, /device:TPU:24, one launch (start us, length us, event | category | flops | bytes accessed | tf_op | source)
XLA Modules:
  0.0 116.1 jit_solution(16323077638272373914)
XLA Ops:
  0.0 2.1 %pack0.1 = bf16[384,1024]{1,0:T(8,128)(2,1)} custom-call(bf16[384,768]{1,0:T(8,128)(2,1)} %k_ref.4, bf16[384,768]{1,0:T(8,128)(2,1)} %v_ref.4), custom_call_target="tpu_custom_call" | custom-call | bytes 1572864 | tf_op jit(solution)/shard_map/pack0/pallas_call | solution.py:202
  2.1 1.6 %collective-permute-start.4 = (bf16[384,1024]{1,0:T(8,128)(2,1)}, bf16[384,1024]{1,0:T(8,128)(2,1)S(1)}, u32[]{:S(2)}, u32[]{:S(2)}) collective-permute-start(bf16[384,1024]{1,0:T(8,128)(2,1)} %pack0.1), channel_id=1, source_target_pairs={{0,8},{4,12},{8,0},{12,4},{16,24},{20,28},{24,16},{28,20},{32,40},... | collective-permute-start | bytes 2359304 | tf_op jit(solution)/shard_map/ppermute | solution.py:267
  4.2 1.8 %pack4.1 = bf16[384,512]{1,0:T(8,128)(2,1)} custom-call(bf16[384,768]{1,0:T(8,128)(2,1)} %k_ref.4, bf16[384,768]{1,0:T(8,128)(2,1)} %v_ref.4), custom_call_target="tpu_custom_call" | custom-call | bytes 786432 | tf_op jit(solution)/shard_map/pack4/pallas_call | solution.py:202
  6.6 11.5 %collective-permute-start.1 = (bf16[384,1024]{1,0:T(8,128)(2,1)}, bf16[384,1024]{1,0:T(8,128)(2,1)S(1)}, u32[]{:S(2)}, u32[]{:S(2)}) collective-permute-start(bf16[384,1024]{1,0:T(8,128)(2,1)} %pack0.1), channel_id=1, source_target_pairs={{8,16},{12,20},{16,8},{20,12},{24,32},{28,36},{32,24},{36,28},{40,... | collective-permute-start | bytes 2359304 | tf_op jit(solution)/shard_map/ppermute | solution.py:263
  18.2 3.0 %columns.1 = (bf16[768,768]{1,0:T(8,128)(2,1)S(1)}, bf16[768,768]{1,0:T(8,128)(2,1)S(1)}, bf16[768,768]{1,0:T(8,128)(2,1)S(1)}, bf16[768,768]{1,0:T(8,128)(2,1)S(1)}) custom-call(s32[4]{0:T(128)S(1)} %pad_add_fusion.which_ref, bf16[768,3072]{1,0:T(8,128)(2,1)} %w_ref.1), custom_call_target="tpu_custom_call" | custom-call | bytes 9437184 | tf_op jit(solution)/shard_map/columns/pallas_call | solution.py:299
  22.0 8.2 %collective-permute-done.refs_0_ = bf16[384,512]{1,0:T(8,128)(2,1)S(1)} collective-permute-done((bf16[384,512]{1,0:T(8,128)(2,1)}, bf16[384,512]{1,0:T(8,128)(2,1)S(1)}, u32[]{:S(2)}, u32[]{:S(2)}) %collective-permute-start) | collective-permute-done | bytes 393248 | tf_op jit(solution)/shard_map/ppermute | solution.py:266
  30.1 1.3 %collective-permute-start.9 = (bf16[384,512]{1,0:T(8,128)(2,1)S(1)}, bf16[384,512]{1,0:T(8,128)(2,1)S(1)}, u32[]{:S(2)}, u32[]{:S(2)}) collective-permute-start(bf16[384,512]{1,0:T(8,128)(2,1)S(1)} %collective-permute-done.refs_0_), channel_id=1, source_target_pairs={{16,32},{20,36},{40,24},{44,28},{48,64},{52,68},{72,56},{76,60},{8... | collective-permute-start | bytes 1179656 | tf_op jit(solution)/shard_map/ppermute | solution.py:276
  31.4 1.3 %collective-permute-start.6 = (bf16[384,512]{1,0:T(8,128)(2,1)S(1)}, bf16[384,512]{1,0:T(8,128)(2,1)S(1)}, u32[]{:S(2)}, u32[]{:S(2)}) collective-permute-start(bf16[384,512]{1,0:T(8,128)(2,1)S(1)} %collective-permute-done.refs_0_), channel_id=1, source_target_pairs={{0,4},{12,8},{16,20},{28,24},{32,36},{44,40},{48,52},{60,56},{64,6... | collective-permute-start | bytes 1179656 | tf_op jit(solution)/shard_map/ppermute | solution.py:281
  33.5 1.3 %collective-permute-start.5 = (bf16[384,1024]{1,0:T(8,128)(2,1)S(1)}, bf16[384,1024]{1,0:T(8,128)(2,1)S(1)}, u32[]{:S(2)}, u32[]{:S(2)}) collective-permute-start(bf16[384,1024]{1,0:T(8,128)(2,1)S(1)} %collective-permute-done.4.refs_0_), channel_id=1, source_target_pairs={{0,4},{12,8},{16,20},{28,24},{32,36},{44,40},{48,52},{60,56},{64,6... | collective-permute-start | bytes 2359304 | tf_op jit(solution)/shard_map/ppermute | solution.py:280
  34.9 4.6 %near.1.state_ref = f32[6,384,384]{2,1,0:T(8,128)S(1)} custom-call(bf16[384,768]{1,0:T(8,128)(2,1)S(1)} %copy-done, bf16[384,768]{1,0:T(8,128)(2,1)S(1)} %copy-done.2, bf16[384,768]{1,0:T(8,128)(2,1)S(1)} %copy-done.4, bf16[384,768]{1,0:T(8,128)(2,1)} %collective-permute-done.2.pk_ref, bf16[384,768]{1,0:T(8,128)(2,1)} %collective-permute-done.3.pv_ref), custom_call_target="tpu_custom_call" | custom-call | flops 40768634880 | bytes 2949120 | tf_op jit(solution)/shard_map/near/pallas_call | solution.py:162
  39.5 1.4 %far4_1.1.state_ref = f32[2,384,384]{2,1,0:T(8,128)S(1)} custom-call(s32[1]{0:T(128)} %get-tuple-element.59.valid_ref, bf16[384,768]{1,0:T(8,128)(2,1)S(1)} %copy-done, f32[6,384,384]{2,1,0:T(8,128)S(1)} %near.1.state_ref, bf16[384,512]{1,0:T(8,128)(2,1)S(1)} %collective-permute-done.refs_0_), custom_call_target="tpu_custom_call" | custom-call | flops 226492416 | bytes 983040 | tf_op jit(solution)/shard_map/far4_1/pallas_call | solution.py:185
  41.0 2.1 %far0_1.3.state_ref = f32[4,384,384]{2,1,0:T(8,128)S(1)} custom-call(s32[1]{0:T(128)} %get-tuple-element.59.valid_ref, bf16[384,768]{1,0:T(8,128)(2,1)S(1)} %copy-done, f32[6,384,384]{2,1,0:T(8,128)S(1)} %near.1.state_ref, bf16[384,1024]{1,0:T(8,128)(2,1)S(1)} %collective-permute-done.4.refs_0_), custom_call_target="tpu_custom_call" | custom-call | flops 452984832 | bytes 1966080 | tf_op jit(solution)/shard_map/far0_1/pallas_call | solution.py:185
  43.0 11.0 %collective-permute-done.1.refs_0_ = bf16[384,1024]{1,0:T(8,128)(2,1)S(1)} collective-permute-done((bf16[384,1024]{1,0:T(8,128)(2,1)}, bf16[384,1024]{1,0:T(8,128)(2,1)S(1)}, u32[]{:S(2)}, u32[]{:S(2)}) %collective-permute-start.1) | collective-permute-done | bytes 786464 | tf_op jit(solution)/shard_map/ppermute | solution.py:263
  54.1 1.3 %collective-permute-start.7 = (bf16[384,1024]{1,0:T(8,128)(2,1)S(1)}, bf16[384,1024]{1,0:T(8,128)(2,1)S(1)}, u32[]{:S(2)}, u32[]{:S(2)}) collective-permute-start(bf16[384,1024]{1,0:T(8,128)(2,1)S(1)} %collective-permute-done.1.refs_0_), channel_id=1, source_target_pairs={{4,0},{8,12},{20,16},{24,28},{36,32},{40,44},{52,48},{56,60},{68,6... | collective-permute-start | bytes 2359304 | tf_op jit(solution)/shard_map/ppermute | solution.py:289
  55.5 1.5 %collective-permute-start.10 = (bf16[384,512]{1,0:T(8,128)(2,1)S(1)}, bf16[384,512]{1,0:T(8,128)(2,1)S(1)}, u32[]{:S(2)}, u32[]{:S(2)}) collective-permute-start(bf16[384,512]{1,0:T(8,128)(2,1)S(1)} %add.17.refs_0_), channel_id=1, source_target_pairs={{4,0},{8,12},{20,16},{24,28},{36,32},{40,44},{52,48},{56,60},{68,6... | collective-permute-start | bytes 1179656 | tf_op jit(solution)/shard_map/ppermute | solution.py:282
  57.1 2.1 %far0_1.4.state_ref = f32[4,384,384]{2,1,0:T(8,128)S(1)} custom-call(s32[1]{0:T(128)} %get-tuple-element.60.valid_ref, bf16[384,768]{1,0:T(8,128)(2,1)S(1)} %copy-done, f32[4,384,384]{2,1,0:T(8,128)S(1)} %far0_1.3.state_ref, bf16[384,1024]{1,0:T(8,128)(2,1)S(1)} %collective-permute-done.1.refs_0_), custom_call_target="tpu_custom_call" | custom-call | flops 452984832 | bytes 1966080 | tf_op jit(solution)/shard_map/far0_1/pallas_call | solution.py:185
  59.2 2.0 %far4_2.1.att1_ref = bf16[384,256]{1,0:T(8,128)(2,1)S(1)} custom-call(s32[2]{0:T(128)S(1)} %slice.16.valid_ref, bf16[384,768]{1,0:T(8,128)(2,1)S(1)} %copy-done, f32[2,384,384]{2,1,0:T(8,128)S(1)} %far4_1.1.state_ref, bf16[384,512]{1,0:T(8,128)(2,1)S(1)} %add.17.refs_0_, bf16[384,512]{1,0:T(8,128)(2,1)S(1)} %collective-permute-done.6.refs_1_, ...), custom_call_target="tpu_custom_call" | custom-call | flops 452984832 | bytes 983040 | tf_op jit(solution)/shard_map/far4_2/pallas_call | solution.py:185
  61.2 2.1 %far0_1.5.att0_ref = bf16[384,512]{1,0:T(8,128)(2,1)S(1)} custom-call(s32[1]{0:T(128)} %get-tuple-element.61.valid_ref, bf16[384,768]{1,0:T(8,128)(2,1)S(1)} %copy-done, f32[4,384,384]{2,1,0:T(8,128)S(1)} %far0_1.4.state_ref, bf16[384,1024]{1,0:T(8,128)(2,1)S(1)} %collective-permute-done.5.refs_0_, bf16[384,1024]{1,0:T(8,128)(2,1)S(1)} %collective-permute-done.7.refs_1_), custom_call_target="tpu_custom_call" | custom-call | flops 452984832 | bytes 1966080 | tf_op jit(solution)/shard_map/far0_1/pallas_call | solution.py:185
  64.8 1.5 %project3.1 = (bf16[384,768]{1,0:T(8,128)(2,1)S(1)}, bf16[384,768]{1,0:T(8,128)(2,1)S(1)}, bf16[384,768]{1,0:T(8,128)(2,1)S(1)}) custom-call(bf16[384,512]{1,0:T(8,128)(2,1)S(1)} %far0_1.5.att0_ref, bf16[384,256]{1,0:T(8,128)(2,1)S(1)} %far4_2.1.att1_ref, bf16[768,768]{1,0:T(8,128)(2,1)S(1)} %get-tuple-element.52.refs_0_, ...), custom_call_target="tpu_custom_call" | custom-call | flops 1358954496 | bytes 3538944 | tf_op jit(solution)/shard_map/project3/pallas_call | solution.py:336
  66.4 1.3 %collective-permute-start.11 = (bf16[384,768]{1,0:T(8,128)(2,1)S(1)}, bf16[384,768]{1,0:T(8,128)(2,1)S(1)}, u32[]{:S(2)}, u32[]{:S(2)}) collective-permute-start(bf16[384,768]{1,0:T(8,128)(2,1)S(1)} %get-tuple-element.56), channel_id=1, source_target_pairs={{0,1},{1,0},{2,3},{3,2},{4,5},{5,4},{6,7},{7,6},{8,9},{9,8},{10,11... | collective-permute-start | bytes 1769480 | tf_op jit(solution)/shard_map/ppermute | solution.py:353
  67.7 12.3 %collective-permute-done.12 = bf16[384,768]{1,0:T(8,128)(2,1)S(1)} collective-permute-done((bf16[384,768]{1,0:T(8,128)(2,1)S(1)}, bf16[384,768]{1,0:T(8,128)(2,1)S(1)}, u32[]{:S(2)}, u32[]{:S(2)}) %collective-permute-start.12) | collective-permute-done | bytes 589856 | tf_op jit(solution)/shard_map/ppermute | solution.py:353
  80.1 8.3 %collective-permute-start.13 = (bf16[384,768]{1,0:T(8,128)(2,1)S(1)}, bf16[384,768]{1,0:T(8,128)(2,1)S(1)}, u32[]{:S(2)}, u32[]{:S(2)}) collective-permute-start(bf16[384,768]{1,0:T(8,128)(2,1)S(1)} %add_convert_fusion), channel_id=1, source_target_pairs={{0,2},{1,3},{2,0},{3,1},{4,6},{5,7},{6,4},{7,5},{8,10},{9,11},{10,... | collective-permute-start | bytes 1769480 | tf_op jit(solution)/shard_map/ppermute | solution.py:353
  88.4 14.9 %collective-permute-done.11.refs_1_ = bf16[384,768]{1,0:T(8,128)(2,1)S(1)} collective-permute-done((bf16[384,768]{1,0:T(8,128)(2,1)S(1)}, bf16[384,768]{1,0:T(8,128)(2,1)S(1)}, u32[]{:S(2)}, u32[]{:S(2)}) %collective-permute-start.11) | collective-permute-done | bytes 589856 | tf_op jit(solution)/shard_map/ppermute | solution.py:353
  103.4 11.7 %collective-permute-done.13.refs_2_ = bf16[384,768]{1,0:T(8,128)(2,1)S(1)} collective-permute-done((bf16[384,768]{1,0:T(8,128)(2,1)S(1)}, bf16[384,768]{1,0:T(8,128)(2,1)S(1)}, u32[]{:S(2)}, u32[]{:S(2)}) %collective-permute-start.13) | collective-permute-done | bytes 589856 | tf_op jit(solution)/shard_map/ppermute | solution.py:353
  (34 shorter events, 5.5 us)
Async XLA Ops:
  0.0 3.7 %copy-start.3 = (bf16[384,768]{1,0:T(8,128)(2,1)S(1)}, bf16[384,768]{1,0:T(8,128)(2,1)}, u32[]{:S(2)}) copy-start(bf16[384,768]{1,0:T(8,128)(2,1)} %v_ref.4) | copy-start | bytes 1769476
  0.0 3.7 %copy-start.1 = (bf16[384,768]{1,0:T(8,128)(2,1)S(1)}, bf16[384,768]{1,0:T(8,128)(2,1)}, u32[]{:S(2)}) copy-start(bf16[384,768]{1,0:T(8,128)(2,1)} %k_ref.4) | copy-start | bytes 1769476
  2.1 31.3 %collective-permute-start.4 = (bf16[384,1024]{1,0:T(8,128)(2,1)}, bf16[384,1024]{1,0:T(8,128)(2,1)S(1)}, u32[]{:S(2)}, u32[]{:S(2)}) collective-permute-start(bf16[384,1024]{1,0:T(8,128)(2,1)} %pack0.1), channel_id=1, source_target_pairs={{0,8},{4,12},{8,0},{12,4},{16,24},{20,28},{24,16},{28,20},{32,40},... | collective-permute-start | bytes 2359304 | tf_op jit(solution)/shard_map/ppermute | solution.py:267
  3.7 27.7 %collective-permute-start.2 = (bf16[384,768]{1,0:T(8,128)(2,1)S(1)}, bf16[384,768]{1,0:T(8,128)(2,1)}, u32[]{:S(2)}, u32[]{:S(2)}) collective-permute-start(bf16[384,768]{1,0:T(8,128)(2,1)S(1)} %copy-done.1), channel_id=1, source_target_pairs={{0,4},{4,0},{8,12},{12,8},{16,20},{20,16},{24,28},{28,24},{32,36},... | collective-permute-start | bytes 1769480 | tf_op jit(solution)/shard_map/ppermute | solution.py:260
  3.7 29.0 %collective-permute-start.3 = (bf16[384,768]{1,0:T(8,128)(2,1)S(1)}, bf16[384,768]{1,0:T(8,128)(2,1)}, u32[]{:S(2)}, u32[]{:S(2)}) collective-permute-start(bf16[384,768]{1,0:T(8,128)(2,1)S(1)} %copy-done.3), channel_id=1, source_target_pairs={{0,4},{4,0},{8,12},{12,8},{16,20},{20,16},{24,28},{28,24},{32,36},... | collective-permute-start | bytes 1769480 | tf_op jit(solution)/shard_map/ppermute | solution.py:261
  6.0 24.1 %collective-permute-start = (bf16[384,512]{1,0:T(8,128)(2,1)}, bf16[384,512]{1,0:T(8,128)(2,1)S(1)}, u32[]{:S(2)}, u32[]{:S(2)}) collective-permute-start(bf16[384,512]{1,0:T(8,128)(2,1)} %pack4.1), channel_id=1, source_target_pairs={{0,8},{4,12},{8,0},{12,4},{16,24},{20,28},{24,16},{28,20},{32,40},... | collective-permute-start | bytes 1179656 | tf_op jit(solution)/shard_map/ppermute | solution.py:266
  6.6 47.5 %collective-permute-start.1 = (bf16[384,1024]{1,0:T(8,128)(2,1)}, bf16[384,1024]{1,0:T(8,128)(2,1)S(1)}, u32[]{:S(2)}, u32[]{:S(2)}) collective-permute-start(bf16[384,1024]{1,0:T(8,128)(2,1)} %pack0.1), channel_id=1, source_target_pairs={{8,16},{12,20},{16,8},{20,12},{24,32},{28,36},{32,24},{36,28},{40,... | collective-permute-start | bytes 2359304 | tf_op jit(solution)/shard_map/ppermute | solution.py:263
  18.2 14.5 %copy-start.5 = (bf16[384,512]{1,0:T(8,128)(2,1)S(1)}, bf16[384,512]{1,0:T(8,128)(2,1)}, u32[]{:S(2)}) copy-start(bf16[384,512]{1,0:T(8,128)(2,1)} %pack4.1) | copy-start | bytes 1179652
  18.2 16.6 %copy-start = (bf16[384,768]{1,0:T(8,128)(2,1)S(1)}, bf16[384,768]{1,0:T(8,128)(2,1)}, u32[]{:S(2)}) copy-start(bf16[384,768]{1,0:T(8,128)(2,1)} %q_ref.5) | copy-start | bytes 1769476
  18.2 16.6 %copy-start.2 = (bf16[384,768]{1,0:T(8,128)(2,1)S(1)}, bf16[384,768]{1,0:T(8,128)(2,1)}, u32[]{:S(2)}) copy-start(bf16[384,768]{1,0:T(8,128)(2,1)} %k_ref.4) | copy-start | bytes 1769476
  18.2 16.6 %copy-start.4 = (bf16[384,768]{1,0:T(8,128)(2,1)S(1)}, bf16[384,768]{1,0:T(8,128)(2,1)}, u32[]{:S(2)}) copy-start(bf16[384,768]{1,0:T(8,128)(2,1)} %v_ref.4) | copy-start | bytes 1769476
  30.1 25.2 %collective-permute-start.9 = (bf16[384,512]{1,0:T(8,128)(2,1)S(1)}, bf16[384,512]{1,0:T(8,128)(2,1)S(1)}, u32[]{:S(2)}, u32[]{:S(2)}) collective-permute-start(bf16[384,512]{1,0:T(8,128)(2,1)S(1)} %collective-permute-done.refs_0_), channel_id=1, source_target_pairs={{16,32},{20,36},{40,24},{44,28},{48,64},{52,68},{72,56},{76,60},{8... | collective-permute-start | bytes 1179656 | tf_op jit(solution)/shard_map/ppermute | solution.py:276
  31.4 8.1 %collective-permute-start.6 = (bf16[384,512]{1,0:T(8,128)(2,1)S(1)}, bf16[384,512]{1,0:T(8,128)(2,1)S(1)}, u32[]{:S(2)}, u32[]{:S(2)}) collective-permute-start(bf16[384,512]{1,0:T(8,128)(2,1)S(1)} %collective-permute-done.refs_0_), channel_id=1, source_target_pairs={{0,4},{12,8},{16,20},{28,24},{32,36},{44,40},{48,52},{60,56},{64,6... | collective-permute-start | bytes 1179656 | tf_op jit(solution)/shard_map/ppermute | solution.py:281
  32.8 22.6 %collective-permute-start.8 = (bf16[384,512]{1,0:T(8,128)(2,1)S(1)}, bf16[384,512]{1,0:T(8,128)(2,1)S(1)}, u32[]{:S(2)}, u32[]{:S(2)}) collective-permute-start(bf16[384,512]{1,0:T(8,128)(2,1)S(1)} %copy-done.5), channel_id=1, source_target_pairs={{8,16},{12,20},{16,8},{20,12},{40,48},{44,52},{48,40},{52,44},{72,... | collective-permute-start | bytes 1179656 | tf_op jit(solution)/shard_map/ppermute | solution.py:269
  33.5 7.5 %collective-permute-start.5 = (bf16[384,1024]{1,0:T(8,128)(2,1)S(1)}, bf16[384,1024]{1,0:T(8,128)(2,1)S(1)}, u32[]{:S(2)}, u32[]{:S(2)}) collective-permute-start(bf16[384,1024]{1,0:T(8,128)(2,1)S(1)} %collective-permute-done.4.refs_0_), channel_id=1, source_target_pairs={{0,4},{12,8},{16,20},{28,24},{32,36},{44,40},{48,52},{60,56},{64,6... | collective-permute-start | bytes 2359304 | tf_op jit(solution)/shard_map/ppermute | solution.py:280
  54.1 7.1 %collective-permute-start.7 = (bf16[384,1024]{1,0:T(8,128)(2,1)S(1)}, bf16[384,1024]{1,0:T(8,128)(2,1)S(1)}, u32[]{:S(2)}, u32[]{:S(2)}) collective-permute-start(bf16[384,1024]{1,0:T(8,128)(2,1)S(1)} %collective-permute-done.1.refs_0_), channel_id=1, source_target_pairs={{4,0},{8,12},{20,16},{24,28},{36,32},{40,44},{52,48},{56,60},{68,6... | collective-permute-start | bytes 2359304 | tf_op jit(solution)/shard_map/ppermute | solution.py:289
  55.5 3.7 %collective-permute-start.10 = (bf16[384,512]{1,0:T(8,128)(2,1)S(1)}, bf16[384,512]{1,0:T(8,128)(2,1)S(1)}, u32[]{:S(2)}, u32[]{:S(2)}) collective-permute-start(bf16[384,512]{1,0:T(8,128)(2,1)S(1)} %add.17.refs_0_), channel_id=1, source_target_pairs={{4,0},{8,12},{20,16},{24,28},{36,32},{40,44},{52,48},{56,60},{68,6... | collective-permute-start | bytes 1179656 | tf_op jit(solution)/shard_map/ppermute | solution.py:282
  63.9 16.1 %collective-permute-start.12 = (bf16[384,768]{1,0:T(8,128)(2,1)S(1)}, bf16[384,768]{1,0:T(8,128)(2,1)S(1)}, u32[]{:S(2)}, u32[]{:S(2)}) collective-permute-start(bf16[384,768]{1,0:T(8,128)(2,1)S(1)} %project1.1), channel_id=1, source_target_pairs={{0,1},{1,0},{2,3},{3,2},{4,5},{5,4},{6,7},{7,6},{8,9},{9,8},{10,11... | collective-permute-start | bytes 1769480 | tf_op jit(solution)/shard_map/ppermute | solution.py:353
  66.4 37.0 %collective-permute-start.11 = (bf16[384,768]{1,0:T(8,128)(2,1)S(1)}, bf16[384,768]{1,0:T(8,128)(2,1)S(1)}, u32[]{:S(2)}, u32[]{:S(2)}) collective-permute-start(bf16[384,768]{1,0:T(8,128)(2,1)S(1)} %get-tuple-element.56), channel_id=1, source_target_pairs={{0,1},{1,0},{2,3},{3,2},{4,5},{5,4},{6,7},{7,6},{8,9},{9,8},{10,11... | collective-permute-start | bytes 1769480 | tf_op jit(solution)/shard_map/ppermute | solution.py:353
  80.1 35.0 %collective-permute-start.13 = (bf16[384,768]{1,0:T(8,128)(2,1)S(1)}, bf16[384,768]{1,0:T(8,128)(2,1)S(1)}, u32[]{:S(2)}, u32[]{:S(2)}) collective-permute-start(bf16[384,768]{1,0:T(8,128)(2,1)S(1)} %add_convert_fusion), channel_id=1, source_target_pairs={{0,2},{1,3},{2,0},{3,1},{4,6},{5,7},{6,4},{7,5},{8,10},{9,11},{10,... | collective-permute-start | bytes 1769480 | tf_op jit(solution)/shard_map/ppermute | solution.py:353

commit v3 on v2

--- a/solution.py
+++ b/solution.py
@@ -12,8 +12,9 @@
 SPANS = 64
 HEAD_PEERS = 4
 ROW = 8
-DIRECT = 4
+KEYS, VALUES = 4, 3
 WEIGHT = 30
+LIGHT = pl.CostEstimate(flops=1, bytes_accessed=1, transcendentals=0)
 SCALE = math.log2(math.e) / math.sqrt(HD)
 LOWEST = -1e30
 
@@ -61,31 +62,37 @@
         state_ref[h, :, 2 * HD :] = top
 
 
-def far_kernel(first, counts, closes, valid_ref, q_ref, state_ref, *refs):
-    *blocks, out_ref = refs
-    half = blocks[0].shape[1] // 2
+def far_kernel(heads, held_from, counts, closes, valid_ref, q_ref, state_ref, *refs):
+    *arrays, out_ref = refs
+    width = q_ref.shape[1] // HD
+    rows = q_ref.shape[0]
     groups, at = [], 0
-    for count in counts:
-        groups.append(blocks[at : at + count])
-        at += count
-    rows = q_ref.shape[0]
-
-    def part(group, lane):
-        value = group[0][:, lane]
-        for ref in group[1:]:
-            value = value + ref[:, lane]
+    for direct, relayed in counts:
+        groups.append((arrays[at : at + direct], arrays[at + direct : at + direct + relayed]))
+        at += direct + relayed
+
+    def part(refs, lane):
+        value = refs[0][:, lanes(lane)]
+        for ref in refs[1:]:
+            value = value + ref[:, lanes(lane)]
         return value
 
-    for i in range(half // HD):
-        h = first + i
+    def key_of(group, h):
+        return part(group[0], h) if h < KEYS else part(group[1], h - KEYS)
+
+    def value_of(group, h):
+        if h < VALUES:
+            return part(group[0], KEYS + h)
+        return part(group[1], width - KEYS + h - VALUES)
+
+    for i, h in enumerate(heads):
         query = q_ref[:, lanes(h)]
-        held = h if state_ref.shape[0] > half // HD else i
-        old = state_ref[held, :, 2 * HD :]
-        before = state_ref[held, :, : 2 * HD]
+        old = state_ref[h - held_from, :, 2 * HD :]
+        before = state_ref[h - held_from, :, : 2 * HD]
         scores = []
         top = old
         for b, group in enumerate(groups):
-            s = scores_of(query, part(group, lanes(i)))
+            s = scores_of(query, key_of(group, h))
             peak = jnp.broadcast_to(jnp.max(s, axis=1, keepdims=True), (rows, HD))
             top = jnp.maximum(top, jnp.where(valid_ref[b] > 0, peak, LOWEST))
             scores.append(s)
@@ -93,9 +100,10 @@
         total = before * widen(jnp.exp2(old * SCALE - shift), 2)
         for b, group in enumerate(groups):
             used = jnp.where(valid_ref[b] > 0, shift, -LOWEST)
-            value = part(group, slice(half + i * HD, half + (i + 1) * HD))
             total += jnp.dot(
-                weights_of(scores[b], used), with_ones(value), preferred_element_type=jnp.float32
+                weights_of(scores[b], used),
+                with_ones(value_of(group, h)),
+                preferred_element_type=jnp.float32,
             )
         if closes:
             out_ref[:, lanes(i)] = (total[:, :HD] * inverse(total[:, HD:])).astype(out_ref.dtype)
@@ -104,18 +112,32 @@
             out_ref[i, :, 2 * HD :] = top
 
 
-def pack_kernel(cut, k_ref, v_ref, out_ref, sems):
-    wide = out_ref.shape[1] // 2
-    copies = [
-        pltpu.make_async_copy(
-            ref.at[:, pl.ds(cut, wide)], out_ref.at[:, pl.ds(i * wide, wide)], sems.at[i]
+def pack_kernel(k_ref, v_ref, direct_ref, relayed_ref, direct_stage, relayed_stage, sems):
+    keys, values = KEYS * HD, VALUES * HD
+    total = k_ref.shape[1]
+    moves = []
+    for ref, start, wide, out, stage, at in (
+        (k_ref, keys, total - keys, relayed_ref, relayed_stage, 0),
+        (v_ref, values, total - values, relayed_ref, relayed_stage, total - keys),
+        (k_ref, 0, keys, direct_ref, direct_stage, 0),
+        (v_ref, 0, values, direct_ref, direct_stage, keys),
+    ):
+        i, place = len(moves), pl.ds(at, wide)
+        moves.append(
+            (
+                pltpu.make_async_copy(
+                    ref.at[:, pl.ds(start, wide)], stage.at[:, place], sems.at[0, i]
+                ),
+                pltpu.make_async_copy(stage.at[:, place], out.at[:, place], sems.at[1, i]),
+            )
         )
-        for i, ref in enumerate((k_ref, v_ref))
-    ]
-    for copy in copies:
-        copy.start()
-    for copy in copies:
-        copy.wait()
+    for come, _ in moves:
+        come.start()
+    for come, go in moves:
+        come.wait()
+        go.start()
+    for _, go in moves:
+        go.wait()
 
 
 def columns_kernel(which_ref, w_ref, *refs):
@@ -174,42 +196,39 @@
     )(q, k, v, pk, pv)
 
 
-def far_part(first, closes, valid, q, state, blocks):
+def far_part(heads, held_from, closes, valid, q, state, blocks):
     rows = q.shape[0]
-    arrays = [array for block in blocks for array in block]
-    heads = arrays[0].shape[1] // 2 // HD
+    arrays = [array for block in blocks for part in block for array in part]
     if closes:
-        shape = jax.ShapeDtypeStruct((rows, heads * HD), jnp.bfloat16)
+        shape = jax.ShapeDtypeStruct((rows, len(heads) * HD), jnp.bfloat16)
     else:
-        shape = jax.ShapeDtypeStruct((heads, rows, 3 * HD), jnp.float32)
-    return pl.pallas_call(
-        functools.partial(far_kernel, first, [len(block) for block in blocks], closes),
+        shape = jax.ShapeDtypeStruct((len(heads), rows, 3 * HD), jnp.float32)
+    counts = [(len(direct), len(relayed)) for direct, relayed in blocks]
+    return pl.pallas_call(
+        functools.partial(far_kernel, list(heads), held_from, counts, closes),
         out_shape=shape,
         in_specs=[pl.BlockSpec(memory_space=pltpu.SMEM)] + in_vmem(2 + len(arrays)),
         out_specs=in_vmem(1)[0],
         compiler_params=pltpu.CompilerParams(vmem_limit_bytes=8 * 2**20),
-        cost_estimate=pl.CostEstimate(
-            flops=6 * len(blocks) * heads * rows * rows * HD,
-            bytes_accessed=10 * rows * heads * HD,
-            transcendentals=len(blocks) * heads * rows * rows,
-        ),
-        name=f"far{first}_{len(blocks)}",
+        cost_estimate=LIGHT,
+        name=f"far{heads[0]}_{len(heads)}",
     )(valid, q, state, *arrays)
 
 
-def packed(k, v, cut, heads):
-    rows = k.shape[0]
-    return pl.pallas_call(
-        functools.partial(pack_kernel, cut * HD),
-        out_shape=jax.ShapeDtypeStruct((rows, 2 * heads * HD), k.dtype),
+def packed(k, v):
+    rows, width = k.shape
+    direct = (KEYS + VALUES) * HD
+    shapes = [(rows, direct), (rows, 2 * width - direct)]
+    return pl.pallas_call(
+        pack_kernel,
+        out_shape=[jax.ShapeDtypeStruct(shape, k.dtype) for shape in shapes],
         in_specs=[pl.BlockSpec(memory_space=pl.ANY)] * 2,
-        out_specs=pl.BlockSpec(memory_space=pltpu.VMEM),
-        scratch_shapes=[pltpu.SemaphoreType.DMA((2,))],
+        out_specs=[pl.BlockSpec(memory_space=pl.ANY)] * 2,
+        scratch_shapes=[pltpu.VMEM(shape, k.dtype) for shape in shapes]
+        + [pltpu.SemaphoreType.DMA((2, 4))],
         compiler_params=pltpu.CompilerParams(vmem_limit_bytes=60 * 2**20),
-        cost_estimate=pl.CostEstimate(
-            flops=0, bytes_accessed=8 * rows * heads * HD, transcendentals=0
-        ),
-        name=f"pack{cut}",
+        cost_estimate=LIGHT,
+        name="pack",
     )(k, v)
 
 
@@ -255,43 +274,45 @@
         return (c >= 0) & (c < SPANS // 2)
 
     valid = jnp.stack([inside(mate_chip), inside(other_chip), inside(third)]).astype(jnp.int32)
-    total_heads = key_states.shape[1] // HD
 
     pair_key = lax.ppermute(key_states, "seq", PAIR)
     pair_value = lax.ppermute(value_states, "seq", PAIR)
-    direct = packed(key_states, value_states, 0, DIRECT)
+    direct, relayed = packed(key_states, value_states)
+    mate1 = lax.ppermute(relayed, "seq", MATE)
     other0 = lax.ppermute(direct, "seq", OTHER)
-    direct, keys, values = lax.optimization_barrier((direct, key_states, value_states))
-    relayed = packed(keys, values, DIRECT, total_heads - DIRECT)
-    mate1 = lax.ppermute(relayed, "seq", MATE)
+    direct, relayed, pair_key, pair_value = lax.optimization_barrier(
+        (direct, relayed, pair_key, pair_value)
+    )
     mate0 = lax.ppermute(direct, "seq", MATE)
-    relayed, pair_key, pair_value = lax.optimization_barrier((relayed, pair_key, pair_value))
     row_other1 = lax.ppermute(relayed, "seq", OTHER_IN_ROW)
 
+    state = near_part(queries, key_states, value_states, pair_key, pair_value)
+    mate1, state, out_weight = lax.optimization_barrier((mate1, state, out_weight))
+    passed_other1 = lax.ppermute(mate1, "seq", ONWARD)
     z = lax.axis_index("head")
-    weights = weight_columns(
-        jnp.stack([z ^ 3, z ^ 1, z ^ 2, z]), out_weight
+    weights = weight_columns(jnp.stack([z ^ 3, z ^ 1, z ^ 2, z]), out_weight)
+    state, *weights = lax.optimization_barrier((state, *weights))
+
+    heads = range(queries.shape[1] // HD)
+    soon, later = heads[: min(KEYS, VALUES)], heads[min(KEYS, VALUES) :]
+    state, mate0 = lax.optimization_barrier((state, mate0))
+    state = far_part(heads, 0, False, valid[:1], queries, state, [[[mate0], [mate1]]])
+    state, other0 = lax.optimization_barrier((state, other0))
+    state0 = far_part(soon, 0, False, valid[1:2], queries, state, [[[other0], []]])
+    passed_other1, state0 = lax.optimization_barrier((passed_other1, state0))
+    other1 = row_other1 + passed_other1
+
+    mate_shared1 = lax.ppermute(mate1, "seq", MATE_SHARED)
+    mate_shared0 = lax.ppermute(mate0, "seq", MATE_SHARED)
+    other_shared0 = lax.ppermute(other0, "seq", OTHER_SHARED)
+    other_shared1 = lax.ppermute(other1, "seq", OTHER_SHARED)
+    state, mate_shared0, mate_shared1 = lax.optimization_barrier(
+        (state, mate_shared0, mate_shared1)
     )
-    queries, mate1, *weights = lax.optimization_barrier((queries, mate1, *weights))
-    passed_other1 = lax.ppermute(mate1, "seq", ONWARD)
-    state = near_part(queries, key_states, value_states, pair_key, pair_value)
-    other1 = row_other1 + passed_other1
-
-    mate_shared0 = lax.ppermute(mate0, "seq", MATE_SHARED)
-    mate_shared1 = lax.ppermute(mate1, "seq", MATE_SHARED)
-    other_shared1 = lax.ppermute(other1, "seq", OTHER_SHARED)
-
-    mate1, mate_shared1 = lax.optimization_barrier((mate1, mate_shared1))
-    state1 = far_part(DIRECT, False, valid[:1], queries, state, [[mate1]])
-    mate0, mate_shared0, state1 = lax.optimization_barrier((mate0, mate_shared0, state1))
-    state0 = far_part(0, False, valid[:1], queries, state, [[mate0]])
-    other0, state0, state1 = lax.optimization_barrier((other0, state0, state1))
-    other_shared0 = lax.ppermute(other0, "seq", OTHER_SHARED)
-    att1 = far_part(
-        DIRECT, True, valid[1:], queries, state1, [[other1], [mate_shared1, other_shared1]]
-    )
-    state0 = far_part(0, False, valid[1:2], queries, state0, [[other0]])
-    att0 = far_part(0, True, valid[2:], queries, state0, [[mate_shared0, other_shared0]])
+    state1 = far_part(later, 0, False, valid[1:2], queries, state, [[[other0], [other1]]])
+    third0, third1 = [mate_shared0, other_shared0], [mate_shared1, other_shared1]
+    att0 = far_part(soon, 0, True, valid[2:], queries, state0, [[third0, []]])
+    att1 = far_part(later, later[0], True, valid[2:], queries, state1, [[third0, third1]])
     return projected(att0, att1, weights)
 
 
@@ -305,11 +326,7 @@
         out_specs=in_vmem(len(out_shape)),
         scratch_shapes=[pltpu.SemaphoreType.DMA((sems,))] if sems else [],
         compiler_params=pltpu.CompilerParams(vmem_limit_bytes=limit),
-        cost_estimate=pl.CostEstimate(
-            flops=0,
-            bytes_accessed=2 * sum(o.size * o.dtype.itemsize for o in out_shape),
-            transcendentals=0,
-        ),
+        cost_estimate=LIGHT,
         name=name,
     )(*[x.astype(jnp.int32) for x in scalars], *in_hbm, *operands)
 
@@ -339,11 +356,7 @@
         in_specs=in_vmem(2 + count),
         out_specs=in_vmem(count * pieces),
         compiler_params=pltpu.CompilerParams(vmem_limit_bytes=8 * 2**20),
-        cost_estimate=pl.CostEstimate(
-            flops=2 * count * rows * depth * cols,
-            bytes_accessed=2 * count * depth * cols,
-            transcendentals=0,
-        ),
+        cost_estimate=LIGHT,
         name=f"project{count}",
     )(att0, att1, *weights)
 

time: 117 us -> 113 us (0.966)
  waiting for transfers between devices: 58.2 us -> 56.2 us
  Pallas kernels: 24.4 us -> 22.5 us
    ppermute x1, waiting for transfers between devices: 0.01 us -> 17.3 us  [body(): mate0 = lax.ppermute(direct, 'seq', MATE)]
    ppermute x1, waiting for transfers between devices: 11 us -> 0.28 us  [body(): other0 = lax.ppermute(direct, 'seq', OTHER)]
    ppermute x1, waiting for transfers between devices: 8.16 us -> 0.01 us  [body(): mate1 = lax.ppermute(relayed, 'seq', MATE)]
    ppermute x1, starting transfers between devices: 1.31 us -> 3.1 us  [body(): mate_shared1 = lax.ppermute(mate1, 'seq', MATE_SHARED)]
    ppermute x1, starting transfers between devices: 1.58 us -> 0.09 us  [body(): mate0 = lax.ppermute(direct, 'seq', MATE)]
    pallas_call x1, Pallas kernels: 4.63 us -> 3.39 us  [near_part(): pl.pallas_call(near_kernel, out_shape=jax.ShapeDtypeStruct((heads, rows,...]
    pallas_call x7 -> x6, Pallas kernels: 13.6 us -> 12.4 us  [the longest x5 10.2 us: far_part(): pl.pallas_call(functools.partial(far_kernel, list(heads), held_from, coun...]
  transfers between devices with their start and end apart: 14 -> 14, of which waited for: 5 -> 5; matrix products, arithmetic and copies ran while one was open for 1% -> 1% of each run, Pallas kernels for 16% -> 17%
where the time goes in v3:
time: 113 us
  waiting for transfers between devices  56.2 us (50%)
  starting transfers between devices  31.8 us (28%)
  Pallas kernels  22.5 us (20%)
  local copies, waits for them, and re-layouts  1.73 us (2%)
    ppermute x3, waiting for transfers between devices, sent(): lax.ppermute(value, 'head', [(i, i ^ apart) for i in range(HEAD_PEERS)])  38.6 us
    ppermute x1, waiting for transfers between devices, body(): mate0 = lax.ppermute(direct, 'seq', MATE)  17.3 us
    ppermute x1, starting transfers between devices, body(): other0 = lax.ppermute(direct, 'seq', OTHER)  10.8 us
    pallas_call x5, Pallas kernels, far_part(): pl.pallas_call(functools.partial(far_kernel, list(heads), held_from, coun...  10.2 us
    ppermute x3, starting transfers between devices, sent(): lax.ppermute(value, 'head', [(i, i ^ apart) for i in range(HEAD_PEERS)])  9.64 us
    pallas_call x2, Pallas kernels, small_call(): pl.pallas_call(kernel, out_shape=out_shape, in_specs=[pl.BlockSpec(memory...  3.96 us
    pallas_call x1, Pallas kernels, near_part(): pl.pallas_call(near_kernel, out_shape=jax.ShapeDtypeStruct((heads, rows,...  3.39 us
    ppermute x1, starting transfers between devices, body(): mate_shared1 = lax.ppermute(mate1, 'seq', MATE_SHARED)  3.1 us
  transfers between devices with their start and end apart: 14, of which 5 were waited for; matrix products, arithmetic and copies ran while one was open for 1% of the time, Pallas kernels for 17%

profile of v3, /device:TPU:24, one launch (start us, length us, event | category | flops | bytes accessed | tf_op | source)
XLA Modules:
  0.0 112.9 jit_solution(18200229265905087889)
XLA Ops:
  0.5 2.1 %pack.1 = (bf16[384,896]{1,0:T(8,128)(2,1)}, bf16[384,640]{1,0:T(8,128)(2,1)}) custom-call(bf16[384,768]{1,0:T(8,128)(2,1)} %k_ref.3, bf16[384,768]{1,0:T(8,128)(2,1)} %v_ref.3), custom_call_target="tpu_custom_call" | custom-call | flops 1 | bytes 1 | tf_op jit(solution)/shard_map/pack/pallas_call | solution.py:222
  2.7 1.6 %collective-permute-start = (bf16[384,640]{1,0:T(8,128)(2,1)}, bf16[384,640]{1,0:T(8,128)(2,1)S(1)}, u32[]{:S(2)}, u32[]{:S(2)}) collective-permute-start(bf16[384,640]{1,0:T(8,128)(2,1)} %get-tuple-element.55), channel_id=1, source_target_pairs={{0,8},{4,12},{8,0},{12,4},{16,24},{20,28},{24,16},{28,20},{32,40},... | collective-permute-start | bytes 1474568 | tf_op jit(solution)/shard_map/ppermute | solution.py:281
  4.2 10.8 %collective-permute-start.5 = (bf16[384,896]{1,0:T(8,128)(2,1)}, bf16[384,896]{1,0:T(8,128)(2,1)S(1)}, u32[]{:S(2)}, u32[]{:S(2)}) collective-permute-start(bf16[384,896]{1,0:T(8,128)(2,1)} %get-tuple-element.47), channel_id=1, source_target_pairs={{8,16},{12,20},{16,8},{20,12},{24,32},{28,36},{32,24},{36,28},{40,... | collective-permute-start | bytes 2064392 | tf_op jit(solution)/shard_map/ppermute | solution.py:282
  15.2 1.1 copy-done.2
  16.3 3.4 %near.1.state_ref = f32[6,384,384]{2,1,0:T(8,128)S(1)} custom-call(bf16[384,768]{1,0:T(8,128)(2,1)S(1)} %copy-done, bf16[384,768]{1,0:T(8,128)(2,1)S(1)} %copy-done.1, bf16[384,768]{1,0:T(8,128)(2,1)S(1)} %copy-done.2, bf16[384,768]{1,0:T(8,128)(2,1)S(1)} %collective-permute-done.1.pk_ref, bf16[384,768]{1,0:T(8,128)(2,1)S(1)} %collective-permute-done.2.pv_ref), custom_call_target="tpu_custom_call" | custom-call | flops 40768634880 | bytes 2949120 | tf_op jit(solution)/shard_map/near/pallas_call | solution.py:184
  19.7 1.3 %collective-permute-start.3 = (bf16[384,640]{1,0:T(8,128)(2,1)S(1)}, bf16[384,640]{1,0:T(8,128)(2,1)S(1)}, u32[]{:S(2)}, u32[]{:S(2)}) collective-permute-start(bf16[384,640]{1,0:T(8,128)(2,1)S(1)} %collective-permute-done.refs_1_), channel_id=1, source_target_pairs={{16,32},{20,36},{40,24},{44,28},{48,64},{52,68},{72,56},{76,60},{8... | collective-permute-start | bytes 1474568 | tf_op jit(solution)/shard_map/ppermute | solution.py:291
  22.5 2.9 %columns.1 = (bf16[768,768]{1,0:T(8,128)(2,1)S(1)}, bf16[768,768]{1,0:T(8,128)(2,1)S(1)}, bf16[768,768]{1,0:T(8,128)(2,1)S(1)}, bf16[768,768]{1,0:T(8,128)(2,1)S(1)}) custom-call(s32[4]{0:T(128)S(1)} %pad_add_fusion.which_ref, bf16[768,3072]{1,0:T(8,128)(2,1)} %w_ref), custom_call_target="tpu_custom_call" | custom-call | flops 1 | bytes 1 | tf_op jit(solution)/shard_map/columns/pallas_call | solution.py:320
  25.5 17.3 %collective-permute-done.4.refs_0_ = bf16[384,896]{1,0:T(8,128)(2,1)S(1)} collective-permute-done((bf16[384,896]{1,0:T(8,128)(2,1)}, bf16[384,896]{1,0:T(8,128)(2,1)S(1)}, u32[]{:S(2)}, u32[]{:S(2)}) %collective-permute-start.4) | collective-permute-done | bytes 688160 | tf_op jit(solution)/shard_map/ppermute | solution.py:286
  42.8 1.3 %collective-permute-start.6 = (bf16[384,896]{1,0:T(8,128)(2,1)S(1)}, bf16[384,896]{1,0:T(8,128)(2,1)S(1)}, u32[]{:S(2)}, u32[]{:S(2)}) collective-permute-start(bf16[384,896]{1,0:T(8,128)(2,1)S(1)} %collective-permute-done.4.refs_0_), channel_id=1, source_target_pairs={{0,4},{12,8},{16,20},{28,24},{32,36},{44,40},{48,52},{60,56},{64,6... | collective-permute-start | bytes 2064392 | tf_op jit(solution)/shard_map/ppermute | solution.py:306
  44.1 2.7 %far0_6.1.state_ref = f32[6,384,384]{2,1,0:T(8,128)S(1)} custom-call(s32[1]{0:T(128)} %get-tuple-element.65.valid_ref, bf16[384,768]{1,0:T(8,128)(2,1)S(1)} %copy-done, f32[6,384,384]{2,1,0:T(8,128)S(1)} %near.1.state_ref, bf16[384,896]{1,0:T(8,128)(2,1)S(1)} %collective-permute-done.4.refs_0_, bf16[384,640]{1,0:T(8,128)(2,1)S(1)} %collective-permute-done.refs_1_), custom_call_target="tpu_custom_call" | custom-call | flops 1 | bytes 1 | tf_op jit(solution)/shard_map/far0_6/pallas_call | solution.py:207
  47.2 1.3 %collective-permute-start.8 = (bf16[384,896]{1,0:T(8,128)(2,1)S(1)}, bf16[384,896]{1,0:T(8,128)(2,1)S(1)}, u32[]{:S(2)}, u32[]{:S(2)}) collective-permute-start(bf16[384,896]{1,0:T(8,128)(2,1)S(1)} %collective-permute-done.5.refs_0_), channel_id=1, source_target_pairs={{4,0},{8,12},{20,16},{24,28},{36,32},{40,44},{52,48},{56,60},{68,6... | collective-permute-start | bytes 2064392 | tf_op jit(solution)/shard_map/ppermute | solution.py:307
  48.5 3.1 %collective-permute-start.7 = (bf16[384,640]{1,0:T(8,128)(2,1)S(1)}, bf16[384,640]{1,0:T(8,128)(2,1)S(1)}, u32[]{:S(2)}, u32[]{:S(2)}) collective-permute-start(bf16[384,640]{1,0:T(8,128)(2,1)S(1)} %collective-permute-done.refs_1_), channel_id=1, source_target_pairs={{0,4},{12,8},{16,20},{28,24},{32,36},{44,40},{48,52},{60,56},{64,6... | collective-permute-start | bytes 1474568 | tf_op jit(solution)/shard_map/ppermute | solution.py:305
  51.6 1.9 %far0_3.2.state_ref = f32[3,384,384]{2,1,0:T(8,128)S(1)} custom-call(s32[1]{0:T(128)} %get-tuple-element.66.valid_ref, bf16[384,768]{1,0:T(8,128)(2,1)S(1)} %copy-done, f32[6,384,384]{2,1,0:T(8,128)S(1)} %far0_6.1.state_ref, bf16[384,896]{1,0:T(8,128)(2,1)S(1)} %collective-permute-done.5.refs_0_), custom_call_target="tpu_custom_call" | custom-call | flops 1 | bytes 1 | tf_op jit(solution)/shard_map/far0_3/pallas_call | solution.py:207
  53.6 1.5 %collective-permute-start.10 = (bf16[384,640]{1,0:T(8,128)(2,1)S(1)}, bf16[384,640]{1,0:T(8,128)(2,1)S(1)}, u32[]{:S(2)}, u32[]{:S(2)}) collective-permute-start(bf16[384,640]{1,0:T(8,128)(2,1)S(1)} %add.17.refs_1_), channel_id=1, source_target_pairs={{4,0},{8,12},{20,16},{24,28},{36,32},{40,44},{52,48},{56,60},{68,6... | collective-permute-start | bytes 1474568 | tf_op jit(solution)/shard_map/ppermute | solution.py:308
  55.1 1.9 %far3_3.2.state_ref = f32[3,384,384]{2,1,0:T(8,128)S(1)} custom-call(s32[1]{0:T(128)} %get-tuple-element.66.valid_ref, bf16[384,768]{1,0:T(8,128)(2,1)S(1)} %copy-done, f32[6,384,384]{2,1,0:T(8,128)S(1)} %far0_6.1.state_ref, bf16[384,896]{1,0:T(8,128)(2,1)S(1)} %collective-permute-done.5.refs_0_, bf16[384,640]{1,0:T(8,128)(2,1)S(1)} %add.17.refs_1_), custom_call_target="tpu_custom_call" | custom-call | flops 1 | bytes 1 | tf_op jit(solution)/shard_map/far3_3/pallas_call | solution.py:207
  57.1 1.8 %far0_3.3.att0_ref = bf16[384,384]{1,0:T(8,128)(2,1)S(1)} custom-call(s32[1]{0:T(128)} %get-tuple-element.67.valid_ref, bf16[384,768]{1,0:T(8,128)(2,1)S(1)} %copy-done, f32[3,384,384]{2,1,0:T(8,128)S(1)} %far0_3.2.state_ref, bf16[384,896]{1,0:T(8,128)(2,1)S(1)} %collective-permute-done.6.refs_0_, bf16[384,896]{1,0:T(8,128)(2,1)S(1)} %collective-permute-done.8.refs_1_), custom_call_target="tpu_custom_call" | custom-call | flops 1 | bytes 1 | tf_op jit(solution)/shard_map/far0_3/pallas_call | solution.py:207
  58.9 1.8 %far3_3.3.att1_ref = bf16[384,384]{1,0:T(8,128)(2,1)S(1)} custom-call(s32[1]{0:T(128)} %get-tuple-element.67.valid_ref, bf16[384,768]{1,0:T(8,128)(2,1)S(1)} %copy-done, f32[3,384,384]{2,1,0:T(8,128)S(1)} %far3_3.2.state_ref, bf16[384,896]{1,0:T(8,128)(2,1)S(1)} %collective-permute-done.6.refs_0_, bf16[384,896]{1,0:T(8,128)(2,1)S(1)} %collective-permute-done.8.refs_1_, ...), custom_call_target="tpu_custom_call" | custom-call | flops 1 | bytes 1 | tf_op jit(solution)/shard_map/far3_3/pallas_call | solution.py:207
  62.4 2.0 %project3.1 = (bf16[384,768]{1,0:T(8,128)(2,1)S(1)}, bf16[384,768]{1,0:T(8,128)(2,1)S(1)}, bf16[384,768]{1,0:T(8,128)(2,1)S(1)}) custom-call(bf16[384,384]{1,0:T(8,128)(2,1)S(1)} %far0_3.3.att0_ref, bf16[384,384]{1,0:T(8,128)(2,1)S(1)} %far3_3.3.att1_ref, bf16[768,768]{1,0:T(8,128)(2,1)S(1)} %get-tuple-element.58.refs_0_, ...), custom_call_target="tpu_custom_call" | custom-call | flops 1 | bytes 1 | tf_op jit(solution)/shard_map/project3/pallas_call | solution.py:353
  64.4 1.3 %collective-permute-start.11 = (bf16[384,768]{1,0:T(8,128)(2,1)S(1)}, bf16[384,768]{1,0:T(8,128)(2,1)S(1)}, u32[]{:S(2)}, u32[]{:S(2)}) collective-permute-start(bf16[384,768]{1,0:T(8,128)(2,1)S(1)} %get-tuple-element.62), channel_id=1, source_target_pairs={{0,1},{1,0},{2,3},{3,2},{4,5},{5,4},{6,7},{7,6},{8,9},{9,8},{10,11... | collective-permute-start | bytes 1769480 | tf_op jit(solution)/shard_map/ppermute | solution.py:366
  65.7 11.9 %collective-permute-done.12 = bf16[384,768]{1,0:T(8,128)(2,1)S(1)} collective-permute-done((bf16[384,768]{1,0:T(8,128)(2,1)S(1)}, bf16[384,768]{1,0:T(8,128)(2,1)S(1)}, u32[]{:S(2)}, u32[]{:S(2)}) %collective-permute-start.12) | collective-permute-done | bytes 589856 | tf_op jit(solution)/shard_map/ppermute | solution.py:366
  77.8 7.4 %collective-permute-start.13 = (bf16[384,768]{1,0:T(8,128)(2,1)S(1)}, bf16[384,768]{1,0:T(8,128)(2,1)S(1)}, u32[]{:S(2)}, u32[]{:S(2)}) collective-permute-start(bf16[384,768]{1,0:T(8,128)(2,1)S(1)} %add_convert_fusion), channel_id=1, source_target_pairs={{0,2},{1,3},{2,0},{3,1},{4,6},{5,7},{6,4},{7,5},{8,10},{9,11},{10,... | collective-permute-start | bytes 1769480 | tf_op jit(solution)/shard_map/ppermute | solution.py:366
  85.2 15.8 %collective-permute-done.11.refs_1_ = bf16[384,768]{1,0:T(8,128)(2,1)S(1)} collective-permute-done((bf16[384,768]{1,0:T(8,128)(2,1)S(1)}, bf16[384,768]{1,0:T(8,128)(2,1)S(1)}, u32[]{:S(2)}, u32[]{:S(2)}) %collective-permute-start.11) | collective-permute-done | bytes 589856 | tf_op jit(solution)/shard_map/ppermute | solution.py:366
  101.0 10.8 %collective-permute-done.13.refs_2_ = bf16[384,768]{1,0:T(8,128)(2,1)S(1)} collective-permute-done((bf16[384,768]{1,0:T(8,128)(2,1)S(1)}, bf16[384,768]{1,0:T(8,128)(2,1)S(1)}, u32[]{:S(2)}, u32[]{:S(2)}) %collective-permute-start.13) | collective-permute-done | bytes 589856 | tf_op jit(solution)/shard_map/ppermute | solution.py:366
  111.9 1.0 last_sum.1
  (28 shorter events, 4.3 us)
Async XLA Ops:
  0.0 15.2 %copy-start.1 = (bf16[384,768]{1,0:T(8,128)(2,1)S(1)}, bf16[384,768]{1,0:T(8,128)(2,1)}, u32[]{:S(2)}) copy-start(bf16[384,768]{1,0:T(8,128)(2,1)} %k_ref.3) | copy-start | bytes 1769476
  0.0 15.2 %copy-start = (bf16[384,768]{1,0:T(8,128)(2,1)S(1)}, bf16[384,768]{1,0:T(8,128)(2,1)}, u32[]{:S(2)}) copy-start(bf16[384,768]{1,0:T(8,128)(2,1)} %q_ref.11) | copy-start | bytes 1769476
  0.0 15.1 %collective-permute-start.1 = (bf16[384,768]{1,0:T(8,128)(2,1)}, bf16[384,768]{1,0:T(8,128)(2,1)S(1)}, u32[]{:S(2)}, u32[]{:S(2)}) collective-permute-start(bf16[384,768]{1,0:T(8,128)(2,1)} %k_ref.3), channel_id=1, source_target_pairs={{0,4},{4,0},{8,12},{12,8},{16,20},{20,16},{24,28},{28,24},{32,36},... | collective-permute-start | bytes 1769480 | tf_op jit(solution)/shard_map/ppermute | solution.py:278
  0.0 15.1 %collective-permute-start.2 = (bf16[384,768]{1,0:T(8,128)(2,1)}, bf16[384,768]{1,0:T(8,128)(2,1)S(1)}, u32[]{:S(2)}, u32[]{:S(2)}) collective-permute-start(bf16[384,768]{1,0:T(8,128)(2,1)} %v_ref.3), channel_id=1, source_target_pairs={{0,4},{4,0},{8,12},{12,8},{16,20},{20,16},{24,28},{28,24},{32,36},... | collective-permute-start | bytes 1769480 | tf_op jit(solution)/shard_map/ppermute | solution.py:279
  2.7 17.0 %collective-permute-start = (bf16[384,640]{1,0:T(8,128)(2,1)}, bf16[384,640]{1,0:T(8,128)(2,1)S(1)}, u32[]{:S(2)}, u32[]{:S(2)}) collective-permute-start(bf16[384,640]{1,0:T(8,128)(2,1)} %get-tuple-element.55), channel_id=1, source_target_pairs={{0,8},{4,12},{8,0},{12,4},{16,24},{20,28},{24,16},{28,20},{32,40},... | collective-permute-start | bytes 1474568 | tf_op jit(solution)/shard_map/ppermute | solution.py:281
  4.2 42.9 %collective-permute-start.5 = (bf16[384,896]{1,0:T(8,128)(2,1)}, bf16[384,896]{1,0:T(8,128)(2,1)S(1)}, u32[]{:S(2)}, u32[]{:S(2)}) collective-permute-start(bf16[384,896]{1,0:T(8,128)(2,1)} %get-tuple-element.47), channel_id=1, source_target_pairs={{8,16},{12,20},{16,8},{20,12},{24,32},{28,36},{32,24},{36,28},{40,... | collective-permute-start | bytes 2064392 | tf_op jit(solution)/shard_map/ppermute | solution.py:282
  15.1 27.7 %collective-permute-start.4 = (bf16[384,896]{1,0:T(8,128)(2,1)}, bf16[384,896]{1,0:T(8,128)(2,1)S(1)}, u32[]{:S(2)}, u32[]{:S(2)}) collective-permute-start(bf16[384,896]{1,0:T(8,128)(2,1)} %get-tuple-element.47), channel_id=1, source_target_pairs={{0,8},{4,12},{8,0},{12,4},{16,24},{20,28},{24,16},{28,20},{32,40},... | collective-permute-start | bytes 2064392 | tf_op jit(solution)/shard_map/ppermute | solution.py:286
  15.2 1.1 copy-start.2
  16.3 4.7 %copy-start.3 = (bf16[384,640]{1,0:T(8,128)(2,1)S(1)}, bf16[384,640]{1,0:T(8,128)(2,1)}, u32[]{:S(2)}) copy-start(bf16[384,640]{1,0:T(8,128)(2,1)} %get-tuple-element.55) | copy-start | bytes 1474564
  19.7 33.8 %collective-permute-start.3 = (bf16[384,640]{1,0:T(8,128)(2,1)S(1)}, bf16[384,640]{1,0:T(8,128)(2,1)S(1)}, u32[]{:S(2)}, u32[]{:S(2)}) collective-permute-start(bf16[384,640]{1,0:T(8,128)(2,1)S(1)} %collective-permute-done.refs_1_), channel_id=1, source_target_pairs={{16,32},{20,36},{40,24},{44,28},{48,64},{52,68},{72,56},{76,60},{8... | collective-permute-start | bytes 1474568 | tf_op jit(solution)/shard_map/ppermute | solution.py:291
  21.0 32.5 %collective-permute-start.9 = (bf16[384,640]{1,0:T(8,128)(2,1)S(1)}, bf16[384,640]{1,0:T(8,128)(2,1)S(1)}, u32[]{:S(2)}, u32[]{:S(2)}) collective-permute-start(bf16[384,640]{1,0:T(8,128)(2,1)S(1)} %copy-done.3), channel_id=1, source_target_pairs={{8,16},{12,20},{16,8},{20,12},{40,48},{44,52},{48,40},{52,44},{72,... | collective-permute-start | bytes 1474568 | tf_op jit(solution)/shard_map/ppermute | solution.py:287
  42.8 12.3 %collective-permute-start.6 = (bf16[384,896]{1,0:T(8,128)(2,1)S(1)}, bf16[384,896]{1,0:T(8,128)(2,1)S(1)}, u32[]{:S(2)}, u32[]{:S(2)}) collective-permute-start(bf16[384,896]{1,0:T(8,128)(2,1)S(1)} %collective-permute-done.4.refs_0_), channel_id=1, source_target_pairs={{0,4},{12,8},{16,20},{28,24},{32,36},{44,40},{48,52},{60,56},{64,6... | collective-permute-start | bytes 2064392 | tf_op jit(solution)/shard_map/ppermute | solution.py:306
  47.2 9.9 %collective-permute-start.8 = (bf16[384,896]{1,0:T(8,128)(2,1)S(1)}, bf16[384,896]{1,0:T(8,128)(2,1)S(1)}, u32[]{:S(2)}, u32[]{:S(2)}) collective-permute-start(bf16[384,896]{1,0:T(8,128)(2,1)S(1)} %collective-permute-done.5.refs_0_), channel_id=1, source_target_pairs={{4,0},{8,12},{20,16},{24,28},{36,32},{40,44},{52,48},{56,60},{68,6... | collective-permute-start | bytes 2064392 | tf_op jit(solution)/shard_map/ppermute | solution.py:307
  48.5 6.7 %collective-permute-start.7 = (bf16[384,640]{1,0:T(8,128)(2,1)S(1)}, bf16[384,640]{1,0:T(8,128)(2,1)S(1)}, u32[]{:S(2)}, u32[]{:S(2)}) collective-permute-start(bf16[384,640]{1,0:T(8,128)(2,1)S(1)} %collective-permute-done.refs_1_), channel_id=1, source_target_pairs={{0,4},{12,8},{16,20},{28,24},{32,36},{44,40},{48,52},{60,56},{64,6... | collective-permute-start | bytes 1474568 | tf_op jit(solution)/shard_map/ppermute | solution.py:305
  53.6 5.3 %collective-permute-start.10 = (bf16[384,640]{1,0:T(8,128)(2,1)S(1)}, bf16[384,640]{1,0:T(8,128)(2,1)S(1)}, u32[]{:S(2)}, u32[]{:S(2)}) collective-permute-start(bf16[384,640]{1,0:T(8,128)(2,1)S(1)} %add.17.refs_1_), channel_id=1, source_target_pairs={{4,0},{8,12},{20,16},{24,28},{36,32},{40,44},{52,48},{56,60},{68,6... | collective-permute-start | bytes 1474568 | tf_op jit(solution)/shard_map/ppermute | solution.py:308
  61.5 16.1 %collective-permute-start.12 = (bf16[384,768]{1,0:T(8,128)(2,1)S(1)}, bf16[384,768]{1,0:T(8,128)(2,1)S(1)}, u32[]{:S(2)}, u32[]{:S(2)}) collective-permute-start(bf16[384,768]{1,0:T(8,128)(2,1)S(1)} %project1.1), channel_id=1, source_target_pairs={{0,1},{1,0},{2,3},{3,2},{4,5},{5,4},{6,7},{7,6},{8,9},{9,8},{10,11... | collective-permute-start | bytes 1769480 | tf_op jit(solution)/shard_map/ppermute | solution.py:366
  64.4 36.6 %collective-permute-start.11 = (bf16[384,768]{1,0:T(8,128)(2,1)S(1)}, bf16[384,768]{1,0:T(8,128)(2,1)S(1)}, u32[]{:S(2)}, u32[]{:S(2)}) collective-permute-start(bf16[384,768]{1,0:T(8,128)(2,1)S(1)} %get-tuple-element.62), channel_id=1, source_target_pairs={{0,1},{1,0},{2,3},{3,2},{4,5},{5,4},{6,7},{7,6},{8,9},{9,8},{10,11... | collective-permute-start | bytes 1769480 | tf_op jit(solution)/shard_map/ppermute | solution.py:366
  77.8 34.1 %collective-permute-start.13 = (bf16[384,768]{1,0:T(8,128)(2,1)S(1)}, bf16[384,768]{1,0:T(8,128)(2,1)S(1)}, u32[]{:S(2)}, u32[]{:S(2)}) collective-permute-start(bf16[384,768]{1,0:T(8,128)(2,1)S(1)} %add_convert_fusion), channel_id=1, source_target_pairs={{0,2},{1,3},{2,0},{3,1},{4,6},{5,7},{6,4},{7,5},{8,10},{9,11},{10,... | collective-permute-start | bytes 1769480 | tf_op jit(solution)/shard_map/ppermute | solution.py:366

commit v4 on v3

--- a/solution.py
+++ b/solution.py
@@ -298,21 +298,20 @@
     state, mate0 = lax.optimization_barrier((state, mate0))
     state = far_part(heads, 0, False, valid[:1], queries, state, [[[mate0], [mate1]]])
     state, other0 = lax.optimization_barrier((state, other0))
+    mate_shared1 = lax.ppermute(mate1, "seq", MATE_SHARED)
+    mate_shared0 = lax.ppermute(mate0, "seq", MATE_SHARED)
+    state, mate_shared1 = lax.optimization_barrier((state, mate_shared1))
     state0 = far_part(soon, 0, False, valid[1:2], queries, state, [[[other0], []]])
     passed_other1, state0 = lax.optimization_barrier((passed_other1, state0))
     other1 = row_other1 + passed_other1
-
-    mate_shared1 = lax.ppermute(mate1, "seq", MATE_SHARED)
-    mate_shared0 = lax.ppermute(mate0, "seq", MATE_SHARED)
     other_shared0 = lax.ppermute(other0, "seq", OTHER_SHARED)
     other_shared1 = lax.ppermute(other1, "seq", OTHER_SHARED)
-    state, mate_shared0, mate_shared1 = lax.optimization_barrier(
-        (state, mate_shared0, mate_shared1)
-    )
-    state1 = far_part(later, 0, False, valid[1:2], queries, state, [[[other0], [other1]]])
     third0, third1 = [mate_shared0, other_shared0], [mate_shared1, other_shared1]
     att0 = far_part(soon, 0, True, valid[2:], queries, state0, [[third0, []]])
-    att1 = far_part(later, later[0], True, valid[2:], queries, state1, [[third0, third1]])
+    state, att0 = lax.optimization_barrier((state, att0))
+    att1 = far_part(
+        later, 0, True, valid[1:], queries, state, [[[other0], [other1]], [third0, third1]]
+    )
     return projected(att0, att1, weights)
 
 

time: 113 us -> 109 us (0.965)
  starting transfers between devices: 31.8 us -> 29.4 us
    ppermute x1, waiting for transfers between devices: 17.3 us -> 10.4 us  [body(): mate0 = lax.ppermute(direct, 'seq', MATE)]
    ppermute x1, waiting for transfers between devices: 0.28 us -> 4.61 us  [body(): other0 = lax.ppermute(direct, 'seq', OTHER)]
    ppermute x1, waiting for transfers between devices: 0.01 us -> 1.96 us  [body(): passed_other1 = lax.ppermute(mate1, 'seq', ONWARD)]
    ppermute x1, starting transfers between devices: 3.1 us -> 1.46 us  [body(): mate_shared1 = lax.ppermute(mate1, 'seq', MATE_SHARED)]
    pallas_call x5 -> x4, Pallas kernels: 10.2 us -> 9.2 us  [far_part(): pl.pallas_call(functools.partial(far_kernel, list(heads), held_from, coun...]
  transfers between devices with their start and end apart: 14 -> 14, of which waited for: 5 -> 7; matrix products, arithmetic and copies ran while one was open for 1% -> 1% of each run, Pallas kernels for 17% -> 16%
where the time goes in v4:
time: 109 us
  waiting for transfers between devices  55.2 us (51%)
  starting transfers between devices  29.4 us (27%)
  Pallas kernels  21.5 us (20%)
  local copies, waits for them, and re-layouts  1.81 us (2%)
    ppermute x3, waiting for transfers between devices, sent(): lax.ppermute(value, 'head', [(i, i ^ apart) for i in range(HEAD_PEERS)])  38 us
    ppermute x1, starting transfers between devices, body(): other0 = lax.ppermute(direct, 'seq', OTHER)  10.8 us
    ppermute x1, waiting for transfers between devices, body(): mate0 = lax.ppermute(direct, 'seq', MATE)  10.4 us
    pallas_call x4, Pallas kernels, far_part(): pl.pallas_call(functools.partial(far_kernel, list(heads), held_from, coun...  9.2 us
    ppermute x3, starting transfers between devices, sent(): lax.ppermute(value, 'head', [(i, i ^ apart) for i in range(HEAD_PEERS)])  8.89 us
    ppermute x1, waiting for transfers between devices, body(): other0 = lax.ppermute(direct, 'seq', OTHER)  4.61 us
    pallas_call x2, Pallas kernels, small_call(): pl.pallas_call(kernel, out_shape=out_shape, in_specs=[pl.BlockSpec(memory...  3.96 us
    pallas_call x1, Pallas kernels, near_part(): pl.pallas_call(near_kernel, out_shape=jax.ShapeDtypeStruct((heads, rows,...  3.43 us
  transfers between devices with their start and end apart: 14, of which 7 were waited for; matrix products, arithmetic and copies ran while one was open for 1% of the time, Pallas kernels for 16%

profile of v4, /device:TPU:24, one launch (start us, length us, event | category | flops | bytes accessed | tf_op | source)
XLA Modules:
  0.0 108.6 jit_solution(6948582001985540994)
XLA Ops:
  0.5 2.1 %pack.1 = (bf16[384,896]{1,0:T(8,128)(2,1)}, bf16[384,640]{1,0:T(8,128)(2,1)}) custom-call(bf16[384,768]{1,0:T(8,128)(2,1)} %k_ref.3, bf16[384,768]{1,0:T(8,128)(2,1)} %v_ref.3), custom_call_target="tpu_custom_call" | custom-call | flops 1 | bytes 1 | tf_op jit(solution)/shard_map/pack/pallas_call | solution.py:222
  2.7 1.6 %collective-permute-start = (bf16[384,640]{1,0:T(8,128)(2,1)}, bf16[384,640]{1,0:T(8,128)(2,1)S(1)}, u32[]{:S(2)}, u32[]{:S(2)}) collective-permute-start(bf16[384,640]{1,0:T(8,128)(2,1)} %get-tuple-element.57), channel_id=1, source_target_pairs={{0,8},{4,12},{8,0},{12,4},{16,24},{20,28},{24,16},{28,20},{32,40},... | collective-permute-start | bytes 1474568 | tf_op jit(solution)/shard_map/ppermute | solution.py:281
  4.2 10.8 %collective-permute-start.4 = (bf16[384,896]{1,0:T(8,128)(2,1)}, bf16[384,896]{1,0:T(8,128)(2,1)S(1)}, u32[]{:S(2)}, u32[]{:S(2)}) collective-permute-start(bf16[384,896]{1,0:T(8,128)(2,1)} %get-tuple-element.47), channel_id=1, source_target_pairs={{8,16},{12,20},{16,8},{20,12},{24,32},{28,36},{32,24},{36,28},{40,... | collective-permute-start | bytes 2064392 | tf_op jit(solution)/shard_map/ppermute | solution.py:282
  15.2 1.1 copy-done.2
  16.3 3.4 %near.1.state_ref = f32[6,384,384]{2,1,0:T(8,128)S(1)} custom-call(bf16[384,768]{1,0:T(8,128)(2,1)S(1)} %copy-done, bf16[384,768]{1,0:T(8,128)(2,1)S(1)} %copy-done.1, bf16[384,768]{1,0:T(8,128)(2,1)S(1)} %copy-done.2, bf16[384,768]{1,0:T(8,128)(2,1)S(1)} %collective-permute-done.1.pk_ref, bf16[384,768]{1,0:T(8,128)(2,1)S(1)} %collective-permute-done.2.pv_ref), custom_call_target="tpu_custom_call" | custom-call | flops 40768634880 | bytes 2949120 | tf_op jit(solution)/shard_map/near/pallas_call | solution.py:184
  19.7 1.5 %collective-permute-start.5 = (bf16[384,640]{1,0:T(8,128)(2,1)S(1)}, bf16[384,640]{1,0:T(8,128)(2,1)S(1)}, u32[]{:S(2)}, u32[]{:S(2)}) collective-permute-start(bf16[384,640]{1,0:T(8,128)(2,1)S(1)} %collective-permute-done.refs_1_), channel_id=1, source_target_pairs={{0,4},{12,8},{16,20},{28,24},{32,36},{44,40},{48,52},{60,56},{64,6... | collective-permute-start | bytes 1474568 | tf_op jit(solution)/shard_map/ppermute | solution.py:301
  21.2 1.3 %collective-permute-start.6 = (bf16[384,640]{1,0:T(8,128)(2,1)S(1)}, bf16[384,640]{1,0:T(8,128)(2,1)S(1)}, u32[]{:S(2)}, u32[]{:S(2)}) collective-permute-start(bf16[384,640]{1,0:T(8,128)(2,1)S(1)} %collective-permute-done.refs_1_), channel_id=1, source_target_pairs={{16,32},{20,36},{40,24},{44,28},{48,64},{52,68},{72,56},{76,60},{8... | collective-permute-start | bytes 1474568 | tf_op jit(solution)/shard_map/ppermute | solution.py:291
  24.0 2.9 %columns.1 = (bf16[768,768]{1,0:T(8,128)(2,1)S(1)}, bf16[768,768]{1,0:T(8,128)(2,1)S(1)}, bf16[768,768]{1,0:T(8,128)(2,1)S(1)}, bf16[768,768]{1,0:T(8,128)(2,1)S(1)}) custom-call(s32[4]{0:T(128)S(1)} %pad_add_fusion.which_ref, bf16[768,3072]{1,0:T(8,128)(2,1)} %w_ref), custom_call_target="tpu_custom_call" | custom-call | flops 1 | bytes 1 | tf_op jit(solution)/shard_map/columns/pallas_call | solution.py:319
  27.0 10.4 %collective-permute-done.3.refs_0_ = bf16[384,896]{1,0:T(8,128)(2,1)S(1)} collective-permute-done((bf16[384,896]{1,0:T(8,128)(2,1)}, bf16[384,896]{1,0:T(8,128)(2,1)S(1)}, u32[]{:S(2)}, u32[]{:S(2)}) %collective-permute-start.3) | collective-permute-done | bytes 688160 | tf_op jit(solution)/shard_map/ppermute | solution.py:286
  37.4 1.3 %collective-permute-start.7 = (bf16[384,896]{1,0:T(8,128)(2,1)S(1)}, bf16[384,896]{1,0:T(8,128)(2,1)S(1)}, u32[]{:S(2)}, u32[]{:S(2)}) collective-permute-start(bf16[384,896]{1,0:T(8,128)(2,1)S(1)} %collective-permute-done.3.refs_0_), channel_id=1, source_target_pairs={{0,4},{12,8},{16,20},{28,24},{32,36},{44,40},{48,52},{60,56},{64,6... | collective-permute-start | bytes 2064392 | tf_op jit(solution)/shard_map/ppermute | solution.py:302
  38.7 2.7 %far0_6.1.state_ref = f32[6,384,384]{2,1,0:T(8,128)S(1)} custom-call(s32[1]{0:T(128)} %get-tuple-element.69.valid_ref, bf16[384,768]{1,0:T(8,128)(2,1)S(1)} %copy-done, f32[6,384,384]{2,1,0:T(8,128)S(1)} %near.1.state_ref, bf16[384,896]{1,0:T(8,128)(2,1)S(1)} %collective-permute-done.3.refs_0_, bf16[384,640]{1,0:T(8,128)(2,1)S(1)} %collective-permute-done.refs_1_), custom_call_target="tpu_custom_call" | custom-call | flops 1 | bytes 1 | tf_op jit(solution)/shard_map/far0_6/pallas_call | solution.py:207
  41.4 4.6 %collective-permute-done.4.refs_0_ = bf16[384,896]{1,0:T(8,128)(2,1)S(1)} collective-permute-done((bf16[384,896]{1,0:T(8,128)(2,1)}, bf16[384,896]{1,0:T(8,128)(2,1)S(1)}, u32[]{:S(2)}, u32[]{:S(2)}) %collective-permute-start.4) | collective-permute-done | bytes 688160 | tf_op jit(solution)/shard_map/ppermute | solution.py:282
  46.1 1.3 %collective-permute-start.8 = (bf16[384,896]{1,0:T(8,128)(2,1)S(1)}, bf16[384,896]{1,0:T(8,128)(2,1)S(1)}, u32[]{:S(2)}, u32[]{:S(2)}) collective-permute-start(bf16[384,896]{1,0:T(8,128)(2,1)S(1)} %collective-permute-done.4.refs_0_), channel_id=1, source_target_pairs={{4,0},{8,12},{20,16},{24,28},{36,32},{40,44},{52,48},{56,60},{68,6... | collective-permute-start | bytes 2064392 | tf_op jit(solution)/shard_map/ppermute | solution.py:307
  47.4 1.9 %far0_3.2.state_ref = f32[3,384,384]{2,1,0:T(8,128)S(1)} custom-call(s32[1]{0:T(128)} %get-tuple-element.67.valid_ref, bf16[384,768]{1,0:T(8,128)(2,1)S(1)} %copy-done, f32[6,384,384]{2,1,0:T(8,128)S(1)} %far0_6.1.state_ref, bf16[384,896]{1,0:T(8,128)(2,1)S(1)} %collective-permute-done.4.refs_0_), custom_call_target="tpu_custom_call" | custom-call | flops 1 | bytes 1 | tf_op jit(solution)/shard_map/far0_3/pallas_call | solution.py:207
  49.2 2.0 %collective-permute-done.6 = bf16[384,640]{1,0:T(8,128)(2,1)S(1)} collective-permute-done((bf16[384,640]{1,0:T(8,128)(2,1)S(1)}, bf16[384,640]{1,0:T(8,128)(2,1)S(1)}, u32[]{:S(2)}, u32[]{:S(2)}) %collective-permute-start.6) | collective-permute-done | bytes 491552 | tf_op jit(solution)/shard_map/ppermute | solution.py:291
  51.3 1.5 %collective-permute-start.10 = (bf16[384,640]{1,0:T(8,128)(2,1)S(1)}, bf16[384,640]{1,0:T(8,128)(2,1)S(1)}, u32[]{:S(2)}, u32[]{:S(2)}) collective-permute-start(bf16[384,640]{1,0:T(8,128)(2,1)S(1)} %add.17.refs_1_), channel_id=1, source_target_pairs={{4,0},{8,12},{20,16},{24,28},{36,32},{40,44},{52,48},{56,60},{68,6... | collective-permute-start | bytes 1474568 | tf_op jit(solution)/shard_map/ppermute | solution.py:308
  52.9 2.0 %far0_3.3.att0_ref = bf16[384,384]{1,0:T(8,128)(2,1)S(1)} custom-call(s32[1]{0:T(128)} %get-tuple-element.68.valid_ref, bf16[384,768]{1,0:T(8,128)(2,1)S(1)} %copy-done, f32[3,384,384]{2,1,0:T(8,128)S(1)} %far0_3.2.state_ref, bf16[384,896]{1,0:T(8,128)(2,1)S(1)} %collective-permute-done.7.refs_0_.refs_2_, ...), custom_call_target="tpu_custom_call" | custom-call | flops 1 | bytes 1 | tf_op jit(solution)/shard_map/far0_3/pallas_call | solution.py:207
  55.1 2.6 %far3_3.1.att1_ref = bf16[384,384]{1,0:T(8,128)(2,1)S(1)} custom-call(s32[2]{0:T(128)S(1)} %slice.15.valid_ref, bf16[384,768]{1,0:T(8,128)(2,1)S(1)} %copy-done, f32[6,384,384]{2,1,0:T(8,128)S(1)} %far0_6.1.state_ref, bf16[384,896]{1,0:T(8,128)(2,1)S(1)} %collective-permute-done.4.refs_0_, bf16[384,640]{1,0:T(8,128)(2,1)S(1)} %add.17.refs_1_, ...), custom_call_target="tpu_custom_call" | custom-call | flops 1 | bytes 1 | tf_op jit(solution)/shard_map/far3_3/pallas_call | solution.py:207
  58.5 3.3 %collective-permute-start.12 = (bf16[384,768]{1,0:T(8,128)(2,1)S(1)}, bf16[384,768]{1,0:T(8,128)(2,1)S(1)}, u32[]{:S(2)}, u32[]{:S(2)}) collective-permute-start(bf16[384,768]{1,0:T(8,128)(2,1)S(1)} %project1.1), channel_id=1, source_target_pairs={{0,1},{1,0},{2,3},{3,2},{4,5},{5,4},{6,7},{7,6},{8,9},{9,8},{10,11... | collective-permute-start | bytes 1769480 | tf_op jit(solution)/shard_map/ppermute | solution.py:365
  61.8 2.0 %project3.1 = (bf16[384,768]{1,0:T(8,128)(2,1)S(1)}, bf16[384,768]{1,0:T(8,128)(2,1)S(1)}, bf16[384,768]{1,0:T(8,128)(2,1)S(1)}) custom-call(bf16[384,384]{1,0:T(8,128)(2,1)S(1)} %far0_3.3.att0_ref, bf16[384,384]{1,0:T(8,128)(2,1)S(1)} %far3_3.1.att1_ref, bf16[768,768]{1,0:T(8,128)(2,1)S(1)} %get-tuple-element.60.refs_0_, ...), custom_call_target="tpu_custom_call" | custom-call | flops 1 | bytes 1 | tf_op jit(solution)/shard_map/project3/pallas_call | solution.py:352
  63.9 11.8 %collective-permute-done.12 = bf16[384,768]{1,0:T(8,128)(2,1)S(1)} collective-permute-done((bf16[384,768]{1,0:T(8,128)(2,1)S(1)}, bf16[384,768]{1,0:T(8,128)(2,1)S(1)}, u32[]{:S(2)}, u32[]{:S(2)}) %collective-permute-start.12) | collective-permute-done | bytes 589856 | tf_op jit(solution)/shard_map/ppermute | solution.py:365
  75.8 5.5 %collective-permute-start.13 = (bf16[384,768]{1,0:T(8,128)(2,1)S(1)}, bf16[384,768]{1,0:T(8,128)(2,1)S(1)}, u32[]{:S(2)}, u32[]{:S(2)}) collective-permute-start(bf16[384,768]{1,0:T(8,128)(2,1)S(1)} %add_convert_fusion), channel_id=1, source_target_pairs={{0,2},{1,3},{2,0},{3,1},{4,6},{5,7},{6,4},{7,5},{8,10},{9,11},{10,... | collective-permute-start | bytes 1769480 | tf_op jit(solution)/shard_map/ppermute | solution.py:365
  81.4 18.0 %collective-permute-done.11.refs_1_ = bf16[384,768]{1,0:T(8,128)(2,1)S(1)} collective-permute-done((bf16[384,768]{1,0:T(8,128)(2,1)S(1)}, bf16[384,768]{1,0:T(8,128)(2,1)S(1)}, u32[]{:S(2)}, u32[]{:S(2)}) %collective-permute-start.11) | collective-permute-done | bytes 589856 | tf_op jit(solution)/shard_map/ppermute | solution.py:365
  99.3 8.2 %collective-permute-done.13.refs_2_ = bf16[384,768]{1,0:T(8,128)(2,1)S(1)} collective-permute-done((bf16[384,768]{1,0:T(8,128)(2,1)S(1)}, bf16[384,768]{1,0:T(8,128)(2,1)S(1)}, u32[]{:S(2)}, u32[]{:S(2)}) %collective-permute-start.13) | collective-permute-done | bytes 589856 | tf_op jit(solution)/shard_map/ppermute | solution.py:365
  (28 shorter events, 4.6 us)
Async XLA Ops:
  0.0 15.2 %copy-start.1 = (bf16[384,768]{1,0:T(8,128)(2,1)S(1)}, bf16[384,768]{1,0:T(8,128)(2,1)}, u32[]{:S(2)}) copy-start(bf16[384,768]{1,0:T(8,128)(2,1)} %k_ref.3) | copy-start | bytes 1769476
  0.0 15.2 %copy-start = (bf16[384,768]{1,0:T(8,128)(2,1)S(1)}, bf16[384,768]{1,0:T(8,128)(2,1)}, u32[]{:S(2)}) copy-start(bf16[384,768]{1,0:T(8,128)(2,1)} %q_ref.9) | copy-start | bytes 1769476
  0.0 15.1 %collective-permute-start.1 = (bf16[384,768]{1,0:T(8,128)(2,1)}, bf16[384,768]{1,0:T(8,128)(2,1)S(1)}, u32[]{:S(2)}, u32[]{:S(2)}) collective-permute-start(bf16[384,768]{1,0:T(8,128)(2,1)} %k_ref.3), channel_id=1, source_target_pairs={{0,4},{4,0},{8,12},{12,8},{16,20},{20,16},{24,28},{28,24},{32,36},... | collective-permute-start | bytes 1769480 | tf_op jit(solution)/shard_map/ppermute | solution.py:278
  0.0 15.1 %collective-permute-start.2 = (bf16[384,768]{1,0:T(8,128)(2,1)}, bf16[384,768]{1,0:T(8,128)(2,1)S(1)}, u32[]{:S(2)}, u32[]{:S(2)}) collective-permute-start(bf16[384,768]{1,0:T(8,128)(2,1)} %v_ref.3), channel_id=1, source_target_pairs={{0,4},{4,0},{8,12},{12,8},{16,20},{20,16},{24,28},{28,24},{32,36},... | collective-permute-start | bytes 1769480 | tf_op jit(solution)/shard_map/ppermute | solution.py:279
  2.7 17.1 %collective-permute-start = (bf16[384,640]{1,0:T(8,128)(2,1)}, bf16[384,640]{1,0:T(8,128)(2,1)S(1)}, u32[]{:S(2)}, u32[]{:S(2)}) collective-permute-start(bf16[384,640]{1,0:T(8,128)(2,1)} %get-tuple-element.57), channel_id=1, source_target_pairs={{0,8},{4,12},{8,0},{12,4},{16,24},{20,28},{24,16},{28,20},{32,40},... | collective-permute-start | bytes 1474568 | tf_op jit(solution)/shard_map/ppermute | solution.py:281
  4.2 41.8 %collective-permute-start.4 = (bf16[384,896]{1,0:T(8,128)(2,1)}, bf16[384,896]{1,0:T(8,128)(2,1)S(1)}, u32[]{:S(2)}, u32[]{:S(2)}) collective-permute-start(bf16[384,896]{1,0:T(8,128)(2,1)} %get-tuple-element.47), channel_id=1, source_target_pairs={{8,16},{12,20},{16,8},{20,12},{24,32},{28,36},{32,24},{36,28},{40,... | collective-permute-start | bytes 2064392 | tf_op jit(solution)/shard_map/ppermute | solution.py:282
  15.1 22.3 %collective-permute-start.3 = (bf16[384,896]{1,0:T(8,128)(2,1)}, bf16[384,896]{1,0:T(8,128)(2,1)S(1)}, u32[]{:S(2)}, u32[]{:S(2)}) collective-permute-start(bf16[384,896]{1,0:T(8,128)(2,1)} %get-tuple-element.47), channel_id=1, source_target_pairs={{0,8},{4,12},{8,0},{12,4},{16,24},{20,28},{24,16},{28,20},{32,40},... | collective-permute-start | bytes 2064392 | tf_op jit(solution)/shard_map/ppermute | solution.py:286
  15.2 1.1 copy-start.2
  16.3 6.2 %copy-start.3 = (bf16[384,640]{1,0:T(8,128)(2,1)S(1)}, bf16[384,640]{1,0:T(8,128)(2,1)}, u32[]{:S(2)}) copy-start(bf16[384,640]{1,0:T(8,128)(2,1)} %get-tuple-element.57) | copy-start | bytes 1474564
  19.7 27.6 %collective-permute-start.5 = (bf16[384,640]{1,0:T(8,128)(2,1)S(1)}, bf16[384,640]{1,0:T(8,128)(2,1)S(1)}, u32[]{:S(2)}, u32[]{:S(2)}) collective-permute-start(bf16[384,640]{1,0:T(8,128)(2,1)S(1)} %collective-permute-done.refs_1_), channel_id=1, source_target_pairs={{0,4},{12,8},{16,20},{28,24},{32,36},{44,40},{48,52},{60,56},{64,6... | collective-permute-start | bytes 1474568 | tf_op jit(solution)/shard_map/ppermute | solution.py:301
  21.2 30.0 %collective-permute-start.6 = (bf16[384,640]{1,0:T(8,128)(2,1)S(1)}, bf16[384,640]{1,0:T(8,128)(2,1)S(1)}, u32[]{:S(2)}, u32[]{:S(2)}) collective-permute-start(bf16[384,640]{1,0:T(8,128)(2,1)S(1)} %collective-permute-done.refs_1_), channel_id=1, source_target_pairs={{16,32},{20,36},{40,24},{44,28},{48,64},{52,68},{72,56},{76,60},{8... | collective-permute-start | bytes 1474568 | tf_op jit(solution)/shard_map/ppermute | solution.py:291
  22.5 28.7 %collective-permute-start.9 = (bf16[384,640]{1,0:T(8,128)(2,1)S(1)}, bf16[384,640]{1,0:T(8,128)(2,1)S(1)}, u32[]{:S(2)}, u32[]{:S(2)}) collective-permute-start(bf16[384,640]{1,0:T(8,128)(2,1)S(1)} %copy-done.3), channel_id=1, source_target_pairs={{8,16},{12,20},{16,8},{20,12},{40,48},{44,52},{48,40},{52,44},{72,... | collective-permute-start | bytes 1474568 | tf_op jit(solution)/shard_map/ppermute | solution.py:287
  37.4 15.5 %collective-permute-start.7 = (bf16[384,896]{1,0:T(8,128)(2,1)S(1)}, bf16[384,896]{1,0:T(8,128)(2,1)S(1)}, u32[]{:S(2)}, u32[]{:S(2)}) collective-permute-start(bf16[384,896]{1,0:T(8,128)(2,1)S(1)} %collective-permute-done.3.refs_0_), channel_id=1, source_target_pairs={{0,4},{12,8},{16,20},{28,24},{32,36},{44,40},{48,52},{60,56},{64,6... | collective-permute-start | bytes 2064392 | tf_op jit(solution)/shard_map/ppermute | solution.py:302
  46.1 6.8 %collective-permute-start.8 = (bf16[384,896]{1,0:T(8,128)(2,1)S(1)}, bf16[384,896]{1,0:T(8,128)(2,1)S(1)}, u32[]{:S(2)}, u32[]{:S(2)}) collective-permute-start(bf16[384,896]{1,0:T(8,128)(2,1)S(1)} %collective-permute-done.4.refs_0_), channel_id=1, source_target_pairs={{4,0},{8,12},{20,16},{24,28},{36,32},{40,44},{52,48},{56,60},{68,6... | collective-permute-start | bytes 2064392 | tf_op jit(solution)/shard_map/ppermute | solution.py:307
  51.3 3.8 %collective-permute-start.10 = (bf16[384,640]{1,0:T(8,128)(2,1)S(1)}, bf16[384,640]{1,0:T(8,128)(2,1)S(1)}, u32[]{:S(2)}, u32[]{:S(2)}) collective-permute-start(bf16[384,640]{1,0:T(8,128)(2,1)S(1)} %add.17.refs_1_), channel_id=1, source_target_pairs={{4,0},{8,12},{20,16},{24,28},{36,32},{40,44},{52,48},{56,60},{68,6... | collective-permute-start | bytes 1474568 | tf_op jit(solution)/shard_map/ppermute | solution.py:308
  58.5 17.2 %collective-permute-start.12 = (bf16[384,768]{1,0:T(8,128)(2,1)S(1)}, bf16[384,768]{1,0:T(8,128)(2,1)S(1)}, u32[]{:S(2)}, u32[]{:S(2)}) collective-permute-start(bf16[384,768]{1,0:T(8,128)(2,1)S(1)} %project1.1), channel_id=1, source_target_pairs={{0,1},{1,0},{2,3},{3,2},{4,5},{5,4},{6,7},{7,6},{8,9},{9,8},{10,11... | collective-permute-start | bytes 1769480 | tf_op jit(solution)/shard_map/ppermute | solution.py:365
  63.8 35.6 %collective-permute-start.11 = (bf16[384,768]{1,0:T(8,128)(2,1)S(1)}, bf16[384,768]{1,0:T(8,128)(2,1)S(1)}, u32[]{:S(2)}, u32[]{:S(2)}) collective-permute-start(bf16[384,768]{1,0:T(8,128)(2,1)S(1)} %get-tuple-element.64), channel_id=1, source_target_pairs={{0,1},{1,0},{2,3},{3,2},{4,5},{5,4},{6,7},{7,6},{8,9},{9,8},{10,11... | collective-permute-start | bytes 1769480 | tf_op jit(solution)/shard_map/ppermute | solution.py:365
  75.8 31.7 %collective-permute-start.13 = (bf16[384,768]{1,0:T(8,128)(2,1)S(1)}, bf16[384,768]{1,0:T(8,128)(2,1)S(1)}, u32[]{:S(2)}, u32[]{:S(2)}) collective-permute-start(bf16[384,768]{1,0:T(8,128)(2,1)S(1)} %add_convert_fusion), channel_id=1, source_target_pairs={{0,2},{1,3},{2,0},{3,1},{4,6},{5,7},{6,4},{7,5},{8,10},{9,11},{10,... | collective-permute-start | bytes 1769480 | tf_op jit(solution)/shard_map/ppermute | solution.py:365

commit v5 on v4

--- a/solution.py
+++ b/solution.py
@@ -112,32 +112,24 @@
             out_ref[i, :, 2 * HD :] = top
 
 
-def pack_kernel(k_ref, v_ref, direct_ref, relayed_ref, direct_stage, relayed_stage, sems):
+def pack_kernel(k_ref, v_ref, direct_ref, relayed_ref, sems):
     keys, values = KEYS * HD, VALUES * HD
     total = k_ref.shape[1]
-    moves = []
-    for ref, start, wide, out, stage, at in (
-        (k_ref, keys, total - keys, relayed_ref, relayed_stage, 0),
-        (v_ref, values, total - values, relayed_ref, relayed_stage, total - keys),
-        (k_ref, 0, keys, direct_ref, direct_stage, 0),
-        (v_ref, 0, values, direct_ref, direct_stage, keys),
-    ):
-        i, place = len(moves), pl.ds(at, wide)
-        moves.append(
+    copies = [
+        pltpu.make_async_copy(ref.at[:, pl.ds(start, wide)], out.at[:, pl.ds(at, wide)], sems.at[i])
+        for i, (ref, start, wide, out, at) in enumerate(
             (
-                pltpu.make_async_copy(
-                    ref.at[:, pl.ds(start, wide)], stage.at[:, place], sems.at[0, i]
-                ),
-                pltpu.make_async_copy(stage.at[:, place], out.at[:, place], sems.at[1, i]),
+                (k_ref, keys, total - keys, relayed_ref, 0),
+                (v_ref, values, total - values, relayed_ref, total - keys),
+                (k_ref, 0, keys, direct_ref, 0),
+                (v_ref, 0, values, direct_ref, keys),
             )
         )
-    for come, _ in moves:
-        come.start()
-    for come, go in moves:
-        come.wait()
-        go.start()
-    for _, go in moves:
-        go.wait()
+    ]
+    for copy in copies:
+        copy.start()
+    for copy in copies:
+        copy.wait()
 
 
 def columns_kernel(which_ref, w_ref, *refs):
@@ -222,14 +214,13 @@
     return pl.pallas_call(
         pack_kernel,
         out_shape=[jax.ShapeDtypeStruct(shape, k.dtype) for shape in shapes],
-        in_specs=[pl.BlockSpec(memory_space=pl.ANY)] * 2,
-        out_specs=[pl.BlockSpec(memory_space=pl.ANY)] * 2,
-        scratch_shapes=[pltpu.VMEM(shape, k.dtype) for shape in shapes]
-        + [pltpu.SemaphoreType.DMA((2, 4))],
-        compiler_params=pltpu.CompilerParams(vmem_limit_bytes=60 * 2**20),
+        in_specs=[pl.BlockSpec(memory_space=pltpu.HBM)] * 2,
+        out_specs=in_vmem(2),
+        scratch_shapes=[pltpu.SemaphoreType.DMA((4,))],
+        compiler_params=pltpu.CompilerParams(vmem_limit_bytes=8 * 2**20),
         cost_estimate=LIGHT,
         name="pack",
-    )(k, v)
+    )(*[pltpu.with_memory_space_constraint(x, pltpu.HBM) for x in (k, v)])
 
 
 def seq_pairs(step_of, among=lambda s: True):
@@ -327,7 +318,11 @@
         compiler_params=pltpu.CompilerParams(vmem_limit_bytes=limit),
         cost_estimate=LIGHT,
         name=name,
-    )(*[x.astype(jnp.int32) for x in scalars], *in_hbm, *operands)
+    )(
+        *[x.astype(jnp.int32) for x in scalars],
+        *[pltpu.with_memory_space_constraint(x, pltpu.HBM) for x in in_hbm],
+        *operands,
+    )
 
 
 def weight_columns(which, out_weight):
@@ -341,7 +336,7 @@
         scalars=(which,),
         in_hbm=(out_weight,),
         sems=HEAD_PEERS,
-        limit=48 * 2**20,
+        limit=12 * 2**20,
     )
 
 

time: 109 us -> 108 us (level)
    ppermute x1, waiting for transfers between devices: 4.61 us -> 11.9 us  [body(): other0 = lax.ppermute(direct, 'seq', OTHER)]
    ppermute x1, waiting for transfers between devices: 10.4 us -> 3.93 us  [body(): mate0 = lax.ppermute(direct, 'seq', MATE)]
    ppermute x1, waiting for transfers between devices: 1.96 us -> 0.01 us  [body(): passed_other1 = lax.ppermute(mate1, 'seq', ONWARD)]
    pallas_call x1, Pallas kernels: 3.43 us -> 4.65 us  [near_part(): pl.pallas_call(near_kernel, out_shape=jax.ShapeDtypeStruct((heads, rows,...]
  transfers between devices with their start and end apart: 14 -> 14, of which waited for: 7 -> 6; matrix products, arithmetic and copies ran while one was open for 1% -> 1% of each run, Pallas kernels for 16% -> 16%
where the time goes in v5:
time: 108 us
  waiting for transfers between devices  54.7 us (51%)
  starting transfers between devices  28.5 us (26%)
  Pallas kernels  21.9 us (20%)
  local copies, waits for them, and re-layouts  1.74 us (2%)
    ppermute x3, waiting for transfers between devices, sent(): lax.ppermute(value, 'head', [(i, i ^ apart) for i in range(HEAD_PEERS)])  38.5 us
    ppermute x1, waiting for transfers between devices, body(): other0 = lax.ppermute(direct, 'seq', OTHER)  11.9 us
    ppermute x1, starting transfers between devices, body(): other0 = lax.ppermute(direct, 'seq', OTHER)  10.8 us
    pallas_call x4, Pallas kernels, far_part(): pl.pallas_call(functools.partial(far_kernel, list(heads), held_from, coun...  9.25 us
    ppermute x3, starting transfers between devices, sent(): lax.ppermute(value, 'head', [(i, i ^ apart) for i in range(HEAD_PEERS)])  8.01 us
    pallas_call x1, Pallas kernels, near_part(): pl.pallas_call(near_kernel, out_shape=jax.ShapeDtypeStruct((heads, rows,...  4.65 us
    pallas_call x2, Pallas kernels, small_call(): pl.pallas_call(kernel, out_shape=out_shape, in_specs=[pl.BlockSpec(memory...  3.96 us
    ppermute x1, waiting for transfers between devices, body(): mate0 = lax.ppermute(direct, 'seq', MATE)  3.93 us
  transfers between devices with their start and end apart: 14, of which 6 were waited for; matrix products, arithmetic and copies ran while one was open for 1% of the time, Pallas kernels for 16%

profile of v5, /device:TPU:24, one launch (start us, length us, event | category | flops | bytes accessed | tf_op | source)
XLA Modules:
  0.0 107.5 jit_solution(9582944995664903771)
XLA Ops:
  0.5 1.3 %pack.1 = (bf16[384,896]{1,0:T(8,128)(2,1)S(1)}, bf16[384,640]{1,0:T(8,128)(2,1)S(1)}) custom-call(bf16[384,768]{1,0:T(8,128)(2,1)} %k_ref.3, bf16[384,768]{1,0:T(8,128)(2,1)} %v_ref.3), custom_call_target="tpu_custom_call" | custom-call | flops 1 | bytes 1 | tf_op jit(solution)/shard_map/pack/pallas_call | solution.py:214
  1.8 1.6 %collective-permute-start = (bf16[384,640]{1,0:T(8,128)(2,1)S(1)}, bf16[384,640]{1,0:T(8,128)(2,1)S(1)}, u32[]{:S(2)}, u32[]{:S(2)}) collective-permute-start(bf16[384,640]{1,0:T(8,128)(2,1)S(1)} %get-tuple-element.57), channel_id=1, source_target_pairs={{0,8},{4,12},{8,0},{12,4},{16,24},{20,28},{24,16},{28,20},{32,40},... | collective-permute-start | bytes 1474568 | tf_op jit(solution)/shard_map/ppermute | solution.py:272
  3.4 10.8 %collective-permute-start.4 = (bf16[384,896]{1,0:T(8,128)(2,1)S(1)}, bf16[384,896]{1,0:T(8,128)(2,1)S(1)}, u32[]{:S(2)}, u32[]{:S(2)}) collective-permute-start(bf16[384,896]{1,0:T(8,128)(2,1)S(1)} %get-tuple-element.47), channel_id=1, source_target_pairs={{8,16},{12,20},{16,8},{20,12},{24,32},{28,36},{32,24},{36,28},{40,... | collective-permute-start | bytes 2064392 | tf_op jit(solution)/shard_map/ppermute | solution.py:273
  14.4 1.1 copy-done.2
  15.5 4.6 %near.1.state_ref = f32[6,384,384]{2,1,0:T(8,128)S(1)} custom-call(bf16[384,768]{1,0:T(8,128)(2,1)S(1)} %copy-done, bf16[384,768]{1,0:T(8,128)(2,1)S(1)} %copy-done.1, bf16[384,768]{1,0:T(8,128)(2,1)S(1)} %copy-done.2, bf16[384,768]{1,0:T(8,128)(2,1)} %collective-permute-done.1.pk_ref, bf16[384,768]{1,0:T(8,128)(2,1)} %collective-permute-done.2.pv_ref), custom_call_target="tpu_custom_call" | custom-call | flops 40768634880 | bytes 2949120 | tf_op jit(solution)/shard_map/near/pallas_call | solution.py:176
  20.1 1.5 %collective-permute-start.5 = (bf16[384,640]{1,0:T(8,128)(2,1)S(1)}, bf16[384,640]{1,0:T(8,128)(2,1)S(1)}, u32[]{:S(2)}, u32[]{:S(2)}) collective-permute-start(bf16[384,640]{1,0:T(8,128)(2,1)S(1)} %collective-permute-done.refs_1_), channel_id=1, source_target_pairs={{0,4},{12,8},{16,20},{28,24},{32,36},{44,40},{48,52},{60,56},{64,6... | collective-permute-start | bytes 1474568 | tf_op jit(solution)/shard_map/ppermute | solution.py:292
  21.6 1.3 %collective-permute-start.6 = (bf16[384,640]{1,0:T(8,128)(2,1)S(1)}, bf16[384,640]{1,0:T(8,128)(2,1)S(1)}, u32[]{:S(2)}, u32[]{:S(2)}) collective-permute-start(bf16[384,640]{1,0:T(8,128)(2,1)S(1)} %collective-permute-done.refs_1_), channel_id=1, source_target_pairs={{16,32},{20,36},{40,24},{44,28},{48,64},{52,68},{72,56},{76,60},{8... | collective-permute-start | bytes 1474568 | tf_op jit(solution)/shard_map/ppermute | solution.py:282
  24.4 2.9 %columns.1 = (bf16[768,768]{1,0:T(8,128)(2,1)S(1)}, bf16[768,768]{1,0:T(8,128)(2,1)S(1)}, bf16[768,768]{1,0:T(8,128)(2,1)S(1)}, bf16[768,768]{1,0:T(8,128)(2,1)S(1)}) custom-call(s32[4]{0:T(128)S(1)} %pad_add_fusion.which_ref, bf16[768,3072]{1,0:T(8,128)(2,1)} %w_ref), custom_call_target="tpu_custom_call" | custom-call | flops 1 | bytes 1 | tf_op jit(solution)/shard_map/columns/pallas_call | solution.py:310
  27.3 3.9 %collective-permute-done.3.refs_0_ = bf16[384,896]{1,0:T(8,128)(2,1)S(1)} collective-permute-done((bf16[384,896]{1,0:T(8,128)(2,1)S(1)}, bf16[384,896]{1,0:T(8,128)(2,1)S(1)}, u32[]{:S(2)}, u32[]{:S(2)}) %collective-permute-start.3) | collective-permute-done | bytes 688160 | tf_op jit(solution)/shard_map/ppermute | solution.py:277
  31.2 1.3 %collective-permute-start.7 = (bf16[384,896]{1,0:T(8,128)(2,1)S(1)}, bf16[384,896]{1,0:T(8,128)(2,1)S(1)}, u32[]{:S(2)}, u32[]{:S(2)}) collective-permute-start(bf16[384,896]{1,0:T(8,128)(2,1)S(1)} %collective-permute-done.3.refs_0_), channel_id=1, source_target_pairs={{0,4},{12,8},{16,20},{28,24},{32,36},{44,40},{48,52},{60,56},{64,6... | collective-permute-start | bytes 2064392 | tf_op jit(solution)/shard_map/ppermute | solution.py:293
  32.6 2.8 %far0_6.1.state_ref = f32[6,384,384]{2,1,0:T(8,128)S(1)} custom-call(s32[1]{0:T(128)} %get-tuple-element.69.valid_ref, bf16[384,768]{1,0:T(8,128)(2,1)S(1)} %copy-done, f32[6,384,384]{2,1,0:T(8,128)S(1)} %near.1.state_ref, bf16[384,896]{1,0:T(8,128)(2,1)S(1)} %collective-permute-done.3.refs_0_, bf16[384,640]{1,0:T(8,128)(2,1)S(1)} %collective-permute-done.refs_1_), custom_call_target="tpu_custom_call" | custom-call | flops 1 | bytes 1 | tf_op jit(solution)/shard_map/far0_6/pallas_call | solution.py:199
  35.4 11.9 %collective-permute-done.4.refs_0_ = bf16[384,896]{1,0:T(8,128)(2,1)S(1)} collective-permute-done((bf16[384,896]{1,0:T(8,128)(2,1)S(1)}, bf16[384,896]{1,0:T(8,128)(2,1)S(1)}, u32[]{:S(2)}, u32[]{:S(2)}) %collective-permute-start.4) | collective-permute-done | bytes 688160 | tf_op jit(solution)/shard_map/ppermute | solution.py:273
  47.2 1.3 %collective-permute-start.8 = (bf16[384,896]{1,0:T(8,128)(2,1)S(1)}, bf16[384,896]{1,0:T(8,128)(2,1)S(1)}, u32[]{:S(2)}, u32[]{:S(2)}) collective-permute-start(bf16[384,896]{1,0:T(8,128)(2,1)S(1)} %collective-permute-done.4.refs_0_), channel_id=1, source_target_pairs={{4,0},{8,12},{20,16},{24,28},{36,32},{40,44},{52,48},{56,60},{68,6... | collective-permute-start | bytes 2064392 | tf_op jit(solution)/shard_map/ppermute | solution.py:298
  48.5 1.9 %far0_3.2.state_ref = f32[3,384,384]{2,1,0:T(8,128)S(1)} custom-call(s32[1]{0:T(128)} %get-tuple-element.67.valid_ref, bf16[384,768]{1,0:T(8,128)(2,1)S(1)} %copy-done, f32[6,384,384]{2,1,0:T(8,128)S(1)} %far0_6.1.state_ref, bf16[384,896]{1,0:T(8,128)(2,1)S(1)} %collective-permute-done.4.refs_0_), custom_call_target="tpu_custom_call" | custom-call | flops 1 | bytes 1 | tf_op jit(solution)/shard_map/far0_3/pallas_call | solution.py:199
  50.6 1.5 %collective-permute-start.10 = (bf16[384,640]{1,0:T(8,128)(2,1)S(1)}, bf16[384,640]{1,0:T(8,128)(2,1)S(1)}, u32[]{:S(2)}, u32[]{:S(2)}) collective-permute-start(bf16[384,640]{1,0:T(8,128)(2,1)S(1)} %add.17.refs_1_), channel_id=1, source_target_pairs={{4,0},{8,12},{20,16},{24,28},{36,32},{40,44},{52,48},{56,60},{68,6... | collective-permute-start | bytes 1474568 | tf_op jit(solution)/shard_map/ppermute | solution.py:299
  52.2 1.9 %far0_3.3.att0_ref = bf16[384,384]{1,0:T(8,128)(2,1)S(1)} custom-call(s32[1]{0:T(128)} %get-tuple-element.68.valid_ref, bf16[384,768]{1,0:T(8,128)(2,1)S(1)} %copy-done, f32[3,384,384]{2,1,0:T(8,128)S(1)} %far0_3.2.state_ref, bf16[384,896]{1,0:T(8,128)(2,1)S(1)} %collective-permute-done.7.refs_0_.refs_2_, ...), custom_call_target="tpu_custom_call" | custom-call | flops 1 | bytes 1 | tf_op jit(solution)/shard_map/far0_3/pallas_call | solution.py:199
  54.4 2.7 %far3_3.1.att1_ref = bf16[384,384]{1,0:T(8,128)(2,1)S(1)} custom-call(s32[2]{0:T(128)S(1)} %slice.15.valid_ref, bf16[384,768]{1,0:T(8,128)(2,1)S(1)} %copy-done, f32[6,384,384]{2,1,0:T(8,128)S(1)} %far0_6.1.state_ref, bf16[384,896]{1,0:T(8,128)(2,1)S(1)} %collective-permute-done.4.refs_0_, bf16[384,640]{1,0:T(8,128)(2,1)S(1)} %add.17.refs_1_, ...), custom_call_target="tpu_custom_call" | custom-call | flops 1 | bytes 1 | tf_op jit(solution)/shard_map/far3_3/pallas_call | solution.py:199
  57.9 5.1 %collective-permute-start.12 = (bf16[384,768]{1,0:T(8,128)(2,1)S(1)}, bf16[384,768]{1,0:T(8,128)(2,1)S(1)}, u32[]{:S(2)}, u32[]{:S(2)}) collective-permute-start(bf16[384,768]{1,0:T(8,128)(2,1)S(1)} %project1.1), channel_id=1, source_target_pairs={{0,1},{1,0},{2,3},{3,2},{4,5},{5,4},{6,7},{7,6},{8,9},{9,8},{10,11... | collective-permute-start | bytes 1769480 | tf_op jit(solution)/shard_map/ppermute | solution.py:360
  63.0 2.0 %project3.1 = (bf16[384,768]{1,0:T(8,128)(2,1)S(1)}, bf16[384,768]{1,0:T(8,128)(2,1)S(1)}, bf16[384,768]{1,0:T(8,128)(2,1)S(1)}) custom-call(bf16[384,384]{1,0:T(8,128)(2,1)S(1)} %far0_3.3.att0_ref, bf16[384,384]{1,0:T(8,128)(2,1)S(1)} %far3_3.1.att1_ref, bf16[768,768]{1,0:T(8,128)(2,1)S(1)} %get-tuple-element.60.refs_0_, ...), custom_call_target="tpu_custom_call" | custom-call | flops 1 | bytes 1 | tf_op jit(solution)/shard_map/project3/pallas_call | solution.py:347
  65.1 11.9 %collective-permute-done.12 = bf16[384,768]{1,0:T(8,128)(2,1)S(1)} collective-permute-done((bf16[384,768]{1,0:T(8,128)(2,1)S(1)}, bf16[384,768]{1,0:T(8,128)(2,1)S(1)}, u32[]{:S(2)}, u32[]{:S(2)}) %collective-permute-start.12) | collective-permute-done | bytes 589856 | tf_op jit(solution)/shard_map/ppermute | solution.py:360
  77.2 2.8 %collective-permute-start.13 = (bf16[384,768]{1,0:T(8,128)(2,1)S(1)}, bf16[384,768]{1,0:T(8,128)(2,1)S(1)}, u32[]{:S(2)}, u32[]{:S(2)}) collective-permute-start(bf16[384,768]{1,0:T(8,128)(2,1)S(1)} %add_convert_fusion), channel_id=1, source_target_pairs={{0,2},{1,3},{2,0},{3,1},{4,6},{5,7},{6,4},{7,5},{8,10},{9,11},{10,... | collective-permute-start | bytes 1769480 | tf_op jit(solution)/shard_map/ppermute | solution.py:360
  80.0 20.2 %collective-permute-done.11.refs_1_ = bf16[384,768]{1,0:T(8,128)(2,1)S(1)} collective-permute-done((bf16[384,768]{1,0:T(8,128)(2,1)S(1)}, bf16[384,768]{1,0:T(8,128)(2,1)S(1)}, u32[]{:S(2)}, u32[]{:S(2)}) %collective-permute-start.11) | collective-permute-done | bytes 589856 | tf_op jit(solution)/shard_map/ppermute | solution.py:360
  100.2 6.3 %collective-permute-done.13.refs_2_ = bf16[384,768]{1,0:T(8,128)(2,1)S(1)} collective-permute-done((bf16[384,768]{1,0:T(8,128)(2,1)S(1)}, bf16[384,768]{1,0:T(8,128)(2,1)S(1)}, u32[]{:S(2)}, u32[]{:S(2)}) %collective-permute-start.13) | collective-permute-done | bytes 589856 | tf_op jit(solution)/shard_map/ppermute | solution.py:360
  106.5 1.0 last_sum.1
  (26 shorter events, 3.7 us)
Async XLA Ops:
  0.0 14.4 %copy-start.1 = (bf16[384,768]{1,0:T(8,128)(2,1)S(1)}, bf16[384,768]{1,0:T(8,128)(2,1)}, u32[]{:S(2)}) copy-start(bf16[384,768]{1,0:T(8,128)(2,1)} %k_ref.3) | copy-start | bytes 1769476
  0.0 14.4 %copy-start = (bf16[384,768]{1,0:T(8,128)(2,1)S(1)}, bf16[384,768]{1,0:T(8,128)(2,1)}, u32[]{:S(2)}) copy-start(bf16[384,768]{1,0:T(8,128)(2,1)} %q_ref.9) | copy-start | bytes 1769476
  0.0 14.3 %collective-permute-start.1 = (bf16[384,768]{1,0:T(8,128)(2,1)}, bf16[384,768]{1,0:T(8,128)(2,1)}, u32[]{:S(2)}, u32[]{:S(2)}) collective-permute-start(bf16[384,768]{1,0:T(8,128)(2,1)} %k_ref.3), channel_id=1, source_target_pairs={{0,4},{4,0},{8,12},{12,8},{16,20},{20,16},{24,28},{28,24},{32,36},... | collective-permute-start | bytes 1769480 | tf_op jit(solution)/shard_map/ppermute | solution.py:269
  0.0 14.3 %collective-permute-start.2 = (bf16[384,768]{1,0:T(8,128)(2,1)}, bf16[384,768]{1,0:T(8,128)(2,1)}, u32[]{:S(2)}, u32[]{:S(2)}) collective-permute-start(bf16[384,768]{1,0:T(8,128)(2,1)} %v_ref.3), channel_id=1, source_target_pairs={{0,4},{4,0},{8,12},{12,8},{16,20},{20,16},{24,28},{28,24},{32,36},... | collective-permute-start | bytes 1769480 | tf_op jit(solution)/shard_map/ppermute | solution.py:270
  1.8 18.3 %collective-permute-start = (bf16[384,640]{1,0:T(8,128)(2,1)S(1)}, bf16[384,640]{1,0:T(8,128)(2,1)S(1)}, u32[]{:S(2)}, u32[]{:S(2)}) collective-permute-start(bf16[384,640]{1,0:T(8,128)(2,1)S(1)} %get-tuple-element.57), channel_id=1, source_target_pairs={{0,8},{4,12},{8,0},{12,4},{16,24},{20,28},{24,16},{28,20},{32,40},... | collective-permute-start | bytes 1474568 | tf_op jit(solution)/shard_map/ppermute | solution.py:272
  3.4 43.8 %collective-permute-start.4 = (bf16[384,896]{1,0:T(8,128)(2,1)S(1)}, bf16[384,896]{1,0:T(8,128)(2,1)S(1)}, u32[]{:S(2)}, u32[]{:S(2)}) collective-permute-start(bf16[384,896]{1,0:T(8,128)(2,1)S(1)} %get-tuple-element.47), channel_id=1, source_target_pairs={{8,16},{12,20},{16,8},{20,12},{24,32},{28,36},{32,24},{36,28},{40,... | collective-permute-start | bytes 2064392 | tf_op jit(solution)/shard_map/ppermute | solution.py:273
  14.3 17.0 %collective-permute-start.3 = (bf16[384,896]{1,0:T(8,128)(2,1)S(1)}, bf16[384,896]{1,0:T(8,128)(2,1)S(1)}, u32[]{:S(2)}, u32[]{:S(2)}) collective-permute-start(bf16[384,896]{1,0:T(8,128)(2,1)S(1)} %get-tuple-element.47), channel_id=1, source_target_pairs={{0,8},{4,12},{8,0},{12,4},{16,24},{20,28},{24,16},{28,20},{32,40},... | collective-permute-start | bytes 2064392 | tf_op jit(solution)/shard_map/ppermute | solution.py:277
  14.4 1.1 copy-start.2
  20.1 28.4 %collective-permute-start.5 = (bf16[384,640]{1,0:T(8,128)(2,1)S(1)}, bf16[384,640]{1,0:T(8,128)(2,1)S(1)}, u32[]{:S(2)}, u32[]{:S(2)}) collective-permute-start(bf16[384,640]{1,0:T(8,128)(2,1)S(1)} %collective-permute-done.refs_1_), channel_id=1, source_target_pairs={{0,4},{12,8},{16,20},{28,24},{32,36},{44,40},{48,52},{60,56},{64,6... | collective-permute-start | bytes 1474568 | tf_op jit(solution)/shard_map/ppermute | solution.py:292
  21.6 28.8 %collective-permute-start.6 = (bf16[384,640]{1,0:T(8,128)(2,1)S(1)}, bf16[384,640]{1,0:T(8,128)(2,1)S(1)}, u32[]{:S(2)}, u32[]{:S(2)}) collective-permute-start(bf16[384,640]{1,0:T(8,128)(2,1)S(1)} %collective-permute-done.refs_1_), channel_id=1, source_target_pairs={{16,32},{20,36},{40,24},{44,28},{48,64},{52,68},{72,56},{76,60},{8... | collective-permute-start | bytes 1474568 | tf_op jit(solution)/shard_map/ppermute | solution.py:282
  22.9 27.5 %collective-permute-start.9 = (bf16[384,640]{1,0:T(8,128)(2,1)S(1)}, bf16[384,640]{1,0:T(8,128)(2,1)S(1)}, u32[]{:S(2)}, u32[]{:S(2)}) collective-permute-start(bf16[384,640]{1,0:T(8,128)(2,1)S(1)} %get-tuple-element.57), channel_id=1, source_target_pairs={{8,16},{12,20},{16,8},{20,12},{40,48},{44,52},{48,40},{52,44},{72,... | collective-permute-start | bytes 1474568 | tf_op jit(solution)/shard_map/ppermute | solution.py:278
  31.2 20.9 %collective-permute-start.7 = (bf16[384,896]{1,0:T(8,128)(2,1)S(1)}, bf16[384,896]{1,0:T(8,128)(2,1)S(1)}, u32[]{:S(2)}, u32[]{:S(2)}) collective-permute-start(bf16[384,896]{1,0:T(8,128)(2,1)S(1)} %collective-permute-done.3.refs_0_), channel_id=1, source_target_pairs={{0,4},{12,8},{16,20},{28,24},{32,36},{44,40},{48,52},{60,56},{64,6... | collective-permute-start | bytes 2064392 | tf_op jit(solution)/shard_map/ppermute | solution.py:293
  47.2 4.9 %collective-permute-start.8 = (bf16[384,896]{1,0:T(8,128)(2,1)S(1)}, bf16[384,896]{1,0:T(8,128)(2,1)S(1)}, u32[]{:S(2)}, u32[]{:S(2)}) collective-permute-start(bf16[384,896]{1,0:T(8,128)(2,1)S(1)} %collective-permute-done.4.refs_0_), channel_id=1, source_target_pairs={{4,0},{8,12},{20,16},{24,28},{36,32},{40,44},{52,48},{56,60},{68,6... | collective-permute-start | bytes 2064392 | tf_op jit(solution)/shard_map/ppermute | solution.py:298
  50.6 3.8 %collective-permute-start.10 = (bf16[384,640]{1,0:T(8,128)(2,1)S(1)}, bf16[384,640]{1,0:T(8,128)(2,1)S(1)}, u32[]{:S(2)}, u32[]{:S(2)}) collective-permute-start(bf16[384,640]{1,0:T(8,128)(2,1)S(1)} %add.17.refs_1_), channel_id=1, source_target_pairs={{4,0},{8,12},{20,16},{24,28},{36,32},{40,44},{52,48},{56,60},{68,6... | collective-permute-start | bytes 1474568 | tf_op jit(solution)/shard_map/ppermute | solution.py:299
  57.9 19.2 %collective-permute-start.12 = (bf16[384,768]{1,0:T(8,128)(2,1)S(1)}, bf16[384,768]{1,0:T(8,128)(2,1)S(1)}, u32[]{:S(2)}, u32[]{:S(2)}) collective-permute-start(bf16[384,768]{1,0:T(8,128)(2,1)S(1)} %project1.1), channel_id=1, source_target_pairs={{0,1},{1,0},{2,3},{3,2},{4,5},{5,4},{6,7},{7,6},{8,9},{9,8},{10,11... | collective-permute-start | bytes 1769480 | tf_op jit(solution)/shard_map/ppermute | solution.py:360
  65.0 35.2 %collective-permute-start.11 = (bf16[384,768]{1,0:T(8,128)(2,1)S(1)}, bf16[384,768]{1,0:T(8,128)(2,1)S(1)}, u32[]{:S(2)}, u32[]{:S(2)}) collective-permute-start(bf16[384,768]{1,0:T(8,128)(2,1)S(1)} %get-tuple-element.64), channel_id=1, source_target_pairs={{0,1},{1,0},{2,3},{3,2},{4,5},{5,4},{6,7},{7,6},{8,9},{9,8},{10,11... | collective-permute-start | bytes 1769480 | tf_op jit(solution)/shard_map/ppermute | solution.py:360
  77.2 29.3 %collective-permute-start.13 = (bf16[384,768]{1,0:T(8,128)(2,1)S(1)}, bf16[384,768]{1,0:T(8,128)(2,1)S(1)}, u32[]{:S(2)}, u32[]{:S(2)}) collective-permute-start(bf16[384,768]{1,0:T(8,128)(2,1)S(1)} %add_convert_fusion), channel_id=1, source_target_pairs={{0,2},{1,3},{2,0},{3,1},{4,6},{5,7},{6,4},{7,5},{8,10},{9,11},{10,... | collective-permute-start | bytes 1769480 | tf_op jit(solution)/shard_map/ppermute | solution.py:360

commit v6 on v5

--- a/solution.py
+++ b/solution.py
@@ -112,6 +112,16 @@
             out_ref[i, :, 2 * HD :] = top
 
 
+def last_kernel(heads, counts, valid_ref, q_ref, state_ref, *refs):
+    *arrays, att_ref, w_ref, out_ref, term_ref = refs
+    far_kernel(heads, 0, counts, True, valid_ref, q_ref, state_ref, *arrays, out_ref)
+    cut = att_ref.shape[1]
+    term_ref[...] = (
+        jnp.dot(att_ref[...], w_ref[:cut, :], preferred_element_type=jnp.float32)
+        + jnp.dot(out_ref[...], w_ref[cut:, :], preferred_element_type=jnp.float32)
+    ).astype(term_ref.dtype)
+
+
 def pack_kernel(k_ref, v_ref, direct_ref, relayed_ref, sems):
     keys, values = KEYS * HD, VALUES * HD
     total = k_ref.shape[1]
@@ -147,18 +157,12 @@
 
 def project_kernel(att0_ref, att1_ref, *refs):
     half = len(refs) // 2
-    weights, outs = (refs[:1], refs[1:]) if len(refs) == 3 else (refs[:half], refs[half:])
     cut = att0_ref.shape[1]
-    each = len(outs) // len(weights)
-    for i, w_ref in enumerate(weights):
-        for j in range(each):
-            out_ref = outs[i * each + j]
-            rows = out_ref.shape[0]
-            at = slice(j * rows, (j + 1) * rows)
-            out_ref[...] = (
-                jnp.dot(att0_ref[at, :], w_ref[:cut, :], preferred_element_type=jnp.float32)
-                + jnp.dot(att1_ref[at, :], w_ref[cut:, :], preferred_element_type=jnp.float32)
-            ).astype(out_ref.dtype)
+    for w_ref, out_ref in zip(refs[:half], refs[half:]):
+        out_ref[...] = (
+            jnp.dot(att0_ref[...], w_ref[:cut, :], preferred_element_type=jnp.float32)
+            + jnp.dot(att1_ref[...], w_ref[cut:, :], preferred_element_type=jnp.float32)
+        ).astype(out_ref.dtype)
 
 
 def last_sum_kernel(*refs):
@@ -205,6 +209,24 @@
         cost_estimate=LIGHT,
         name=f"far{heads[0]}_{len(heads)}",
     )(valid, q, state, *arrays)
+
+
+def last_part(heads, valid, q, state, blocks, att, weight):
+    rows = q.shape[0]
+    arrays = [array for block in blocks for part in block for array in part]
+    counts = [(len(direct), len(relayed)) for direct, relayed in blocks]
+    return pl.pallas_call(
+        functools.partial(last_kernel, list(heads), counts),
+        out_shape=[
+            jax.ShapeDtypeStruct((rows, len(heads) * HD), jnp.bfloat16),
+            jax.ShapeDtypeStruct((rows, weight.shape[1]), jnp.bfloat16),
+        ],
+        in_specs=[pl.BlockSpec(memory_space=pltpu.SMEM)] + in_vmem(4 + len(arrays)),
+        out_specs=in_vmem(2),
+        compiler_params=pltpu.CompilerParams(vmem_limit_bytes=8 * 2**20),
+        cost_estimate=LIGHT,
+        name="last",
+    )(valid, q, state, *arrays, att, weight)
 
 
 def packed(k, v):
@@ -289,21 +311,20 @@
     state, mate0 = lax.optimization_barrier((state, mate0))
     state = far_part(heads, 0, False, valid[:1], queries, state, [[[mate0], [mate1]]])
     state, other0 = lax.optimization_barrier((state, other0))
-    mate_shared1 = lax.ppermute(mate1, "seq", MATE_SHARED)
     mate_shared0 = lax.ppermute(mate0, "seq", MATE_SHARED)
-    state, mate_shared1 = lax.optimization_barrier((state, mate_shared1))
     state0 = far_part(soon, 0, False, valid[1:2], queries, state, [[[other0], []]])
     passed_other1, state0 = lax.optimization_barrier((passed_other1, state0))
     other1 = row_other1 + passed_other1
+    to_swap = jnp.where(place % 2 == chip % 2, mate1, other1)
     other_shared0 = lax.ppermute(other0, "seq", OTHER_SHARED)
-    other_shared1 = lax.ppermute(other1, "seq", OTHER_SHARED)
-    third0, third1 = [mate_shared0, other_shared0], [mate_shared1, other_shared1]
+    swapped1 = lax.ppermute(to_swap, "seq", PAIR)
+    third0, third1 = [mate_shared0, other_shared0], [swapped1]
     att0 = far_part(soon, 0, True, valid[2:], queries, state0, [[third0, []]])
     state, att0 = lax.optimization_barrier((state, att0))
-    att1 = far_part(
-        later, 0, True, valid[1:], queries, state, [[[other0], [other1]], [third0, third1]]
-    )
-    return projected(att0, att1, weights)
+    att1, distant = last_part(
+        later, valid[1:], queries, state, [[[other0], [other1]], [third0, third1]], att0, weights[0]
+    )
+    return projected(att0, att1, distant, weights[1:])
 
 
 def small_call(kernel, name, out_shape, operands, scalars=(), in_hbm=(), sems=0, limit=8 * 2**20):
@@ -340,28 +361,25 @@
     )
 
 
-def projection(att0, att1, weights, pieces):
-    rows = att0.shape[0]
-    depth, cols = weights[0].shape
-    count = len(weights)
+def projection(att0, att1, weights):
+    rows, cols, count = att0.shape[0], weights[0].shape[1], len(weights)
     return pl.pallas_call(
         project_kernel,
-        out_shape=[jax.ShapeDtypeStruct((rows // pieces, cols), jnp.bfloat16)] * (count * pieces),
+        out_shape=[jax.ShapeDtypeStruct((rows, cols), jnp.bfloat16)] * count,
         in_specs=in_vmem(2 + count),
-        out_specs=in_vmem(count * pieces),
-        compiler_params=pltpu.CompilerParams(vmem_limit_bytes=8 * 2**20),
-        cost_estimate=LIGHT,
-        name=f"project{count}",
+        out_specs=in_vmem(count),
+        compiler_params=pltpu.CompilerParams(vmem_limit_bytes=8 * 2**20),
+        cost_estimate=LIGHT,
+        name="project",
     )(att0, att1, *weights)
 
 
-def projected(att0, att1, weights):
+def projected(att0, att1, distant, weights):
     def sent(value, apart):
         return lax.ppermute(value, "head", [(i, i ^ apart) for i in range(HEAD_PEERS)])
 
-    (distant,) = projection(att0, att1, weights[:1], 1)
     distant_in = sent(distant, 1)
-    beside, across, own = projection(att0, att1, weights[1:], 1)
+    beside, across, own = projection(att0, att1, weights)
     beside_in = sent(beside, 1)
     across = (across.astype(jnp.float32) + distant_in.astype(jnp.float32)).astype(jnp.bfloat16)
     across_in = sent(across, 2)

time: 108 us -> 107 us (level)
  starting transfers between devices: 28.5 us -> 24.2 us
  local copies, waits for them, and re-layouts: 1.74 us -> 3.57 us
  other arithmetic: 0.42 us -> 1.56 us
    ppermute x3, starting transfers between devices: 8.01 us -> 4.46 us  [sent(): lax.ppermute(value, 'head', [(i, i ^ apart) for i in range(HEAD_PEERS)])]
    ppermute x1, waiting for transfers between devices: 3.93 us -> 7.06 us  [body(): mate0 = lax.ppermute(direct, 'seq', MATE)]
    pallas_call x4 -> x3, Pallas kernels: 9.25 us -> 6.58 us  [far_part(): pl.pallas_call(functools.partial(far_kernel, list(heads), held_from, coun...]
    pallas_call x2, Pallas kernels: 2.78 us -> 5.38 us  [the longest x1 3.38 us: last_part(): pl.pallas_call(functools.partial(last_kernel, list(heads), counts), out_s...]
    unnamed x6 -> x10, local copies, waits for them, and re-layouts: 1.07 us -> 2.82 us
    ppermute x2 -> x1, starting transfers between devices: 2.95 us -> 1.43 us  [body(): swapped1 = lax.ppermute(to_swap, 'seq', PAIR)]
    select_n x0 -> x1, other arithmetic: none -> 1.27 us  [body(): to_swap = jnp.where(place % 2 == chip % 2, mate1, other1)]
    pallas_call x1, Pallas kernels: 4.65 us -> 3.4 us  [near_part(): pl.pallas_call(near_kernel, out_shape=jax.ShapeDtypeStruct((heads, rows,...]
  transfers between devices with their start and end apart: 14 -> 13, of which waited for: 6 -> 5; matrix products, arithmetic and copies ran while one was open for 1% -> 2% of each run, Pallas kernels for 16% -> 16%
where the time goes in v6:
time: 107 us
  waiting for transfers between devices  55.7 us (52%)
  starting transfers between devices  24.2 us (23%)
  Pallas kernels  21.7 us (20%)
  local copies, waits for them, and re-layouts  3.57 us (3%)
  other arithmetic  1.56 us (1%)
    ppermute x3, waiting for transfers between devices, sent(): lax.ppermute(value, 'head', [(i, i ^ apart) for i in range(HEAD_PEERS)])  37.6 us
    ppermute x1, waiting for transfers between devices, body(): other0 = lax.ppermute(direct, 'seq', OTHER)  11 us
    ppermute x1, starting transfers between devices, body(): other0 = lax.ppermute(direct, 'seq', OTHER)  10.8 us
    ppermute x1, waiting for transfers between devices, body(): mate0 = lax.ppermute(direct, 'seq', MATE)  7.06 us
    pallas_call x3, Pallas kernels, far_part(): pl.pallas_call(functools.partial(far_kernel, list(heads), held_from, coun...  6.58 us
    ppermute x3, starting transfers between devices, sent(): lax.ppermute(value, 'head', [(i, i ^ apart) for i in range(HEAD_PEERS)])  4.46 us
    pallas_call x2, Pallas kernels, small_call(): pl.pallas_call(kernel, out_shape=out_shape, in_specs=[pl.BlockSpec(memory...  4.23 us
    pallas_call x1, Pallas kernels, near_part(): pl.pallas_call(near_kernel, out_shape=jax.ShapeDtypeStruct((heads, rows,...  3.4 us
  transfers between devices with their start and end apart: 13, of which 5 were waited for; matrix products, arithmetic and copies ran while one was open for 2% of the time, Pallas kernels for 16%

profile of v6, /device:TPU:24, one launch (start us, length us, event | category | flops | bytes accessed | tf_op | source)
XLA Modules:
  0.0 106.9 jit_solution(3687927588663902327)
XLA Ops:
  0.5 2.1 %pack.1 = (bf16[384,896]{1,0:T(8,128)(2,1)S(1)}, bf16[384,640]{1,0:T(8,128)(2,1)}) custom-call(bf16[384,768]{1,0:T(8,128)(2,1)} %k_ref.3, bf16[384,768]{1,0:T(8,128)(2,1)} %v_ref.3), custom_call_target="tpu_custom_call" | custom-call | flops 1 | bytes 1 | tf_op jit(solution)/shard_map/pack/pallas_call | solution.py:236
  2.6 1.6 %collective-permute-start = (bf16[384,640]{1,0:T(8,128)(2,1)}, bf16[384,640]{1,0:T(8,128)(2,1)S(1)}, u32[]{:S(2)}, u32[]{:S(2)}) collective-permute-start(bf16[384,640]{1,0:T(8,128)(2,1)} %get-tuple-element.56), channel_id=1, source_target_pairs={{0,8},{4,12},{8,0},{12,4},{16,24},{20,28},{24,16},{28,20},{32,40},... | collective-permute-start | bytes 1474568 | tf_op jit(solution)/shard_map/ppermute | solution.py:294
  4.2 10.8 %collective-permute-start.4 = (bf16[384,896]{1,0:T(8,128)(2,1)S(1)}, bf16[384,896]{1,0:T(8,128)(2,1)S(1)}, u32[]{:S(2)}, u32[]{:S(2)}) collective-permute-start(bf16[384,896]{1,0:T(8,128)(2,1)S(1)} %get-tuple-element.47), channel_id=1, source_target_pairs={{8,16},{12,20},{16,8},{20,12},{24,32},{28,36},{32,24},{36,28},{40,... | collective-permute-start | bytes 2064392 | tf_op jit(solution)/shard_map/ppermute | solution.py:295
  16.2 3.4 %near.1.state_ref = f32[6,384,384]{2,1,0:T(8,128)S(1)} custom-call(bf16[384,768]{1,0:T(8,128)(2,1)S(1)} %copy-done, bf16[384,768]{1,0:T(8,128)(2,1)S(1)} %copy-done.3, bf16[384,768]{1,0:T(8,128)(2,1)S(1)} %copy-done.4, bf16[384,768]{1,0:T(8,128)(2,1)S(1)} %collective-permute-done.1.pk_ref, bf16[384,768]{1,0:T(8,128)(2,1)S(1)} %collective-permute-done.2.pv_ref), custom_call_target="tpu_custom_call" | custom-call | flops 40768634880 | bytes 2949120 | tf_op jit(solution)/shard_map/near/pallas_call | solution.py:180
  19.6 1.8 %copy-done.1 = f32[6,384,384]{2,1,0:T(8,128)} copy-done((f32[6,384,384]{2,1,0:T(8,128)}, f32[6,384,384]{2,1,0:T(8,128)S(1)}, u32[]{:S(2)}) %copy-start.1) | copy-done | bytes 3538968
  21.4 1.3 %collective-permute-start.5 = (bf16[384,640]{1,0:T(8,128)(2,1)S(1)}, bf16[384,640]{1,0:T(8,128)(2,1)}, u32[]{:S(2)}, u32[]{:S(2)}) collective-permute-start(bf16[384,640]{1,0:T(8,128)(2,1)S(1)} %collective-permute-done.refs_1_), channel_id=1, source_target_pairs={{16,32},{20,36},{40,24},{44,28},{48,64},{52,68},{72,56},{76,60},{8... | collective-permute-start | bytes 1474568 | tf_op jit(solution)/shard_map/ppermute | solution.py:304
  22.7 1.4 %collective-permute-start.8 = (bf16[384,640]{1,0:T(8,128)(2,1)}, bf16[384,640]{1,0:T(8,128)(2,1)}, u32[]{:S(2)}, u32[]{:S(2)}) collective-permute-start(bf16[384,640]{1,0:T(8,128)(2,1)} %get-tuple-element.56), channel_id=1, source_target_pairs={{8,16},{12,20},{16,8},{20,12},{40,48},{44,52},{48,40},{52,44},{72,... | collective-permute-start | bytes 1474568 | tf_op jit(solution)/shard_map/ppermute | solution.py:300
  24.9 3.2 %columns.1 = (bf16[768,768]{1,0:T(8,128)(2,1)S(1)}, bf16[768,768]{1,0:T(8,128)(2,1)S(1)}, bf16[768,768]{1,0:T(8,128)(2,1)S(1)}, bf16[768,768]{1,0:T(8,128)(2,1)S(1)}) custom-call(s32[4]{0:T(128)S(1)} %pad_add_fusion.which_ref, bf16[768,3072]{1,0:T(8,128)(2,1)} %w_ref), custom_call_target="tpu_custom_call" | custom-call | flops 1 | bytes 1 | tf_op jit(solution)/shard_map/columns/pallas_call | solution.py:331
  28.1 7.1 %collective-permute-done.3.refs_0_ = bf16[384,896]{1,0:T(8,128)(2,1)S(1)} collective-permute-done((bf16[384,896]{1,0:T(8,128)(2,1)S(1)}, bf16[384,896]{1,0:T(8,128)(2,1)S(1)}, u32[]{:S(2)}, u32[]{:S(2)}) %collective-permute-start.3) | collective-permute-done | bytes 688160 | tf_op jit(solution)/shard_map/ppermute | solution.py:299
  35.2 1.3 %collective-permute-start.6 = (bf16[384,896]{1,0:T(8,128)(2,1)S(1)}, bf16[384,896]{1,0:T(8,128)(2,1)S(1)}, u32[]{:S(2)}, u32[]{:S(2)}) collective-permute-start(bf16[384,896]{1,0:T(8,128)(2,1)S(1)} %collective-permute-done.3.refs_0_), channel_id=1, source_target_pairs={{0,4},{12,8},{16,20},{28,24},{32,36},{44,40},{48,52},{60,56},{64,6... | collective-permute-start | bytes 2064392 | tf_op jit(solution)/shard_map/ppermute | solution.py:314
  36.5 2.8 %far0_6.1.state_ref = f32[6,384,384]{2,1,0:T(8,128)S(1)} custom-call(s32[1]{0:T(128)} %get-tuple-element.71.valid_ref, bf16[384,768]{1,0:T(8,128)(2,1)S(1)} %copy-done, f32[6,384,384]{2,1,0:T(8,128)S(1)} %copy-done.2, bf16[384,896]{1,0:T(8,128)(2,1)S(1)} %collective-permute-done.3.refs_0_, bf16[384,640]{1,0:T(8,128)(2,1)S(1)} %collective-permute-done.refs_1_), custom_call_target="tpu_custom_call" | custom-call | flops 1 | bytes 1 | tf_op jit(solution)/shard_map/far0_6/pallas_call | solution.py:203
  39.4 11.0 %collective-permute-done.4.refs_0_ = bf16[384,896]{1,0:T(8,128)(2,1)S(1)} collective-permute-done((bf16[384,896]{1,0:T(8,128)(2,1)S(1)}, bf16[384,896]{1,0:T(8,128)(2,1)S(1)}, u32[]{:S(2)}, u32[]{:S(2)}) %collective-permute-start.4) | collective-permute-done | bytes 688160 | tf_op jit(solution)/shard_map/ppermute | solution.py:295
  50.4 1.3 %collective-permute-start.7 = (bf16[384,896]{1,0:T(8,128)(2,1)S(1)}, bf16[384,896]{1,0:T(8,128)(2,1)S(1)}, u32[]{:S(2)}, u32[]{:S(2)}) collective-permute-start(bf16[384,896]{1,0:T(8,128)(2,1)S(1)} %collective-permute-done.4.refs_0_), channel_id=1, source_target_pairs={{4,0},{8,12},{20,16},{24,28},{36,32},{40,44},{52,48},{56,60},{68,6... | collective-permute-start | bytes 2064392 | tf_op jit(solution)/shard_map/ppermute | solution.py:319
  51.7 1.9 %far0_3.2.state_ref = f32[3,384,384]{2,1,0:T(8,128)S(1)} custom-call(s32[1]{0:T(128)} %get-tuple-element.69.valid_ref, bf16[384,768]{1,0:T(8,128)(2,1)S(1)} %copy-done, f32[6,384,384]{2,1,0:T(8,128)S(1)} %far0_6.1.state_ref, bf16[384,896]{1,0:T(8,128)(2,1)S(1)} %collective-permute-done.4.refs_0_), custom_call_target="tpu_custom_call" | custom-call | flops 1 | bytes 1 | tf_op jit(solution)/shard_map/far0_3/pallas_call | solution.py:203
  53.6 1.3 %broadcast_select_fusion = (bf16[384,640]{1,0:T(8,128)(2,1)S(1)}, bf16[384,640]{1,0:T(8,128)(2,1)S(1)}) fusion(bf16[384,640]{1,0:T(8,128)(2,1)S(1)} %collective-permute-done.refs_1_, pred[]{:T(512)S(6)} %eq.11, bf16[384,640]{1,0:T(8,128)(2,1)} %collective-permute-done.8, bf16[384,640]{1,0:T(8,128)(2,1)} %collective-permute-done.5), kind=kLoop, calls=%fused_computation.1 | loop fusion | flops 491520 | bytes 2457601 | tf_op jit(solution)/shard_map/jit(_where)/select_n | solution.py:318
  54.9 1.4 %collective-permute-start.9 = (bf16[384,640]{1,0:T(8,128)(2,1)S(1)}, bf16[384,640]{1,0:T(8,128)(2,1)S(1)}, u32[]{:S(2)}, u32[]{:S(2)}) collective-permute-start(bf16[384,640]{1,0:T(8,128)(2,1)S(1)} %get-tuple-element.67), channel_id=1, source_target_pairs={{0,4},{4,0},{8,12},{12,8},{16,20},{20,16},{24,28},{28,24},{32,36},... | collective-permute-start | bytes 1474568 | tf_op jit(solution)/shard_map/ppermute | solution.py:320
  56.4 1.8 %far0_3.3.refs_5_.att0_ref = bf16[384,384]{1,0:T(8,128)(2,1)S(1)} custom-call(s32[1]{0:T(128)} %get-tuple-element.70.valid_ref, bf16[384,768]{1,0:T(8,128)(2,1)S(1)} %copy-done, f32[3,384,384]{2,1,0:T(8,128)S(1)} %far0_3.2.state_ref, bf16[384,896]{1,0:T(8,128)(2,1)S(1)} %collective-permute-done.6.refs_0_.refs_2_, ...), custom_call_target="tpu_custom_call" | custom-call | flops 1 | bytes 1 | tf_op jit(solution)/shard_map/far0_3/pallas_call | solution.py:203
  58.3 3.4 %last.1 = (bf16[384,384]{1,0:T(8,128)(2,1)S(1)}, bf16[384,768]{1,0:T(8,128)(2,1)S(1)}) custom-call(s32[2]{0:T(128)S(1)} %slice.15.valid_ref, bf16[384,768]{1,0:T(8,128)(2,1)S(1)} %copy-done, f32[6,384,384]{2,1,0:T(8,128)S(1)} %far0_6.1.state_ref, bf16[384,896]{1,0:T(8,128)(2,1)S(1)} %collective-permute-done.4.refs_0_, ...), custom_call_target="tpu_custom_call" | custom-call | flops 1 | bytes 1 | tf_op jit(solution)/shard_map/last/pallas_call | solution.py:218
  62.1 2.0 %project.1 = (bf16[384,768]{1,0:T(8,128)(2,1)S(1)}, bf16[384,768]{1,0:T(8,128)(2,1)S(1)}, bf16[384,768]{1,0:T(8,128)(2,1)S(1)}) custom-call(bf16[384,384]{1,0:T(8,128)(2,1)S(1)} %far0_3.3.refs_5_.att0_ref, bf16[384,384]{1,0:T(8,128)(2,1)S(1)} %get-tuple-element.59.att1_ref, bf16[768,768]{1,0:T(8,128)(2,1)S(1)} %get-tuple-element.60.refs_0_, ...), custom_call_target="tpu_custom_call" | custom-call | flops 1 | bytes 1 | tf_op jit(solution)/shard_map/project/pallas_call | solution.py:366
  64.1 1.7 %collective-permute-start.10 = (bf16[384,768]{1,0:T(8,128)(2,1)S(1)}, bf16[384,768]{1,0:T(8,128)(2,1)S(1)}, u32[]{:S(2)}, u32[]{:S(2)}) collective-permute-start(bf16[384,768]{1,0:T(8,128)(2,1)S(1)} %get-tuple-element.64), channel_id=1, source_target_pairs={{0,1},{1,0},{2,3},{3,2},{4,5},{5,4},{6,7},{7,6},{8,9},{9,8},{10,11... | collective-permute-start | bytes 1769480 | tf_op jit(solution)/shard_map/ppermute | solution.py:379
  65.9 12.1 %collective-permute-done.11 = bf16[384,768]{1,0:T(8,128)(2,1)S(1)} collective-permute-done((bf16[384,768]{1,0:T(8,128)(2,1)S(1)}, bf16[384,768]{1,0:T(8,128)(2,1)S(1)}, u32[]{:S(2)}, u32[]{:S(2)}) %collective-permute-start.11) | collective-permute-done | bytes 589856 | tf_op jit(solution)/shard_map/ppermute | solution.py:379
  78.1 2.3 %collective-permute-start.12 = (bf16[384,768]{1,0:T(8,128)(2,1)S(1)}, bf16[384,768]{1,0:T(8,128)(2,1)S(1)}, u32[]{:S(2)}, u32[]{:S(2)}) collective-permute-start(bf16[384,768]{1,0:T(8,128)(2,1)S(1)} %add_convert_fusion), channel_id=1, source_target_pairs={{0,2},{1,3},{2,0},{3,1},{4,6},{5,7},{6,4},{7,5},{8,10},{9,11},{10,... | collective-permute-start | bytes 1769480 | tf_op jit(solution)/shard_map/ppermute | solution.py:379
  80.3 20.6 %collective-permute-done.10.refs_1_ = bf16[384,768]{1,0:T(8,128)(2,1)S(1)} collective-permute-done((bf16[384,768]{1,0:T(8,128)(2,1)S(1)}, bf16[384,768]{1,0:T(8,128)(2,1)S(1)}, u32[]{:S(2)}, u32[]{:S(2)}) %collective-permute-start.10) | collective-permute-done | bytes 589856 | tf_op jit(solution)/shard_map/ppermute | solution.py:379
  101.0 4.9 %collective-permute-done.12.refs_2_ = bf16[384,768]{1,0:T(8,128)(2,1)S(1)} collective-permute-done((bf16[384,768]{1,0:T(8,128)(2,1)S(1)}, bf16[384,768]{1,0:T(8,128)(2,1)S(1)}, u32[]{:S(2)}, u32[]{:S(2)}) %collective-permute-start.12) | collective-permute-done | bytes 589856 | tf_op jit(solution)/shard_map/ppermute | solution.py:379
  (27 shorter events, 4.2 us)
Async XLA Ops:
  0.0 15.1 %copy-start.3 = (bf16[384,768]{1,0:T(8,128)(2,1)S(1)}, bf16[384,768]{1,0:T(8,128)(2,1)}, u32[]{:S(2)}) copy-start(bf16[384,768]{1,0:T(8,128)(2,1)} %k_ref.3) | copy-start | bytes 1769476
  0.0 15.1 %copy-start = (bf16[384,768]{1,0:T(8,128)(2,1)S(1)}, bf16[384,768]{1,0:T(8,128)(2,1)}, u32[]{:S(2)}) copy-start(bf16[384,768]{1,0:T(8,128)(2,1)} %q_ref.9) | copy-start | bytes 1769476
  0.0 15.0 %collective-permute-start.1 = (bf16[384,768]{1,0:T(8,128)(2,1)}, bf16[384,768]{1,0:T(8,128)(2,1)S(1)}, u32[]{:S(2)}, u32[]{:S(2)}) collective-permute-start(bf16[384,768]{1,0:T(8,128)(2,1)} %k_ref.3), channel_id=1, source_target_pairs={{0,4},{4,0},{8,12},{12,8},{16,20},{20,16},{24,28},{28,24},{32,36},... | collective-permute-start | bytes 1769480 | tf_op jit(solution)/shard_map/ppermute | solution.py:291
  0.0 15.0 %collective-permute-start.2 = (bf16[384,768]{1,0:T(8,128)(2,1)}, bf16[384,768]{1,0:T(8,128)(2,1)S(1)}, u32[]{:S(2)}, u32[]{:S(2)}) collective-permute-start(bf16[384,768]{1,0:T(8,128)(2,1)} %v_ref.3), channel_id=1, source_target_pairs={{0,4},{4,0},{8,12},{12,8},{16,20},{20,16},{24,28},{28,24},{32,36},... | collective-permute-start | bytes 1769480 | tf_op jit(solution)/shard_map/ppermute | solution.py:292
  2.6 18.8 %collective-permute-start = (bf16[384,640]{1,0:T(8,128)(2,1)}, bf16[384,640]{1,0:T(8,128)(2,1)S(1)}, u32[]{:S(2)}, u32[]{:S(2)}) collective-permute-start(bf16[384,640]{1,0:T(8,128)(2,1)} %get-tuple-element.56), channel_id=1, source_target_pairs={{0,8},{4,12},{8,0},{12,4},{16,24},{20,28},{24,16},{28,20},{32,40},... | collective-permute-start | bytes 1474568 | tf_op jit(solution)/shard_map/ppermute | solution.py:294
  4.2 46.2 %collective-permute-start.4 = (bf16[384,896]{1,0:T(8,128)(2,1)S(1)}, bf16[384,896]{1,0:T(8,128)(2,1)S(1)}, u32[]{:S(2)}, u32[]{:S(2)}) collective-permute-start(bf16[384,896]{1,0:T(8,128)(2,1)S(1)} %get-tuple-element.47), channel_id=1, source_target_pairs={{8,16},{12,20},{16,8},{20,12},{24,32},{28,36},{32,24},{36,28},{40,... | collective-permute-start | bytes 2064392 | tf_op jit(solution)/shard_map/ppermute | solution.py:295
  15.0 20.2 %collective-permute-start.3 = (bf16[384,896]{1,0:T(8,128)(2,1)S(1)}, bf16[384,896]{1,0:T(8,128)(2,1)S(1)}, u32[]{:S(2)}, u32[]{:S(2)}) collective-permute-start(bf16[384,896]{1,0:T(8,128)(2,1)S(1)} %get-tuple-element.47), channel_id=1, source_target_pairs={{0,8},{4,12},{8,0},{12,4},{16,24},{20,28},{24,16},{28,20},{32,40},... | collective-permute-start | bytes 2064392 | tf_op jit(solution)/shard_map/ppermute | solution.py:299
  15.1 1.1 copy-start.4
  19.6 1.8 %copy-start.1 = (f32[6,384,384]{2,1,0:T(8,128)}, f32[6,384,384]{2,1,0:T(8,128)S(1)}, u32[]{:S(2)}) copy-start(f32[6,384,384]{2,1,0:T(8,128)S(1)} %near.1.state_ref) | copy-start | bytes 10616836
  21.4 32.2 %collective-permute-start.5 = (bf16[384,640]{1,0:T(8,128)(2,1)S(1)}, bf16[384,640]{1,0:T(8,128)(2,1)}, u32[]{:S(2)}, u32[]{:S(2)}) collective-permute-start(bf16[384,640]{1,0:T(8,128)(2,1)S(1)} %collective-permute-done.refs_1_), channel_id=1, source_target_pairs={{16,32},{20,36},{40,24},{44,28},{48,64},{52,68},{72,56},{76,60},{8... | collective-permute-start | bytes 1474568 | tf_op jit(solution)/shard_map/ppermute | solution.py:304
  22.7 31.0 %collective-permute-start.8 = (bf16[384,640]{1,0:T(8,128)(2,1)}, bf16[384,640]{1,0:T(8,128)(2,1)}, u32[]{:S(2)}, u32[]{:S(2)}) collective-permute-start(bf16[384,640]{1,0:T(8,128)(2,1)} %get-tuple-element.56), channel_id=1, source_target_pairs={{8,16},{12,20},{16,8},{20,12},{40,48},{44,52},{48,40},{52,44},{72,... | collective-permute-start | bytes 1474568 | tf_op jit(solution)/shard_map/ppermute | solution.py:300
  24.9 11.6 %copy-start.2 = (f32[6,384,384]{2,1,0:T(8,128)S(1)}, f32[6,384,384]{2,1,0:T(8,128)}, u32[]{:S(2)}) copy-start(f32[6,384,384]{2,1,0:T(8,128)} %copy-done.1) | copy-start | bytes 10616836
  35.2 21.2 %collective-permute-start.6 = (bf16[384,896]{1,0:T(8,128)(2,1)S(1)}, bf16[384,896]{1,0:T(8,128)(2,1)S(1)}, u32[]{:S(2)}, u32[]{:S(2)}) collective-permute-start(bf16[384,896]{1,0:T(8,128)(2,1)S(1)} %collective-permute-done.3.refs_0_), channel_id=1, source_target_pairs={{0,4},{12,8},{16,20},{28,24},{32,36},{44,40},{48,52},{60,56},{64,6... | collective-permute-start | bytes 2064392 | tf_op jit(solution)/shard_map/ppermute | solution.py:314
  50.4 6.0 %collective-permute-start.7 = (bf16[384,896]{1,0:T(8,128)(2,1)S(1)}, bf16[384,896]{1,0:T(8,128)(2,1)S(1)}, u32[]{:S(2)}, u32[]{:S(2)}) collective-permute-start(bf16[384,896]{1,0:T(8,128)(2,1)S(1)} %collective-permute-done.4.refs_0_), channel_id=1, source_target_pairs={{4,0},{8,12},{20,16},{24,28},{36,32},{40,44},{52,48},{56,60},{68,6... | collective-permute-start | bytes 2064392 | tf_op jit(solution)/shard_map/ppermute | solution.py:319
  54.9 3.4 %collective-permute-start.9 = (bf16[384,640]{1,0:T(8,128)(2,1)S(1)}, bf16[384,640]{1,0:T(8,128)(2,1)S(1)}, u32[]{:S(2)}, u32[]{:S(2)}) collective-permute-start(bf16[384,640]{1,0:T(8,128)(2,1)S(1)} %get-tuple-element.67), channel_id=1, source_target_pairs={{0,4},{4,0},{8,12},{12,8},{16,20},{20,16},{24,28},{28,24},{32,36},... | collective-permute-start | bytes 1474568 | tf_op jit(solution)/shard_map/ppermute | solution.py:320
  61.7 16.3 %collective-permute-start.11 = (bf16[384,768]{1,0:T(8,128)(2,1)S(1)}, bf16[384,768]{1,0:T(8,128)(2,1)S(1)}, u32[]{:S(2)}, u32[]{:S(2)}) collective-permute-start(bf16[384,768]{1,0:T(8,128)(2,1)S(1)} %get-tuple-element.66), channel_id=1, source_target_pairs={{0,1},{1,0},{2,3},{3,2},{4,5},{5,4},{6,7},{7,6},{8,9},{9,8},{10,11... | collective-permute-start | bytes 1769480 | tf_op jit(solution)/shard_map/ppermute | solution.py:379
  64.1 36.8 %collective-permute-start.10 = (bf16[384,768]{1,0:T(8,128)(2,1)S(1)}, bf16[384,768]{1,0:T(8,128)(2,1)S(1)}, u32[]{:S(2)}, u32[]{:S(2)}) collective-permute-start(bf16[384,768]{1,0:T(8,128)(2,1)S(1)} %get-tuple-element.64), channel_id=1, source_target_pairs={{0,1},{1,0},{2,3},{3,2},{4,5},{5,4},{6,7},{7,6},{8,9},{9,8},{10,11... | collective-permute-start | bytes 1769480 | tf_op jit(solution)/shard_map/ppermute | solution.py:379
  78.1 27.8 %collective-permute-start.12 = (bf16[384,768]{1,0:T(8,128)(2,1)S(1)}, bf16[384,768]{1,0:T(8,128)(2,1)S(1)}, u32[]{:S(2)}, u32[]{:S(2)}) collective-permute-start(bf16[384,768]{1,0:T(8,128)(2,1)S(1)} %add_convert_fusion), channel_id=1, source_target_pairs={{0,2},{1,3},{2,0},{3,1},{4,6},{5,7},{6,4},{7,5},{8,10},{9,11},{10,... | collective-permute-start | bytes 1769480 | tf_op jit(solution)/shard_map/ppermute | solution.py:379

commit v7 on v6

--- a/solution.py
+++ b/solution.py
@@ -14,7 +14,7 @@
 ROW = 8
 KEYS, VALUES = 4, 3
 WEIGHT = 30
-LIGHT = pl.CostEstimate(flops=1, bytes_accessed=1, transcendentals=0)
+LIGHT = pl.CostEstimate(flops=1, bytes_accessed=2 * 10**6, transcendentals=0)
 SCALE = math.log2(math.e) / math.sqrt(HD)
 LOWEST = -1e30
 
@@ -293,15 +293,16 @@
     direct, relayed = packed(key_states, value_states)
     mate1 = lax.ppermute(relayed, "seq", MATE)
     other0 = lax.ppermute(direct, "seq", OTHER)
-    direct, relayed, pair_key, pair_value = lax.optimization_barrier(
-        (direct, relayed, pair_key, pair_value)
-    )
+    direct, pair_key, pair_value = lax.optimization_barrier((direct, pair_key, pair_value))
     mate0 = lax.ppermute(direct, "seq", MATE)
-    row_other1 = lax.ppermute(relayed, "seq", OTHER_IN_ROW)
 
     state = near_part(queries, key_states, value_states, pair_key, pair_value)
-    mate1, state, out_weight = lax.optimization_barrier((mate1, state, out_weight))
+    mate1, state, out_weight, key_states, value_states = lax.optimization_barrier(
+        (mate1, state, out_weight, key_states, value_states)
+    )
     passed_other1 = lax.ppermute(mate1, "seq", ONWARD)
+    again = jnp.concatenate([key_states[:, KEYS * HD :], value_states[:, VALUES * HD :]], axis=1)
+    row_other1 = lax.ppermute(again, "seq", OTHER_IN_ROW)
     z = lax.axis_index("head")
     weights = weight_columns(jnp.stack([z ^ 3, z ^ 1, z ^ 2, z]), out_weight)
     state, *weights = lax.optimization_barrier((state, *weights))

time: 107 us -> 107 us (level)
  waiting for transfers between devices: 55.7 us -> 54.2 us
    ppermute x1, waiting for transfers between devices: 7.06 us -> 5.26 us  [body(): mate0 = lax.ppermute(direct, 'seq', MATE)]
  transfers between devices with their start and end apart: 13 -> 13, of which waited for: 5 -> 5; matrix products, arithmetic and copies ran while one was open for 2% -> 4% of each run, Pallas kernels for 16% -> 15%
where the time goes in v7:
time: 107 us; the launch traced here: 106 us
  waiting for transfers between devices  54.2 us (51%)
  starting transfers between devices  24.1 us (23%)
  Pallas kernels  20.9 us (20%)
  local copies, waits for them, and re-layouts  4.54 us (4%)
  other arithmetic  2.38 us (2%)
    ppermute x3, waiting for transfers between devices, sent(): lax.ppermute(value, 'head', [(i, i ^ apart) for i in range(HEAD_PEERS)])  37.6 us
    ppermute x1, waiting for transfers between devices, body(): other0 = lax.ppermute(direct, 'seq', OTHER)  11.4 us
    ppermute x1, starting transfers between devices, body(): other0 = lax.ppermute(direct, 'seq', OTHER)  10.8 us
    pallas_call x3, Pallas kernels, far_part(): pl.pallas_call(functools.partial(far_kernel, list(heads), held_from, coun...  6.58 us
    ppermute x1, waiting for transfers between devices, body(): mate0 = lax.ppermute(direct, 'seq', MATE)  5.26 us
    ppermute x3, starting transfers between devices, sent(): lax.ppermute(value, 'head', [(i, i ^ apart) for i in range(HEAD_PEERS)])  4.42 us
    pallas_call x2, Pallas kernels, small_call(): pl.pallas_call(kernel, out_shape=out_shape, in_specs=[pl.BlockSpec(memory...  4.23 us
    pallas_call x1, Pallas kernels, near_part(): pl.pallas_call(near_kernel, out_shape=jax.ShapeDtypeStruct((heads, rows,...  3.39 us
  transfers between devices with their start and end apart: 13, of which 5 were waited for; matrix products, arithmetic and copies ran while one was open for 4% of the time, Pallas kernels for 15%

profile of v7, /device:TPU:24, one launch (start us, length us, event | category | flops | bytes accessed | tf_op | source)
XLA Modules:
  0.0 106.4 jit_solution(5000267642111418482)
XLA Ops:
  0.5 1.3 %pack.1 = (bf16[384,896]{1,0:T(8,128)(2,1)S(1)}, bf16[384,640]{1,0:T(8,128)(2,1)S(1)}) custom-call(bf16[384,768]{1,0:T(8,128)(2,1)} %k_ref.3, bf16[384,768]{1,0:T(8,128)(2,1)} %v_ref.3), custom_call_target="tpu_custom_call" | custom-call | flops 1 | bytes 2000000 | tf_op jit(solution)/shard_map/pack/pallas_call | solution.py:236
  1.8 1.6 %collective-permute-start = (bf16[384,640]{1,0:T(8,128)(2,1)S(1)}, bf16[384,640]{1,0:T(8,128)(2,1)S(1)}, u32[]{:S(2)}, u32[]{:S(2)}) collective-permute-start(bf16[384,640]{1,0:T(8,128)(2,1)S(1)} %get-tuple-element.37), channel_id=1, source_target_pairs={{0,8},{4,12},{8,0},{12,4},{16,24},{20,28},{24,16},{28,20},{32,40},... | collective-permute-start | bytes 1474568 | tf_op jit(solution)/shard_map/ppermute | solution.py:294
  3.4 10.8 %collective-permute-start.4 = (bf16[384,896]{1,0:T(8,128)(2,1)S(1)}, bf16[384,896]{1,0:T(8,128)(2,1)S(1)}, u32[]{:S(2)}, u32[]{:S(2)}) collective-permute-start(bf16[384,896]{1,0:T(8,128)(2,1)S(1)} %get-tuple-element.48), channel_id=1, source_target_pairs={{8,16},{12,20},{16,8},{20,12},{24,32},{28,36},{32,24},{36,28},{40,... | collective-permute-start | bytes 2064392 | tf_op jit(solution)/shard_map/ppermute | solution.py:295
  15.4 3.4 %near.1.state_ref = f32[6,384,384]{2,1,0:T(8,128)S(1)} custom-call(bf16[384,768]{1,0:T(8,128)(2,1)S(1)} %copy-done, bf16[384,768]{1,0:T(8,128)(2,1)S(1)} %copy-done.4, bf16[384,768]{1,0:T(8,128)(2,1)S(1)} %copy-done.3, bf16[384,768]{1,0:T(8,128)(2,1)S(1)} %collective-permute-done.1.pk_ref, bf16[384,768]{1,0:T(8,128)(2,1)S(1)} %collective-permute-done.2.pv_ref), custom_call_target="tpu_custom_call" | custom-call | flops 40768634880 | bytes 2949120 | tf_op jit(solution)/shard_map/near/pallas_call | solution.py:180
  18.8 1.8 %copy-done.1 = f32[6,384,384]{2,1,0:T(8,128)} copy-done((f32[6,384,384]{2,1,0:T(8,128)}, f32[6,384,384]{2,1,0:T(8,128)S(1)}, u32[]{:S(2)}) %copy-start.1) | copy-done | bytes 3538968
  20.6 1.3 %collective-permute-start.5 = (bf16[384,640]{1,0:T(8,128)(2,1)S(1)}, bf16[384,640]{1,0:T(8,128)(2,1)}, u32[]{:S(2)}, u32[]{:S(2)}) collective-permute-start(bf16[384,640]{1,0:T(8,128)(2,1)S(1)} %collective-permute-done.refs_1_), channel_id=1, source_target_pairs={{16,32},{20,36},{40,24},{44,28},{48,64},{52,68},{72,56},{76,60},{8... | collective-permute-start | bytes 1474568 | tf_op jit(solution)/shard_map/ppermute | solution.py:303
  23.7 1.4 %collective-permute-start.8 = (bf16[384,640]{1,0:T(8,128)(2,1)}, bf16[384,640]{1,0:T(8,128)(2,1)}, u32[]{:S(2)}, u32[]{:S(2)}) collective-permute-start(bf16[384,640]{1,0:T(8,128)(2,1)} %pad_maximum_fusion), channel_id=1, source_target_pairs={{8,16},{12,20},{16,8},{20,12},{40,48},{44,52},{48,40},{52,44},{72,... | collective-permute-start | bytes 1474568 | tf_op jit(solution)/shard_map/ppermute | solution.py:305
  26.0 3.2 %columns.1 = (bf16[768,768]{1,0:T(8,128)(2,1)S(1)}, bf16[768,768]{1,0:T(8,128)(2,1)S(1)}, bf16[768,768]{1,0:T(8,128)(2,1)S(1)}, bf16[768,768]{1,0:T(8,128)(2,1)S(1)}) custom-call(s32[4]{0:T(128)S(1)} %pad_add_fusion.which_ref, bf16[768,3072]{1,0:T(8,128)(2,1)} %w_ref), custom_call_target="tpu_custom_call" | custom-call | flops 1 | bytes 2000000 | tf_op jit(solution)/shard_map/columns/pallas_call | solution.py:332
  29.2 5.3 %collective-permute-done.3.refs_0_ = bf16[384,896]{1,0:T(8,128)(2,1)S(1)} collective-permute-done((bf16[384,896]{1,0:T(8,128)(2,1)S(1)}, bf16[384,896]{1,0:T(8,128)(2,1)S(1)}, u32[]{:S(2)}, u32[]{:S(2)}) %collective-permute-start.3) | collective-permute-done | bytes 688160 | tf_op jit(solution)/shard_map/ppermute | solution.py:297
  34.4 1.3 %collective-permute-start.6 = (bf16[384,896]{1,0:T(8,128)(2,1)S(1)}, bf16[384,896]{1,0:T(8,128)(2,1)S(1)}, u32[]{:S(2)}, u32[]{:S(2)}) collective-permute-start(bf16[384,896]{1,0:T(8,128)(2,1)S(1)} %collective-permute-done.3.refs_0_), channel_id=1, source_target_pairs={{0,4},{12,8},{16,20},{28,24},{32,36},{44,40},{48,52},{60,56},{64,6... | collective-permute-start | bytes 2064392 | tf_op jit(solution)/shard_map/ppermute | solution.py:315
  35.8 2.8 %far0_6.1.state_ref = f32[6,384,384]{2,1,0:T(8,128)S(1)} custom-call(s32[1]{0:T(128)} %get-tuple-element.73.valid_ref, bf16[384,768]{1,0:T(8,128)(2,1)S(1)} %copy-done, f32[6,384,384]{2,1,0:T(8,128)S(1)} %copy-done.2, bf16[384,896]{1,0:T(8,128)(2,1)S(1)} %collective-permute-done.3.refs_0_, bf16[384,640]{1,0:T(8,128)(2,1)S(1)} %collective-permute-done.refs_1_), custom_call_target="tpu_custom_call" | custom-call | flops 1 | bytes 2000000 | tf_op jit(solution)/shard_map/far0_6/pallas_call | solution.py:203
  38.6 11.4 %collective-permute-done.4.refs_0_ = bf16[384,896]{1,0:T(8,128)(2,1)S(1)} collective-permute-done((bf16[384,896]{1,0:T(8,128)(2,1)S(1)}, bf16[384,896]{1,0:T(8,128)(2,1)S(1)}, u32[]{:S(2)}, u32[]{:S(2)}) %collective-permute-start.4) | collective-permute-done | bytes 688160 | tf_op jit(solution)/shard_map/ppermute | solution.py:295
  49.9 1.3 %collective-permute-start.7 = (bf16[384,896]{1,0:T(8,128)(2,1)S(1)}, bf16[384,896]{1,0:T(8,128)(2,1)S(1)}, u32[]{:S(2)}, u32[]{:S(2)}) collective-permute-start(bf16[384,896]{1,0:T(8,128)(2,1)S(1)} %collective-permute-done.4.refs_0_), channel_id=1, source_target_pairs={{4,0},{8,12},{20,16},{24,28},{36,32},{40,44},{52,48},{56,60},{68,6... | collective-permute-start | bytes 2064392 | tf_op jit(solution)/shard_map/ppermute | solution.py:320
  51.2 1.9 %far0_3.2.state_ref = f32[3,384,384]{2,1,0:T(8,128)S(1)} custom-call(s32[1]{0:T(128)} %get-tuple-element.71.valid_ref, bf16[384,768]{1,0:T(8,128)(2,1)S(1)} %copy-done, f32[6,384,384]{2,1,0:T(8,128)S(1)} %far0_6.1.state_ref, bf16[384,896]{1,0:T(8,128)(2,1)S(1)} %collective-permute-done.4.refs_0_), custom_call_target="tpu_custom_call" | custom-call | flops 1 | bytes 2000000 | tf_op jit(solution)/shard_map/far0_3/pallas_call | solution.py:203
  53.2 1.3 %broadcast_select_fusion = (bf16[384,640]{1,0:T(8,128)(2,1)S(1)}, bf16[384,640]{1,0:T(8,128)(2,1)S(1)}) fusion(bf16[384,640]{1,0:T(8,128)(2,1)S(1)} %collective-permute-done.refs_1_, pred[]{:T(512)S(6)} %eq.11, bf16[384,640]{1,0:T(8,128)(2,1)} %collective-permute-done.8, bf16[384,640]{1,0:T(8,128)(2,1)} %collective-permute-done.5), kind=kLoop, calls=%fused_computation.2 | loop fusion | flops 491520 | bytes 2457601 | tf_op jit(solution)/shard_map/jit(_where)/select_n | solution.py:319
  54.5 1.4 %collective-permute-start.9 = (bf16[384,640]{1,0:T(8,128)(2,1)S(1)}, bf16[384,640]{1,0:T(8,128)(2,1)S(1)}, u32[]{:S(2)}, u32[]{:S(2)}) collective-permute-start(bf16[384,640]{1,0:T(8,128)(2,1)S(1)} %get-tuple-element.69), channel_id=1, source_target_pairs={{0,4},{4,0},{8,12},{12,8},{16,20},{20,16},{24,28},{28,24},{32,36},... | collective-permute-start | bytes 1474568 | tf_op jit(solution)/shard_map/ppermute | solution.py:321
  56.0 1.8 %far0_3.3.refs_5_.att0_ref = bf16[384,384]{1,0:T(8,128)(2,1)S(1)} custom-call(s32[1]{0:T(128)} %get-tuple-element.72.valid_ref, bf16[384,768]{1,0:T(8,128)(2,1)S(1)} %copy-done, f32[3,384,384]{2,1,0:T(8,128)S(1)} %far0_3.2.state_ref, bf16[384,896]{1,0:T(8,128)(2,1)S(1)} %collective-permute-done.6.refs_0_.refs_2_, ...), custom_call_target="tpu_custom_call" | custom-call | flops 1 | bytes 2000000 | tf_op jit(solution)/shard_map/far0_3/pallas_call | solution.py:203
  57.8 3.4 %last.1 = (bf16[384,384]{1,0:T(8,128)(2,1)S(1)}, bf16[384,768]{1,0:T(8,128)(2,1)S(1)}) custom-call(s32[2]{0:T(128)S(1)} %slice.21.valid_ref, bf16[384,768]{1,0:T(8,128)(2,1)S(1)} %copy-done, f32[6,384,384]{2,1,0:T(8,128)S(1)} %far0_6.1.state_ref, bf16[384,896]{1,0:T(8,128)(2,1)S(1)} %collective-permute-done.4.refs_0_, ...), custom_call_target="tpu_custom_call" | custom-call | flops 1 | bytes 2000000 | tf_op jit(solution)/shard_map/last/pallas_call | solution.py:218
  61.4 2.0 %project.1 = (bf16[384,768]{1,0:T(8,128)(2,1)S(1)}, bf16[384,768]{1,0:T(8,128)(2,1)S(1)}, bf16[384,768]{1,0:T(8,128)(2,1)S(1)}) custom-call(bf16[384,384]{1,0:T(8,128)(2,1)S(1)} %far0_3.3.refs_5_.att0_ref, bf16[384,384]{1,0:T(8,128)(2,1)S(1)} %get-tuple-element.61.att1_ref, bf16[768,768]{1,0:T(8,128)(2,1)S(1)} %get-tuple-element.62.refs_0_, ...), custom_call_target="tpu_custom_call" | custom-call | flops 1 | bytes 2000000 | tf_op jit(solution)/shard_map/project/pallas_call | solution.py:367
  63.4 2.0 %collective-permute-start.10 = (bf16[384,768]{1,0:T(8,128)(2,1)S(1)}, bf16[384,768]{1,0:T(8,128)(2,1)S(1)}, u32[]{:S(2)}, u32[]{:S(2)}) collective-permute-start(bf16[384,768]{1,0:T(8,128)(2,1)S(1)} %get-tuple-element.66), channel_id=1, source_target_pairs={{0,1},{1,0},{2,3},{3,2},{4,5},{5,4},{6,7},{7,6},{8,9},{9,8},{10,11... | collective-permute-start | bytes 1769480 | tf_op jit(solution)/shard_map/ppermute | solution.py:380
  65.4 12.1 %collective-permute-done.11 = bf16[384,768]{1,0:T(8,128)(2,1)S(1)} collective-permute-done((bf16[384,768]{1,0:T(8,128)(2,1)S(1)}, bf16[384,768]{1,0:T(8,128)(2,1)S(1)}, u32[]{:S(2)}, u32[]{:S(2)}) %collective-permute-start.11) | collective-permute-done | bytes 589856 | tf_op jit(solution)/shard_map/ppermute | solution.py:380
  77.6 2.2 %collective-permute-start.12 = (bf16[384,768]{1,0:T(8,128)(2,1)S(1)}, bf16[384,768]{1,0:T(8,128)(2,1)S(1)}, u32[]{:S(2)}, u32[]{:S(2)}) collective-permute-start(bf16[384,768]{1,0:T(8,128)(2,1)S(1)} %add_convert_fusion), channel_id=1, source_target_pairs={{0,2},{1,3},{2,0},{3,1},{4,6},{5,7},{6,4},{7,5},{8,10},{9,11},{10,... | collective-permute-start | bytes 1769480 | tf_op jit(solution)/shard_map/ppermute | solution.py:380
  79.9 20.7 %collective-permute-done.10.refs_1_ = bf16[384,768]{1,0:T(8,128)(2,1)S(1)} collective-permute-done((bf16[384,768]{1,0:T(8,128)(2,1)S(1)}, bf16[384,768]{1,0:T(8,128)(2,1)S(1)}, u32[]{:S(2)}, u32[]{:S(2)}) %collective-permute-start.10) | collective-permute-done | bytes 589856 | tf_op jit(solution)/shard_map/ppermute | solution.py:380
  100.5 4.8 %collective-permute-done.12.refs_2_ = bf16[384,768]{1,0:T(8,128)(2,1)S(1)} collective-permute-done((bf16[384,768]{1,0:T(8,128)(2,1)S(1)}, bf16[384,768]{1,0:T(8,128)(2,1)S(1)}, u32[]{:S(2)}, u32[]{:S(2)}) %collective-permute-start.12) | collective-permute-done | bytes 589856 | tf_op jit(solution)/shard_map/ppermute | solution.py:380
  (30 shorter events, 5.7 us)
Async XLA Ops:
  0.0 14.3 %copy-start.3 = (bf16[384,768]{1,0:T(8,128)(2,1)S(1)}, bf16[384,768]{1,0:T(8,128)(2,1)}, u32[]{:S(2)}) copy-start(bf16[384,768]{1,0:T(8,128)(2,1)} %v_ref.3) | copy-start | bytes 1769476
  0.0 14.3 %copy-start = (bf16[384,768]{1,0:T(8,128)(2,1)S(1)}, bf16[384,768]{1,0:T(8,128)(2,1)}, u32[]{:S(2)}) copy-start(bf16[384,768]{1,0:T(8,128)(2,1)} %q_ref.9) | copy-start | bytes 1769476
  0.0 14.2 %collective-permute-start.1 = (bf16[384,768]{1,0:T(8,128)(2,1)}, bf16[384,768]{1,0:T(8,128)(2,1)S(1)}, u32[]{:S(2)}, u32[]{:S(2)}) collective-permute-start(bf16[384,768]{1,0:T(8,128)(2,1)} %k_ref.3), channel_id=1, source_target_pairs={{0,4},{4,0},{8,12},{12,8},{16,20},{20,16},{24,28},{28,24},{32,36},... | collective-permute-start | bytes 1769480 | tf_op jit(solution)/shard_map/ppermute | solution.py:291
  0.0 14.2 %collective-permute-start.2 = (bf16[384,768]{1,0:T(8,128)(2,1)}, bf16[384,768]{1,0:T(8,128)(2,1)S(1)}, u32[]{:S(2)}, u32[]{:S(2)}) collective-permute-start(bf16[384,768]{1,0:T(8,128)(2,1)} %v_ref.3), channel_id=1, source_target_pairs={{0,4},{4,0},{8,12},{12,8},{16,20},{20,16},{24,28},{28,24},{32,36},... | collective-permute-start | bytes 1769480 | tf_op jit(solution)/shard_map/ppermute | solution.py:292
  1.8 18.8 %collective-permute-start = (bf16[384,640]{1,0:T(8,128)(2,1)S(1)}, bf16[384,640]{1,0:T(8,128)(2,1)S(1)}, u32[]{:S(2)}, u32[]{:S(2)}) collective-permute-start(bf16[384,640]{1,0:T(8,128)(2,1)S(1)} %get-tuple-element.37), channel_id=1, source_target_pairs={{0,8},{4,12},{8,0},{12,4},{16,24},{20,28},{24,16},{28,20},{32,40},... | collective-permute-start | bytes 1474568 | tf_op jit(solution)/shard_map/ppermute | solution.py:294
  3.4 46.5 %collective-permute-start.4 = (bf16[384,896]{1,0:T(8,128)(2,1)S(1)}, bf16[384,896]{1,0:T(8,128)(2,1)S(1)}, u32[]{:S(2)}, u32[]{:S(2)}) collective-permute-start(bf16[384,896]{1,0:T(8,128)(2,1)S(1)} %get-tuple-element.48), channel_id=1, source_target_pairs={{8,16},{12,20},{16,8},{20,12},{24,32},{28,36},{32,24},{36,28},{40,... | collective-permute-start | bytes 2064392 | tf_op jit(solution)/shard_map/ppermute | solution.py:295
  14.2 20.2 %collective-permute-start.3 = (bf16[384,896]{1,0:T(8,128)(2,1)S(1)}, bf16[384,896]{1,0:T(8,128)(2,1)S(1)}, u32[]{:S(2)}, u32[]{:S(2)}) collective-permute-start(bf16[384,896]{1,0:T(8,128)(2,1)S(1)} %get-tuple-element.48), channel_id=1, source_target_pairs={{0,8},{4,12},{8,0},{12,4},{16,24},{20,28},{24,16},{28,20},{32,40},... | collective-permute-start | bytes 2064392 | tf_op jit(solution)/shard_map/ppermute | solution.py:297
  14.4 1.1 %copy-start.4 = (bf16[384,768]{1,0:T(8,128)(2,1)S(1)}, bf16[384,768]{1,0:T(8,128)(2,1)}, u32[]{:S(2)}) copy-start(bf16[384,768]{1,0:T(8,128)(2,1)} %k_ref.3) | copy-start | bytes 1769476
  18.8 1.8 %copy-start.1 = (f32[6,384,384]{2,1,0:T(8,128)}, f32[6,384,384]{2,1,0:T(8,128)S(1)}, u32[]{:S(2)}) copy-start(f32[6,384,384]{2,1,0:T(8,128)S(1)} %near.1.state_ref) | copy-start | bytes 10616836
  20.6 32.6 %collective-permute-start.5 = (bf16[384,640]{1,0:T(8,128)(2,1)S(1)}, bf16[384,640]{1,0:T(8,128)(2,1)}, u32[]{:S(2)}, u32[]{:S(2)}) collective-permute-start(bf16[384,640]{1,0:T(8,128)(2,1)S(1)} %collective-permute-done.refs_1_), channel_id=1, source_target_pairs={{16,32},{20,36},{40,24},{44,28},{48,64},{52,68},{72,56},{76,60},{8... | collective-permute-start | bytes 1474568 | tf_op jit(solution)/shard_map/ppermute | solution.py:303
  23.7 29.5 %collective-permute-start.8 = (bf16[384,640]{1,0:T(8,128)(2,1)}, bf16[384,640]{1,0:T(8,128)(2,1)}, u32[]{:S(2)}, u32[]{:S(2)}) collective-permute-start(bf16[384,640]{1,0:T(8,128)(2,1)} %pad_maximum_fusion), channel_id=1, source_target_pairs={{8,16},{12,20},{16,8},{20,12},{40,48},{44,52},{48,40},{52,44},{72,... | collective-permute-start | bytes 1474568 | tf_op jit(solution)/shard_map/ppermute | solution.py:305
  25.9 9.8 %copy-start.2 = (f32[6,384,384]{2,1,0:T(8,128)S(1)}, f32[6,384,384]{2,1,0:T(8,128)}, u32[]{:S(2)}) copy-start(f32[6,384,384]{2,1,0:T(8,128)} %copy-done.1) | copy-start | bytes 10616836
  34.4 21.5 %collective-permute-start.6 = (bf16[384,896]{1,0:T(8,128)(2,1)S(1)}, bf16[384,896]{1,0:T(8,128)(2,1)S(1)}, u32[]{:S(2)}, u32[]{:S(2)}) collective-permute-start(bf16[384,896]{1,0:T(8,128)(2,1)S(1)} %collective-permute-done.3.refs_0_), channel_id=1, source_target_pairs={{0,4},{12,8},{16,20},{28,24},{32,36},{44,40},{48,52},{60,56},{64,6... | collective-permute-start | bytes 2064392 | tf_op jit(solution)/shard_map/ppermute | solution.py:315
  49.9 6.0 %collective-permute-start.7 = (bf16[384,896]{1,0:T(8,128)(2,1)S(1)}, bf16[384,896]{1,0:T(8,128)(2,1)S(1)}, u32[]{:S(2)}, u32[]{:S(2)}) collective-permute-start(bf16[384,896]{1,0:T(8,128)(2,1)S(1)} %collective-permute-done.4.refs_0_), channel_id=1, source_target_pairs={{4,0},{8,12},{20,16},{24,28},{36,32},{40,44},{52,48},{56,60},{68,6... | collective-permute-start | bytes 2064392 | tf_op jit(solution)/shard_map/ppermute | solution.py:320
  54.5 3.4 %collective-permute-start.9 = (bf16[384,640]{1,0:T(8,128)(2,1)S(1)}, bf16[384,640]{1,0:T(8,128)(2,1)S(1)}, u32[]{:S(2)}, u32[]{:S(2)}) collective-permute-start(bf16[384,640]{1,0:T(8,128)(2,1)S(1)} %get-tuple-element.69), channel_id=1, source_target_pairs={{0,4},{4,0},{8,12},{12,8},{16,20},{20,16},{24,28},{28,24},{32,36},... | collective-permute-start | bytes 1474568 | tf_op jit(solution)/shard_map/ppermute | solution.py:321
  61.2 16.3 %collective-permute-start.11 = (bf16[384,768]{1,0:T(8,128)(2,1)S(1)}, bf16[384,768]{1,0:T(8,128)(2,1)S(1)}, u32[]{:S(2)}, u32[]{:S(2)}) collective-permute-start(bf16[384,768]{1,0:T(8,128)(2,1)S(1)} %get-tuple-element.68), channel_id=1, source_target_pairs={{0,1},{1,0},{2,3},{3,2},{4,5},{5,4},{6,7},{7,6},{8,9},{9,8},{10,11... | collective-permute-start | bytes 1769480 | tf_op jit(solution)/shard_map/ppermute | solution.py:380
  63.4 37.1 %collective-permute-start.10 = (bf16[384,768]{1,0:T(8,128)(2,1)S(1)}, bf16[384,768]{1,0:T(8,128)(2,1)S(1)}, u32[]{:S(2)}, u32[]{:S(2)}) collective-permute-start(bf16[384,768]{1,0:T(8,128)(2,1)S(1)} %get-tuple-element.66), channel_id=1, source_target_pairs={{0,1},{1,0},{2,3},{3,2},{4,5},{5,4},{6,7},{7,6},{8,9},{9,8},{10,11... | collective-permute-start | bytes 1769480 | tf_op jit(solution)/shard_map/ppermute | solution.py:380
  77.6 27.7 %collective-permute-start.12 = (bf16[384,768]{1,0:T(8,128)(2,1)S(1)}, bf16[384,768]{1,0:T(8,128)(2,1)S(1)}, u32[]{:S(2)}, u32[]{:S(2)}) collective-permute-start(bf16[384,768]{1,0:T(8,128)(2,1)S(1)} %add_convert_fusion), channel_id=1, source_target_pairs={{0,2},{1,3},{2,0},{3,1},{4,6},{5,7},{6,4},{7,5},{8,10},{9,11},{10,... | collective-permute-start | bytes 1769480 | tf_op jit(solution)/shard_map/ppermute | solution.py:380

commit v8 on v7

--- a/solution.py
+++ b/solution.py
@@ -14,7 +14,7 @@
 ROW = 8
 KEYS, VALUES = 4, 3
 WEIGHT = 30
-LIGHT = pl.CostEstimate(flops=1, bytes_accessed=2 * 10**6, transcendentals=0)
+LIGHT = pl.CostEstimate(flops=1, bytes_accessed=1, transcendentals=0)
 SCALE = math.log2(math.e) / math.sqrt(HD)
 LOWEST = -1e30
 
@@ -315,15 +315,14 @@
     mate_shared0 = lax.ppermute(mate0, "seq", MATE_SHARED)
     state0 = far_part(soon, 0, False, valid[1:2], queries, state, [[[other0], []]])
     passed_other1, state0 = lax.optimization_barrier((passed_other1, state0))
-    other1 = row_other1 + passed_other1
-    to_swap = jnp.where(place % 2 == chip % 2, mate1, other1)
+    to_swap = jnp.where(place % 2 == chip % 2, mate1, row_other1 + passed_other1)
     other_shared0 = lax.ppermute(other0, "seq", OTHER_SHARED)
     swapped1 = lax.ppermute(to_swap, "seq", PAIR)
     third0, third1 = [mate_shared0, other_shared0], [swapped1]
     att0 = far_part(soon, 0, True, valid[2:], queries, state0, [[third0, []]])
     state, att0 = lax.optimization_barrier((state, att0))
     att1, distant = last_part(
-        later, valid[1:], queries, state, [[[other0], [other1]], [third0, third1]], att0, weights[0]
+        later, valid[1:], queries, state, [[[other0], [row_other1, passed_other1]], [third0, third1]], att0, weights[0]
     )
     return projected(att0, att1, distant, weights[1:])
 

time: 107 us -> 107 us (level)
  other arithmetic: 2.38 us -> 1.19 us
    select_n x1, other arithmetic: 1.27 us -> 0.08 us  [body(): jnp.where(place % 2 == chip % 2, mate1, row_other1 + passed_other1)]
  transfers between devices with their start and end apart: 13 -> 13, of which waited for: 5 -> 5; matrix products, arithmetic and copies ran while one was open for 4% -> 3% of each run, Pallas kernels for 15% -> 16%
where the time goes in v8:
time: 107 us; the launch traced here: 106 us
  waiting for transfers between devices  55.2 us (52%)
  starting transfers between devices  23.3 us (22%)
  Pallas kernels  21.8 us (20%)
  local copies, waits for them, and re-layouts  4.53 us (4%)
  other arithmetic  1.19 us (1%)
    ppermute x3, waiting for transfers between devices, sent(): lax.ppermute(value, 'head', [(i, i ^ apart) for i in range(HEAD_PEERS)])  37.6 us
    ppermute x1, waiting for transfers between devices, body(): other0 = lax.ppermute(direct, 'seq', OTHER)  11.4 us
    ppermute x1, starting transfers between devices, body(): other0 = lax.ppermute(direct, 'seq', OTHER)  10.8 us
    pallas_call x3, Pallas kernels, far_part(): pl.pallas_call(functools.partial(far_kernel, list(heads), held_from, coun...  6.63 us
    ppermute x1, waiting for transfers between devices, body(): mate0 = lax.ppermute(direct, 'seq', MATE)  6.19 us
    ppermute x3, starting transfers between devices, sent(): lax.ppermute(value, 'head', [(i, i ^ apart) for i in range(HEAD_PEERS)])  4.31 us
    pallas_call x2, Pallas kernels, small_call(): pl.pallas_call(kernel, out_shape=out_shape, in_specs=[pl.BlockSpec(memory...  4.23 us
    pallas_call x1, Pallas kernels, last_part(): pl.pallas_call(functools.partial(last_kernel, list(heads), counts), out_s...  3.43 us
  transfers between devices with their start and end apart: 13, of which 5 were waited for; matrix products, arithmetic and copies ran while one was open for 3% of the time, Pallas kernels for 16%

profile of v8, /device:TPU:24, one launch (start us, length us, event | category | flops | bytes accessed | tf_op | source)
XLA Modules:
  0.0 106.3 jit_solution(12429127948309982626)
XLA Ops:
  0.5 2.1 %pack.1 = (bf16[384,896]{1,0:T(8,128)(2,1)}, bf16[384,640]{1,0:T(8,128)(2,1)S(1)}) custom-call(bf16[384,768]{1,0:T(8,128)(2,1)} %k_ref.3, bf16[384,768]{1,0:T(8,128)(2,1)} %v_ref.3), custom_call_target="tpu_custom_call" | custom-call | flops 1 | bytes 1 | tf_op jit(solution)/shard_map/pack/pallas_call | solution.py:236
  2.7 1.6 %collective-permute-start = (bf16[384,640]{1,0:T(8,128)(2,1)S(1)}, bf16[384,640]{1,0:T(8,128)(2,1)S(1)}, u32[]{:S(2)}, u32[]{:S(2)}) collective-permute-start(bf16[384,640]{1,0:T(8,128)(2,1)S(1)} %get-tuple-element.37), channel_id=1, source_target_pairs={{0,8},{4,12},{8,0},{12,4},{16,24},{20,28},{24,16},{28,20},{32,40},... | collective-permute-start | bytes 1474568 | tf_op jit(solution)/shard_map/ppermute | solution.py:294
  4.2 10.8 %collective-permute-start.4 = (bf16[384,896]{1,0:T(8,128)(2,1)}, bf16[384,896]{1,0:T(8,128)(2,1)S(1)}, u32[]{:S(2)}, u32[]{:S(2)}) collective-permute-start(bf16[384,896]{1,0:T(8,128)(2,1)} %get-tuple-element.48), channel_id=1, source_target_pairs={{8,16},{12,20},{16,8},{20,12},{24,32},{28,36},{32,24},{36,28},{40,... | collective-permute-start | bytes 2064392 | tf_op jit(solution)/shard_map/ppermute | solution.py:295
  15.2 1.1 copy-done.4
  16.3 3.4 %near.1.state_ref = f32[6,384,384]{2,1,0:T(8,128)S(1)} custom-call(bf16[384,768]{1,0:T(8,128)(2,1)S(1)} %copy-done, bf16[384,768]{1,0:T(8,128)(2,1)S(1)} %copy-done.4, bf16[384,768]{1,0:T(8,128)(2,1)S(1)} %copy-done.3, bf16[384,768]{1,0:T(8,128)(2,1)S(1)} %collective-permute-done.1.pk_ref, bf16[384,768]{1,0:T(8,128)(2,1)S(1)} %collective-permute-done.2.pv_ref), custom_call_target="tpu_custom_call" | custom-call | flops 40768634880 | bytes 2949120 | tf_op jit(solution)/shard_map/near/pallas_call | solution.py:180
  19.7 1.8 %copy-done.1 = f32[6,384,384]{2,1,0:T(8,128)} copy-done((f32[6,384,384]{2,1,0:T(8,128)}, f32[6,384,384]{2,1,0:T(8,128)S(1)}, u32[]{:S(2)}) %copy-start.1) | copy-done | bytes 3538968
  21.4 1.3 %collective-permute-start.5 = (bf16[384,640]{1,0:T(8,128)(2,1)S(1)}, bf16[384,640]{1,0:T(8,128)(2,1)S(1)}, u32[]{:S(2)}, u32[]{:S(2)}) collective-permute-start(bf16[384,640]{1,0:T(8,128)(2,1)S(1)} %collective-permute-done.refs_1_), channel_id=1, source_target_pairs={{16,32},{20,36},{40,24},{44,28},{48,64},{52,68},{72,56},{76,60},{8... | collective-permute-start | bytes 1474568 | tf_op jit(solution)/shard_map/ppermute | solution.py:303
  26.1 3.2 %columns.1 = (bf16[768,768]{1,0:T(8,128)(2,1)S(1)}, bf16[768,768]{1,0:T(8,128)(2,1)S(1)}, bf16[768,768]{1,0:T(8,128)(2,1)S(1)}, bf16[768,768]{1,0:T(8,128)(2,1)S(1)}) custom-call(s32[4]{0:T(128)S(1)} %pad_add_fusion.which_ref, bf16[768,3072]{1,0:T(8,128)(2,1)} %w_ref), custom_call_target="tpu_custom_call" | custom-call | flops 1 | bytes 1 | tf_op jit(solution)/shard_map/columns/pallas_call | solution.py:331
  29.3 6.2 %collective-permute-done.3.refs_0_ = bf16[384,896]{1,0:T(8,128)(2,1)S(1)} collective-permute-done((bf16[384,896]{1,0:T(8,128)(2,1)}, bf16[384,896]{1,0:T(8,128)(2,1)S(1)}, u32[]{:S(2)}, u32[]{:S(2)}) %collective-permute-start.3) | collective-permute-done | bytes 688160 | tf_op jit(solution)/shard_map/ppermute | solution.py:297
  35.5 1.3 %collective-permute-start.6 = (bf16[384,896]{1,0:T(8,128)(2,1)S(1)}, bf16[384,896]{1,0:T(8,128)(2,1)S(1)}, u32[]{:S(2)}, u32[]{:S(2)}) collective-permute-start(bf16[384,896]{1,0:T(8,128)(2,1)S(1)} %collective-permute-done.3.refs_0_), channel_id=1, source_target_pairs={{0,4},{12,8},{16,20},{28,24},{32,36},{44,40},{48,52},{60,56},{64,6... | collective-permute-start | bytes 2064392 | tf_op jit(solution)/shard_map/ppermute | solution.py:315
  36.8 2.8 %far0_6.1.state_ref = f32[6,384,384]{2,1,0:T(8,128)S(1)} custom-call(s32[1]{0:T(128)} %get-tuple-element.71.valid_ref, bf16[384,768]{1,0:T(8,128)(2,1)S(1)} %copy-done, f32[6,384,384]{2,1,0:T(8,128)S(1)} %copy-done.2, bf16[384,896]{1,0:T(8,128)(2,1)S(1)} %collective-permute-done.3.refs_0_, bf16[384,640]{1,0:T(8,128)(2,1)S(1)} %collective-permute-done.refs_1_), custom_call_target="tpu_custom_call" | custom-call | flops 1 | bytes 1 | tf_op jit(solution)/shard_map/far0_6/pallas_call | solution.py:203
  39.6 11.4 %collective-permute-done.4.refs_0_ = bf16[384,896]{1,0:T(8,128)(2,1)S(1)} collective-permute-done((bf16[384,896]{1,0:T(8,128)(2,1)}, bf16[384,896]{1,0:T(8,128)(2,1)S(1)}, u32[]{:S(2)}, u32[]{:S(2)}) %collective-permute-start.4) | collective-permute-done | bytes 688160 | tf_op jit(solution)/shard_map/ppermute | solution.py:295
  51.1 1.3 %collective-permute-start.7 = (bf16[384,896]{1,0:T(8,128)(2,1)S(1)}, bf16[384,896]{1,0:T(8,128)(2,1)S(1)}, u32[]{:S(2)}, u32[]{:S(2)}) collective-permute-start(bf16[384,896]{1,0:T(8,128)(2,1)S(1)} %collective-permute-done.4.refs_0_), channel_id=1, source_target_pairs={{4,0},{8,12},{20,16},{24,28},{36,32},{40,44},{52,48},{56,60},{68,6... | collective-permute-start | bytes 2064392 | tf_op jit(solution)/shard_map/ppermute | solution.py:319
  52.4 1.9 %far0_3.2.state_ref = f32[3,384,384]{2,1,0:T(8,128)S(1)} custom-call(s32[1]{0:T(128)} %get-tuple-element.69.valid_ref, bf16[384,768]{1,0:T(8,128)(2,1)S(1)} %copy-done, f32[6,384,384]{2,1,0:T(8,128)S(1)} %far0_6.1.state_ref, bf16[384,896]{1,0:T(8,128)(2,1)S(1)} %collective-permute-done.4.refs_0_), custom_call_target="tpu_custom_call" | custom-call | flops 1 | bytes 1 | tf_op jit(solution)/shard_map/far0_3/pallas_call | solution.py:203
  54.4 1.4 %collective-permute-start.9 = (bf16[384,640]{1,0:T(8,128)(2,1)S(1)}, bf16[384,640]{1,0:T(8,128)(2,1)S(1)}, u32[]{:S(2)}, u32[]{:S(2)}) collective-permute-start(bf16[384,640]{1,0:T(8,128)(2,1)S(1)} %add_select_fusion), channel_id=1, source_target_pairs={{0,4},{4,0},{8,12},{12,8},{16,20},{20,16},{24,28},{28,24},{32,36},... | collective-permute-start | bytes 1474568 | tf_op jit(solution)/shard_map/ppermute | solution.py:320
  55.9 1.9 %far0_3.3.refs_6_.att0_ref = bf16[384,384]{1,0:T(8,128)(2,1)S(1)} custom-call(s32[1]{0:T(128)} %get-tuple-element.70.valid_ref, bf16[384,768]{1,0:T(8,128)(2,1)S(1)} %copy-done, f32[3,384,384]{2,1,0:T(8,128)S(1)} %far0_3.2.state_ref, bf16[384,896]{1,0:T(8,128)(2,1)S(1)} %collective-permute-done.6.refs_0_.refs_3_, ...), custom_call_target="tpu_custom_call" | custom-call | flops 1 | bytes 1 | tf_op jit(solution)/shard_map/far0_3/pallas_call | solution.py:203
  57.8 3.4 %last.1 = (bf16[384,384]{1,0:T(8,128)(2,1)S(1)}, bf16[384,768]{1,0:T(8,128)(2,1)S(1)}) custom-call(s32[2]{0:T(128)S(1)} %slice.21.valid_ref, bf16[384,768]{1,0:T(8,128)(2,1)S(1)} %copy-done, f32[6,384,384]{2,1,0:T(8,128)S(1)} %far0_6.1.state_ref, bf16[384,896]{1,0:T(8,128)(2,1)S(1)} %collective-permute-done.4.refs_0_, ...), custom_call_target="tpu_custom_call" | custom-call | flops 1 | bytes 1 | tf_op jit(solution)/shard_map/last/pallas_call | solution.py:218
  61.4 2.0 %project.1 = (bf16[384,768]{1,0:T(8,128)(2,1)S(1)}, bf16[384,768]{1,0:T(8,128)(2,1)S(1)}, bf16[384,768]{1,0:T(8,128)(2,1)S(1)}) custom-call(bf16[384,384]{1,0:T(8,128)(2,1)S(1)} %far0_3.3.refs_6_.att0_ref, bf16[384,384]{1,0:T(8,128)(2,1)S(1)} %get-tuple-element.61.att1_ref, bf16[768,768]{1,0:T(8,128)(2,1)S(1)} %get-tuple-element.62.refs_0_, ...), custom_call_target="tpu_custom_call" | custom-call | flops 1 | bytes 1 | tf_op jit(solution)/shard_map/project/pallas_call | solution.py:366
  63.4 2.1 %collective-permute-start.10 = (bf16[384,768]{1,0:T(8,128)(2,1)S(1)}, bf16[384,768]{1,0:T(8,128)(2,1)S(1)}, u32[]{:S(2)}, u32[]{:S(2)}) collective-permute-start(bf16[384,768]{1,0:T(8,128)(2,1)S(1)} %get-tuple-element.66), channel_id=1, source_target_pairs={{0,1},{1,0},{2,3},{3,2},{4,5},{5,4},{6,7},{7,6},{8,9},{9,8},{10,11... | collective-permute-start | bytes 1769480 | tf_op jit(solution)/shard_map/ppermute | solution.py:379
  65.5 12.1 %collective-permute-done.11 = bf16[384,768]{1,0:T(8,128)(2,1)S(1)} collective-permute-done((bf16[384,768]{1,0:T(8,128)(2,1)S(1)}, bf16[384,768]{1,0:T(8,128)(2,1)S(1)}, u32[]{:S(2)}, u32[]{:S(2)}) %collective-permute-start.11) | collective-permute-done | bytes 589856 | tf_op jit(solution)/shard_map/ppermute | solution.py:379
  77.7 2.1 %collective-permute-start.12 = (bf16[384,768]{1,0:T(8,128)(2,1)S(1)}, bf16[384,768]{1,0:T(8,128)(2,1)S(1)}, u32[]{:S(2)}, u32[]{:S(2)}) collective-permute-start(bf16[384,768]{1,0:T(8,128)(2,1)S(1)} %add_convert_fusion), channel_id=1, source_target_pairs={{0,2},{1,3},{2,0},{3,1},{4,6},{5,7},{6,4},{7,5},{8,10},{9,11},{10,... | collective-permute-start | bytes 1769480 | tf_op jit(solution)/shard_map/ppermute | solution.py:379
  79.8 20.8 %collective-permute-done.10.refs_1_ = bf16[384,768]{1,0:T(8,128)(2,1)S(1)} collective-permute-done((bf16[384,768]{1,0:T(8,128)(2,1)S(1)}, bf16[384,768]{1,0:T(8,128)(2,1)S(1)}, u32[]{:S(2)}, u32[]{:S(2)}) %collective-permute-start.10) | collective-permute-done | bytes 589856 | tf_op jit(solution)/shard_map/ppermute | solution.py:379
  100.6 4.7 %collective-permute-done.12.refs_2_ = bf16[384,768]{1,0:T(8,128)(2,1)S(1)} collective-permute-done((bf16[384,768]{1,0:T(8,128)(2,1)S(1)}, bf16[384,768]{1,0:T(8,128)(2,1)S(1)}, u32[]{:S(2)}, u32[]{:S(2)}) %collective-permute-start.12) | collective-permute-done | bytes 589856 | tf_op jit(solution)/shard_map/ppermute | solution.py:379
  105.3 1.0 last_sum.1
  (30 shorter events, 4.3 us)
Async XLA Ops:
  0.0 15.2 %copy-start.3 = (bf16[384,768]{1,0:T(8,128)(2,1)S(1)}, bf16[384,768]{1,0:T(8,128)(2,1)}, u32[]{:S(2)}) copy-start(bf16[384,768]{1,0:T(8,128)(2,1)} %v_ref.3) | copy-start | bytes 1769476
  0.0 15.2 %copy-start = (bf16[384,768]{1,0:T(8,128)(2,1)S(1)}, bf16[384,768]{1,0:T(8,128)(2,1)}, u32[]{:S(2)}) copy-start(bf16[384,768]{1,0:T(8,128)(2,1)} %q_ref.9) | copy-start | bytes 1769476
  0.0 15.1 %collective-permute-start.1 = (bf16[384,768]{1,0:T(8,128)(2,1)}, bf16[384,768]{1,0:T(8,128)(2,1)S(1)}, u32[]{:S(2)}, u32[]{:S(2)}) collective-permute-start(bf16[384,768]{1,0:T(8,128)(2,1)} %k_ref.3), channel_id=1, source_target_pairs={{0,4},{4,0},{8,12},{12,8},{16,20},{20,16},{24,28},{28,24},{32,36},... | collective-permute-start | bytes 1769480 | tf_op jit(solution)/shard_map/ppermute | solution.py:291
  0.0 15.1 %collective-permute-start.2 = (bf16[384,768]{1,0:T(8,128)(2,1)}, bf16[384,768]{1,0:T(8,128)(2,1)S(1)}, u32[]{:S(2)}, u32[]{:S(2)}) collective-permute-start(bf16[384,768]{1,0:T(8,128)(2,1)} %v_ref.3), channel_id=1, source_target_pairs={{0,4},{4,0},{8,12},{12,8},{16,20},{20,16},{24,28},{28,24},{32,36},... | collective-permute-start | bytes 1769480 | tf_op jit(solution)/shard_map/ppermute | solution.py:292
  2.7 18.8 %collective-permute-start = (bf16[384,640]{1,0:T(8,128)(2,1)S(1)}, bf16[384,640]{1,0:T(8,128)(2,1)S(1)}, u32[]{:S(2)}, u32[]{:S(2)}) collective-permute-start(bf16[384,640]{1,0:T(8,128)(2,1)S(1)} %get-tuple-element.37), channel_id=1, source_target_pairs={{0,8},{4,12},{8,0},{12,4},{16,24},{20,28},{24,16},{28,20},{32,40},... | collective-permute-start | bytes 1474568 | tf_op jit(solution)/shard_map/ppermute | solution.py:294
  4.2 46.8 %collective-permute-start.4 = (bf16[384,896]{1,0:T(8,128)(2,1)}, bf16[384,896]{1,0:T(8,128)(2,1)S(1)}, u32[]{:S(2)}, u32[]{:S(2)}) collective-permute-start(bf16[384,896]{1,0:T(8,128)(2,1)} %get-tuple-element.48), channel_id=1, source_target_pairs={{8,16},{12,20},{16,8},{20,12},{24,32},{28,36},{32,24},{36,28},{40,... | collective-permute-start | bytes 2064392 | tf_op jit(solution)/shard_map/ppermute | solution.py:295
  15.1 20.4 %collective-permute-start.3 = (bf16[384,896]{1,0:T(8,128)(2,1)}, bf16[384,896]{1,0:T(8,128)(2,1)S(1)}, u32[]{:S(2)}, u32[]{:S(2)}) collective-permute-start(bf16[384,896]{1,0:T(8,128)(2,1)} %get-tuple-element.48), channel_id=1, source_target_pairs={{0,8},{4,12},{8,0},{12,4},{16,24},{20,28},{24,16},{28,20},{32,40},... | collective-permute-start | bytes 2064392 | tf_op jit(solution)/shard_map/ppermute | solution.py:297
  15.2 1.1 %copy-start.4 = (bf16[384,768]{1,0:T(8,128)(2,1)S(1)}, bf16[384,768]{1,0:T(8,128)(2,1)}, u32[]{:S(2)}) copy-start(bf16[384,768]{1,0:T(8,128)(2,1)} %k_ref.3) | copy-start | bytes 1769476
  19.7 1.8 %copy-start.1 = (f32[6,384,384]{2,1,0:T(8,128)}, f32[6,384,384]{2,1,0:T(8,128)S(1)}, u32[]{:S(2)}) copy-start(f32[6,384,384]{2,1,0:T(8,128)S(1)} %near.1.state_ref) | copy-start | bytes 10616836
  21.4 32.9 %collective-permute-start.5 = (bf16[384,640]{1,0:T(8,128)(2,1)S(1)}, bf16[384,640]{1,0:T(8,128)(2,1)S(1)}, u32[]{:S(2)}, u32[]{:S(2)}) collective-permute-start(bf16[384,640]{1,0:T(8,128)(2,1)S(1)} %collective-permute-done.refs_1_), channel_id=1, source_target_pairs={{16,32},{20,36},{40,24},{44,28},{48,64},{52,68},{72,56},{76,60},{8... | collective-permute-start | bytes 1474568 | tf_op jit(solution)/shard_map/ppermute | solution.py:303
  24.5 29.8 %collective-permute-start.8 = (bf16[384,640]{1,0:T(8,128)(2,1)}, bf16[384,640]{1,0:T(8,128)(2,1)S(1)}, u32[]{:S(2)}, u32[]{:S(2)}) collective-permute-start(bf16[384,640]{1,0:T(8,128)(2,1)} %pad_maximum_fusion), channel_id=1, source_target_pairs={{8,16},{12,20},{16,8},{20,12},{40,48},{44,52},{48,40},{52,44},{72,... | collective-permute-start | bytes 1474568 | tf_op jit(solution)/shard_map/ppermute | solution.py:305
  26.1 10.7 %copy-start.2 = (f32[6,384,384]{2,1,0:T(8,128)S(1)}, f32[6,384,384]{2,1,0:T(8,128)}, u32[]{:S(2)}) copy-start(f32[6,384,384]{2,1,0:T(8,128)} %copy-done.1) | copy-start | bytes 10616836
  35.5 20.4 %collective-permute-start.6 = (bf16[384,896]{1,0:T(8,128)(2,1)S(1)}, bf16[384,896]{1,0:T(8,128)(2,1)S(1)}, u32[]{:S(2)}, u32[]{:S(2)}) collective-permute-start(bf16[384,896]{1,0:T(8,128)(2,1)S(1)} %collective-permute-done.3.refs_0_), channel_id=1, source_target_pairs={{0,4},{12,8},{16,20},{28,24},{32,36},{44,40},{48,52},{60,56},{64,6... | collective-permute-start | bytes 2064392 | tf_op jit(solution)/shard_map/ppermute | solution.py:315
  51.1 4.8 %collective-permute-start.7 = (bf16[384,896]{1,0:T(8,128)(2,1)S(1)}, bf16[384,896]{1,0:T(8,128)(2,1)S(1)}, u32[]{:S(2)}, u32[]{:S(2)}) collective-permute-start(bf16[384,896]{1,0:T(8,128)(2,1)S(1)} %collective-permute-done.4.refs_0_), channel_id=1, source_target_pairs={{4,0},{8,12},{20,16},{24,28},{36,32},{40,44},{52,48},{56,60},{68,6... | collective-permute-start | bytes 2064392 | tf_op jit(solution)/shard_map/ppermute | solution.py:319
  54.4 3.4 %collective-permute-start.9 = (bf16[384,640]{1,0:T(8,128)(2,1)S(1)}, bf16[384,640]{1,0:T(8,128)(2,1)S(1)}, u32[]{:S(2)}, u32[]{:S(2)}) collective-permute-start(bf16[384,640]{1,0:T(8,128)(2,1)S(1)} %add_select_fusion), channel_id=1, source_target_pairs={{0,4},{4,0},{8,12},{12,8},{16,20},{20,16},{24,28},{28,24},{32,36},... | collective-permute-start | bytes 1474568 | tf_op jit(solution)/shard_map/ppermute | solution.py:320
  61.3 16.3 %collective-permute-start.11 = (bf16[384,768]{1,0:T(8,128)(2,1)S(1)}, bf16[384,768]{1,0:T(8,128)(2,1)S(1)}, u32[]{:S(2)}, u32[]{:S(2)}) collective-permute-start(bf16[384,768]{1,0:T(8,128)(2,1)S(1)} %get-tuple-element.68), channel_id=1, source_target_pairs={{0,1},{1,0},{2,3},{3,2},{4,5},{5,4},{6,7},{7,6},{8,9},{9,8},{10,11... | collective-permute-start | bytes 1769480 | tf_op jit(solution)/shard_map/ppermute | solution.py:379
  63.4 37.2 %collective-permute-start.10 = (bf16[384,768]{1,0:T(8,128)(2,1)S(1)}, bf16[384,768]{1,0:T(8,128)(2,1)S(1)}, u32[]{:S(2)}, u32[]{:S(2)}) collective-permute-start(bf16[384,768]{1,0:T(8,128)(2,1)S(1)} %get-tuple-element.66), channel_id=1, source_target_pairs={{0,1},{1,0},{2,3},{3,2},{4,5},{5,4},{6,7},{7,6},{8,9},{9,8},{10,11... | collective-permute-start | bytes 1769480 | tf_op jit(solution)/shard_map/ppermute | solution.py:379
  77.7 27.6 %collective-permute-start.12 = (bf16[384,768]{1,0:T(8,128)(2,1)S(1)}, bf16[384,768]{1,0:T(8,128)(2,1)S(1)}, u32[]{:S(2)}, u32[]{:S(2)}) collective-permute-start(bf16[384,768]{1,0:T(8,128)(2,1)S(1)} %add_convert_fusion), channel_id=1, source_target_pairs={{0,2},{1,3},{2,0},{3,1},{4,6},{5,7},{6,4},{7,5},{8,10},{9,11},{10,... | collective-permute-start | bytes 1769480 | tf_op jit(solution)/shard_map/ppermute | solution.py:379

commit v9 on v8

--- a/solution.py
+++ b/solution.py
@@ -12,7 +12,7 @@
 SPANS = 64
 HEAD_PEERS = 4
 ROW = 8
-KEYS, VALUES = 4, 3
+KEYS, VALUES = 3, 4
 WEIGHT = 30
 LIGHT = pl.CostEstimate(flops=1, bytes_accessed=1, transcendentals=0)
 SCALE = math.log2(math.e) / math.sqrt(HD)

time: 107 us -> 107 us (level)
  no operation moved by 1% of the time
where the time goes in v9:
time: 107 us; the launch traced here: 106 us
  waiting for transfers between devices  55.2 us (52%)
  starting transfers between devices  23.3 us (22%)
  Pallas kernels  21.8 us (20%)
  local copies, waits for them, and re-layouts  4.53 us (4%)
  other arithmetic  1.2 us (1%)
    ppermute x3, waiting for transfers between devices, sent(): lax.ppermute(value, 'head', [(i, i ^ apart) for i in range(HEAD_PEERS)])  37.6 us
    ppermute x1, waiting for transfers between devices, body(): other0 = lax.ppermute(direct, 'seq', OTHER)  11.4 us
    ppermute x1, starting transfers between devices, body(): other0 = lax.ppermute(direct, 'seq', OTHER)  10.8 us
    pallas_call x3, Pallas kernels, far_part(): pl.pallas_call(functools.partial(far_kernel, list(heads), held_from, coun...  6.61 us
    ppermute x1, waiting for transfers between devices, body(): mate0 = lax.ppermute(direct, 'seq', MATE)  6.19 us
    ppermute x3, starting transfers between devices, sent(): lax.ppermute(value, 'head', [(i, i ^ apart) for i in range(HEAD_PEERS)])  4.33 us
    pallas_call x2, Pallas kernels, small_call(): pl.pallas_call(kernel, out_shape=out_shape, in_specs=[pl.BlockSpec(memory...  4.23 us
    pallas_call x1, Pallas kernels, last_part(): pl.pallas_call(functools.partial(last_kernel, list(heads), counts), out_s...  3.43 us
  transfers between devices with their start and end apart: 13, of which 5 were waited for; matrix products, arithmetic and copies ran while one was open for 3% of the time, Pallas kernels for 16%

profile of v9, /device:TPU:24, one launch (start us, length us, event | category | flops | bytes accessed | tf_op | source)
XLA Modules:
  0.0 106.3 jit_solution(11041312273916706413)
XLA Ops:
  0.5 2.1 %pack.1 = (bf16[384,896]{1,0:T(8,128)(2,1)}, bf16[384,640]{1,0:T(8,128)(2,1)S(1)}) custom-call(bf16[384,768]{1,0:T(8,128)(2,1)} %k_ref.3, bf16[384,768]{1,0:T(8,128)(2,1)} %v_ref.3), custom_call_target="tpu_custom_call" | custom-call | flops 1 | bytes 1 | tf_op jit(solution)/shard_map/pack/pallas_call | solution.py:236
  2.7 1.6 %collective-permute-start = (bf16[384,640]{1,0:T(8,128)(2,1)S(1)}, bf16[384,640]{1,0:T(8,128)(2,1)S(1)}, u32[]{:S(2)}, u32[]{:S(2)}) collective-permute-start(bf16[384,640]{1,0:T(8,128)(2,1)S(1)} %get-tuple-element.37), channel_id=1, source_target_pairs={{0,8},{4,12},{8,0},{12,4},{16,24},{20,28},{24,16},{28,20},{32,40},... | collective-permute-start | bytes 1474568 | tf_op jit(solution)/shard_map/ppermute | solution.py:294
  4.2 10.8 %collective-permute-start.4 = (bf16[384,896]{1,0:T(8,128)(2,1)}, bf16[384,896]{1,0:T(8,128)(2,1)S(1)}, u32[]{:S(2)}, u32[]{:S(2)}) collective-permute-start(bf16[384,896]{1,0:T(8,128)(2,1)} %get-tuple-element.48), channel_id=1, source_target_pairs={{8,16},{12,20},{16,8},{20,12},{24,32},{28,36},{32,24},{36,28},{40,... | collective-permute-start | bytes 2064392 | tf_op jit(solution)/shard_map/ppermute | solution.py:295
  15.2 1.1 copy-done.4
  16.3 3.4 %near.1.state_ref = f32[6,384,384]{2,1,0:T(8,128)S(1)} custom-call(bf16[384,768]{1,0:T(8,128)(2,1)S(1)} %copy-done, bf16[384,768]{1,0:T(8,128)(2,1)S(1)} %copy-done.3, bf16[384,768]{1,0:T(8,128)(2,1)S(1)} %copy-done.4, bf16[384,768]{1,0:T(8,128)(2,1)S(1)} %collective-permute-done.1.pk_ref, bf16[384,768]{1,0:T(8,128)(2,1)S(1)} %collective-permute-done.2.pv_ref), custom_call_target="tpu_custom_call" | custom-call | flops 40768634880 | bytes 2949120 | tf_op jit(solution)/shard_map/near/pallas_call | solution.py:180
  19.7 1.8 %copy-done.1 = f32[6,384,384]{2,1,0:T(8,128)} copy-done((f32[6,384,384]{2,1,0:T(8,128)}, f32[6,384,384]{2,1,0:T(8,128)S(1)}, u32[]{:S(2)}) %copy-start.1) | copy-done | bytes 3538968
  21.4 1.3 %collective-permute-start.5 = (bf16[384,640]{1,0:T(8,128)(2,1)S(1)}, bf16[384,640]{1,0:T(8,128)(2,1)S(1)}, u32[]{:S(2)}, u32[]{:S(2)}) collective-permute-start(bf16[384,640]{1,0:T(8,128)(2,1)S(1)} %collective-permute-done.refs_1_), channel_id=1, source_target_pairs={{16,32},{20,36},{40,24},{44,28},{48,64},{52,68},{72,56},{76,60},{8... | collective-permute-start | bytes 1474568 | tf_op jit(solution)/shard_map/ppermute | solution.py:303
  26.1 3.2 %columns.1 = (bf16[768,768]{1,0:T(8,128)(2,1)S(1)}, bf16[768,768]{1,0:T(8,128)(2,1)S(1)}, bf16[768,768]{1,0:T(8,128)(2,1)S(1)}, bf16[768,768]{1,0:T(8,128)(2,1)S(1)}) custom-call(s32[4]{0:T(128)S(1)} %pad_add_fusion.which_ref, bf16[768,3072]{1,0:T(8,128)(2,1)} %w_ref), custom_call_target="tpu_custom_call" | custom-call | flops 1 | bytes 1 | tf_op jit(solution)/shard_map/columns/pallas_call | solution.py:331
  29.3 6.2 %collective-permute-done.3.refs_0_ = bf16[384,896]{1,0:T(8,128)(2,1)S(1)} collective-permute-done((bf16[384,896]{1,0:T(8,128)(2,1)}, bf16[384,896]{1,0:T(8,128)(2,1)S(1)}, u32[]{:S(2)}, u32[]{:S(2)}) %collective-permute-start.3) | collective-permute-done | bytes 688160 | tf_op jit(solution)/shard_map/ppermute | solution.py:297
  35.5 1.3 %collective-permute-start.6 = (bf16[384,896]{1,0:T(8,128)(2,1)S(1)}, bf16[384,896]{1,0:T(8,128)(2,1)S(1)}, u32[]{:S(2)}, u32[]{:S(2)}) collective-permute-start(bf16[384,896]{1,0:T(8,128)(2,1)S(1)} %collective-permute-done.3.refs_0_), channel_id=1, source_target_pairs={{0,4},{12,8},{16,20},{28,24},{32,36},{44,40},{48,52},{60,56},{64,6... | collective-permute-start | bytes 2064392 | tf_op jit(solution)/shard_map/ppermute | solution.py:315
  36.8 2.8 %far0_6.1.state_ref = f32[6,384,384]{2,1,0:T(8,128)S(1)} custom-call(s32[1]{0:T(128)} %get-tuple-element.71.valid_ref, bf16[384,768]{1,0:T(8,128)(2,1)S(1)} %copy-done, f32[6,384,384]{2,1,0:T(8,128)S(1)} %copy-done.2, bf16[384,896]{1,0:T(8,128)(2,1)S(1)} %collective-permute-done.3.refs_0_, bf16[384,640]{1,0:T(8,128)(2,1)S(1)} %collective-permute-done.refs_1_), custom_call_target="tpu_custom_call" | custom-call | flops 1 | bytes 1 | tf_op jit(solution)/shard_map/far0_6/pallas_call | solution.py:203
  39.6 11.4 %collective-permute-done.4.refs_0_ = bf16[384,896]{1,0:T(8,128)(2,1)S(1)} collective-permute-done((bf16[384,896]{1,0:T(8,128)(2,1)}, bf16[384,896]{1,0:T(8,128)(2,1)S(1)}, u32[]{:S(2)}, u32[]{:S(2)}) %collective-permute-start.4) | collective-permute-done | bytes 688160 | tf_op jit(solution)/shard_map/ppermute | solution.py:295
  51.1 1.3 %collective-permute-start.7 = (bf16[384,896]{1,0:T(8,128)(2,1)S(1)}, bf16[384,896]{1,0:T(8,128)(2,1)S(1)}, u32[]{:S(2)}, u32[]{:S(2)}) collective-permute-start(bf16[384,896]{1,0:T(8,128)(2,1)S(1)} %collective-permute-done.4.refs_0_), channel_id=1, source_target_pairs={{4,0},{8,12},{20,16},{24,28},{36,32},{40,44},{52,48},{56,60},{68,6... | collective-permute-start | bytes 2064392 | tf_op jit(solution)/shard_map/ppermute | solution.py:319
  52.3 1.9 %far0_3.2.state_ref = f32[3,384,384]{2,1,0:T(8,128)S(1)} custom-call(s32[1]{0:T(128)} %get-tuple-element.69.valid_ref, bf16[384,768]{1,0:T(8,128)(2,1)S(1)} %copy-done, f32[6,384,384]{2,1,0:T(8,128)S(1)} %far0_6.1.state_ref, bf16[384,896]{1,0:T(8,128)(2,1)S(1)} %collective-permute-done.4.refs_0_), custom_call_target="tpu_custom_call" | custom-call | flops 1 | bytes 1 | tf_op jit(solution)/shard_map/far0_3/pallas_call | solution.py:203
  54.4 1.4 %collective-permute-start.9 = (bf16[384,640]{1,0:T(8,128)(2,1)S(1)}, bf16[384,640]{1,0:T(8,128)(2,1)S(1)}, u32[]{:S(2)}, u32[]{:S(2)}) collective-permute-start(bf16[384,640]{1,0:T(8,128)(2,1)S(1)} %add_select_fusion), channel_id=1, source_target_pairs={{0,4},{4,0},{8,12},{12,8},{16,20},{20,16},{24,28},{28,24},{32,36},... | collective-permute-start | bytes 1474568 | tf_op jit(solution)/shard_map/ppermute | solution.py:320
  55.9 1.9 %far0_3.3.refs_6_.att0_ref = bf16[384,384]{1,0:T(8,128)(2,1)S(1)} custom-call(s32[1]{0:T(128)} %get-tuple-element.70.valid_ref, bf16[384,768]{1,0:T(8,128)(2,1)S(1)} %copy-done, f32[3,384,384]{2,1,0:T(8,128)S(1)} %far0_3.2.state_ref, bf16[384,896]{1,0:T(8,128)(2,1)S(1)} %collective-permute-done.6.refs_0_.refs_3_, ...), custom_call_target="tpu_custom_call" | custom-call | flops 1 | bytes 1 | tf_op jit(solution)/shard_map/far0_3/pallas_call | solution.py:203
  57.8 3.4 %last.1 = (bf16[384,384]{1,0:T(8,128)(2,1)S(1)}, bf16[384,768]{1,0:T(8,128)(2,1)S(1)}) custom-call(s32[2]{0:T(128)S(1)} %slice.21.valid_ref, bf16[384,768]{1,0:T(8,128)(2,1)S(1)} %copy-done, f32[6,384,384]{2,1,0:T(8,128)S(1)} %far0_6.1.state_ref, bf16[384,896]{1,0:T(8,128)(2,1)S(1)} %collective-permute-done.4.refs_0_, ...), custom_call_target="tpu_custom_call" | custom-call | flops 1 | bytes 1 | tf_op jit(solution)/shard_map/last/pallas_call | solution.py:218
  61.4 2.0 %project.1 = (bf16[384,768]{1,0:T(8,128)(2,1)S(1)}, bf16[384,768]{1,0:T(8,128)(2,1)S(1)}, bf16[384,768]{1,0:T(8,128)(2,1)S(1)}) custom-call(bf16[384,384]{1,0:T(8,128)(2,1)S(1)} %far0_3.3.refs_6_.att0_ref, bf16[384,384]{1,0:T(8,128)(2,1)S(1)} %get-tuple-element.61.att1_ref, bf16[768,768]{1,0:T(8,128)(2,1)S(1)} %get-tuple-element.62.refs_0_, ...), custom_call_target="tpu_custom_call" | custom-call | flops 1 | bytes 1 | tf_op jit(solution)/shard_map/project/pallas_call | solution.py:366
  63.4 2.1 %collective-permute-start.10 = (bf16[384,768]{1,0:T(8,128)(2,1)S(1)}, bf16[384,768]{1,0:T(8,128)(2,1)S(1)}, u32[]{:S(2)}, u32[]{:S(2)}) collective-permute-start(bf16[384,768]{1,0:T(8,128)(2,1)S(1)} %get-tuple-element.66), channel_id=1, source_target_pairs={{0,1},{1,0},{2,3},{3,2},{4,5},{5,4},{6,7},{7,6},{8,9},{9,8},{10,11... | collective-permute-start | bytes 1769480 | tf_op jit(solution)/shard_map/ppermute | solution.py:379
  65.5 12.1 %collective-permute-done.11 = bf16[384,768]{1,0:T(8,128)(2,1)S(1)} collective-permute-done((bf16[384,768]{1,0:T(8,128)(2,1)S(1)}, bf16[384,768]{1,0:T(8,128)(2,1)S(1)}, u32[]{:S(2)}, u32[]{:S(2)}) %collective-permute-start.11) | collective-permute-done | bytes 589856 | tf_op jit(solution)/shard_map/ppermute | solution.py:379
  77.7 2.1 %collective-permute-start.12 = (bf16[384,768]{1,0:T(8,128)(2,1)S(1)}, bf16[384,768]{1,0:T(8,128)(2,1)S(1)}, u32[]{:S(2)}, u32[]{:S(2)}) collective-permute-start(bf16[384,768]{1,0:T(8,128)(2,1)S(1)} %add_convert_fusion), channel_id=1, source_target_pairs={{0,2},{1,3},{2,0},{3,1},{4,6},{5,7},{6,4},{7,5},{8,10},{9,11},{10,... | collective-permute-start | bytes 1769480 | tf_op jit(solution)/shard_map/ppermute | solution.py:379
  79.8 20.8 %collective-permute-done.10.refs_1_ = bf16[384,768]{1,0:T(8,128)(2,1)S(1)} collective-permute-done((bf16[384,768]{1,0:T(8,128)(2,1)S(1)}, bf16[384,768]{1,0:T(8,128)(2,1)S(1)}, u32[]{:S(2)}, u32[]{:S(2)}) %collective-permute-start.10) | collective-permute-done | bytes 589856 | tf_op jit(solution)/shard_map/ppermute | solution.py:379
  100.6 4.7 %collective-permute-done.12.refs_2_ = bf16[384,768]{1,0:T(8,128)(2,1)S(1)} collective-permute-done((bf16[384,768]{1,0:T(8,128)(2,1)S(1)}, bf16[384,768]{1,0:T(8,128)(2,1)S(1)}, u32[]{:S(2)}, u32[]{:S(2)}) %collective-permute-start.12) | collective-permute-done | bytes 589856 | tf_op jit(solution)/shard_map/ppermute | solution.py:379
  105.3 1.0 last_sum.1
  (30 shorter events, 4.3 us)
Async XLA Ops:
  0.0 15.2 %copy-start.3 = (bf16[384,768]{1,0:T(8,128)(2,1)S(1)}, bf16[384,768]{1,0:T(8,128)(2,1)}, u32[]{:S(2)}) copy-start(bf16[384,768]{1,0:T(8,128)(2,1)} %k_ref.3) | copy-start | bytes 1769476
  0.0 15.2 %copy-start = (bf16[384,768]{1,0:T(8,128)(2,1)S(1)}, bf16[384,768]{1,0:T(8,128)(2,1)}, u32[]{:S(2)}) copy-start(bf16[384,768]{1,0:T(8,128)(2,1)} %q_ref.9) | copy-start | bytes 1769476
  0.0 15.0 %collective-permute-start.1 = (bf16[384,768]{1,0:T(8,128)(2,1)}, bf16[384,768]{1,0:T(8,128)(2,1)S(1)}, u32[]{:S(2)}, u32[]{:S(2)}) collective-permute-start(bf16[384,768]{1,0:T(8,128)(2,1)} %k_ref.3), channel_id=1, source_target_pairs={{0,4},{4,0},{8,12},{12,8},{16,20},{20,16},{24,28},{28,24},{32,36},... | collective-permute-start | bytes 1769480 | tf_op jit(solution)/shard_map/ppermute | solution.py:291
  0.0 15.1 %collective-permute-start.2 = (bf16[384,768]{1,0:T(8,128)(2,1)}, bf16[384,768]{1,0:T(8,128)(2,1)S(1)}, u32[]{:S(2)}, u32[]{:S(2)}) collective-permute-start(bf16[384,768]{1,0:T(8,128)(2,1)} %v_ref.3), channel_id=1, source_target_pairs={{0,4},{4,0},{8,12},{12,8},{16,20},{20,16},{24,28},{28,24},{32,36},... | collective-permute-start | bytes 1769480 | tf_op jit(solution)/shard_map/ppermute | solution.py:292
  2.7 18.8 %collective-permute-start = (bf16[384,640]{1,0:T(8,128)(2,1)S(1)}, bf16[384,640]{1,0:T(8,128)(2,1)S(1)}, u32[]{:S(2)}, u32[]{:S(2)}) collective-permute-start(bf16[384,640]{1,0:T(8,128)(2,1)S(1)} %get-tuple-element.37), channel_id=1, source_target_pairs={{0,8},{4,12},{8,0},{12,4},{16,24},{20,28},{24,16},{28,20},{32,40},... | collective-permute-start | bytes 1474568 | tf_op jit(solution)/shard_map/ppermute | solution.py:294
  4.2 46.8 %collective-permute-start.4 = (bf16[384,896]{1,0:T(8,128)(2,1)}, bf16[384,896]{1,0:T(8,128)(2,1)S(1)}, u32[]{:S(2)}, u32[]{:S(2)}) collective-permute-start(bf16[384,896]{1,0:T(8,128)(2,1)} %get-tuple-element.48), channel_id=1, source_target_pairs={{8,16},{12,20},{16,8},{20,12},{24,32},{28,36},{32,24},{36,28},{40,... | collective-permute-start | bytes 2064392 | tf_op jit(solution)/shard_map/ppermute | solution.py:295
  15.1 20.4 %collective-permute-start.3 = (bf16[384,896]{1,0:T(8,128)(2,1)}, bf16[384,896]{1,0:T(8,128)(2,1)S(1)}, u32[]{:S(2)}, u32[]{:S(2)}) collective-permute-start(bf16[384,896]{1,0:T(8,128)(2,1)} %get-tuple-element.48), channel_id=1, source_target_pairs={{0,8},{4,12},{8,0},{12,4},{16,24},{20,28},{24,16},{28,20},{32,40},... | collective-permute-start | bytes 2064392 | tf_op jit(solution)/shard_map/ppermute | solution.py:297
  15.2 1.1 %copy-start.4 = (bf16[384,768]{1,0:T(8,128)(2,1)S(1)}, bf16[384,768]{1,0:T(8,128)(2,1)}, u32[]{:S(2)}) copy-start(bf16[384,768]{1,0:T(8,128)(2,1)} %v_ref.3) | copy-start | bytes 1769476
  19.7 1.8 %copy-start.1 = (f32[6,384,384]{2,1,0:T(8,128)}, f32[6,384,384]{2,1,0:T(8,128)S(1)}, u32[]{:S(2)}) copy-start(f32[6,384,384]{2,1,0:T(8,128)S(1)} %near.1.state_ref) | copy-start | bytes 10616836
  21.4 32.8 %collective-permute-start.5 = (bf16[384,640]{1,0:T(8,128)(2,1)S(1)}, bf16[384,640]{1,0:T(8,128)(2,1)S(1)}, u32[]{:S(2)}, u32[]{:S(2)}) collective-permute-start(bf16[384,640]{1,0:T(8,128)(2,1)S(1)} %collective-permute-done.refs_1_), channel_id=1, source_target_pairs={{16,32},{20,36},{40,24},{44,28},{48,64},{52,68},{72,56},{76,60},{8... | collective-permute-start | bytes 1474568 | tf_op jit(solution)/shard_map/ppermute | solution.py:303
  24.5 29.8 %collective-permute-start.8 = (bf16[384,640]{1,0:T(8,128)(2,1)}, bf16[384,640]{1,0:T(8,128)(2,1)S(1)}, u32[]{:S(2)}, u32[]{:S(2)}) collective-permute-start(bf16[384,640]{1,0:T(8,128)(2,1)} %pad_maximum_fusion), channel_id=1, source_target_pairs={{8,16},{12,20},{16,8},{20,12},{40,48},{44,52},{48,40},{52,44},{72,... | collective-permute-start | bytes 1474568 | tf_op jit(solution)/shard_map/ppermute | solution.py:305
  26.1 10.7 %copy-start.2 = (f32[6,384,384]{2,1,0:T(8,128)S(1)}, f32[6,384,384]{2,1,0:T(8,128)}, u32[]{:S(2)}) copy-start(f32[6,384,384]{2,1,0:T(8,128)} %copy-done.1) | copy-start | bytes 10616836
  35.5 20.4 %collective-permute-start.6 = (bf16[384,896]{1,0:T(8,128)(2,1)S(1)}, bf16[384,896]{1,0:T(8,128)(2,1)S(1)}, u32[]{:S(2)}, u32[]{:S(2)}) collective-permute-start(bf16[384,896]{1,0:T(8,128)(2,1)S(1)} %collective-permute-done.3.refs_0_), channel_id=1, source_target_pairs={{0,4},{12,8},{16,20},{28,24},{32,36},{44,40},{48,52},{60,56},{64,6... | collective-permute-start | bytes 2064392 | tf_op jit(solution)/shard_map/ppermute | solution.py:315
  51.1 4.8 %collective-permute-start.7 = (bf16[384,896]{1,0:T(8,128)(2,1)S(1)}, bf16[384,896]{1,0:T(8,128)(2,1)S(1)}, u32[]{:S(2)}, u32[]{:S(2)}) collective-permute-start(bf16[384,896]{1,0:T(8,128)(2,1)S(1)} %collective-permute-done.4.refs_0_), channel_id=1, source_target_pairs={{4,0},{8,12},{20,16},{24,28},{36,32},{40,44},{52,48},{56,60},{68,6... | collective-permute-start | bytes 2064392 | tf_op jit(solution)/shard_map/ppermute | solution.py:319
  54.4 3.4 %collective-permute-start.9 = (bf16[384,640]{1,0:T(8,128)(2,1)S(1)}, bf16[384,640]{1,0:T(8,128)(2,1)S(1)}, u32[]{:S(2)}, u32[]{:S(2)}) collective-permute-start(bf16[384,640]{1,0:T(8,128)(2,1)S(1)} %add_select_fusion), channel_id=1, source_target_pairs={{0,4},{4,0},{8,12},{12,8},{16,20},{20,16},{24,28},{28,24},{32,36},... | collective-permute-start | bytes 1474568 | tf_op jit(solution)/shard_map/ppermute | solution.py:320
  61.3 16.3 %collective-permute-start.11 = (bf16[384,768]{1,0:T(8,128)(2,1)S(1)}, bf16[384,768]{1,0:T(8,128)(2,1)S(1)}, u32[]{:S(2)}, u32[]{:S(2)}) collective-permute-start(bf16[384,768]{1,0:T(8,128)(2,1)S(1)} %get-tuple-element.68), channel_id=1, source_target_pairs={{0,1},{1,0},{2,3},{3,2},{4,5},{5,4},{6,7},{7,6},{8,9},{9,8},{10,11... | collective-permute-start | bytes 1769480 | tf_op jit(solution)/shard_map/ppermute | solution.py:379
  63.4 37.2 %collective-permute-start.10 = (bf16[384,768]{1,0:T(8,128)(2,1)S(1)}, bf16[384,768]{1,0:T(8,128)(2,1)S(1)}, u32[]{:S(2)}, u32[]{:S(2)}) collective-permute-start(bf16[384,768]{1,0:T(8,128)(2,1)S(1)} %get-tuple-element.66), channel_id=1, source_target_pairs={{0,1},{1,0},{2,3},{3,2},{4,5},{5,4},{6,7},{7,6},{8,9},{9,8},{10,11... | collective-permute-start | bytes 1769480 | tf_op jit(solution)/shard_map/ppermute | solution.py:379
  77.7 27.6 %collective-permute-start.12 = (bf16[384,768]{1,0:T(8,128)(2,1)S(1)}, bf16[384,768]{1,0:T(8,128)(2,1)S(1)}, u32[]{:S(2)}, u32[]{:S(2)}) collective-permute-start(bf16[384,768]{1,0:T(8,128)(2,1)S(1)} %add_convert_fusion), channel_id=1, source_target_pairs={{0,2},{1,3},{2,0},{3,1},{4,6},{5,7},{6,4},{7,5},{8,10},{9,11},{10,... | collective-permute-start | bytes 1769480 | tf_op jit(solution)/shard_map/ppermute | solution.py:379
